TPU v7x, 32 devices: a whole 2x2x4 slice. The times are simulated.
32 devices in a mesh: groups: 2 (over y), loans: 4 (over z), paths: 4 (over x, core).
Axes of the slice: x: 2, y: 2, z: 4, core: 2. Of those that a mesh axis runs over, the one named last changes fastest.
Arguments:
- loan_features: bfloat16 [8192, 128], P(('groups', 'loans')), parts along dimension 0, may hold values from -6 to 6
- hazard_coef: bfloat16 [128, 2], replicated, may hold values from -0.5 to 0.5
- coupon: float32 [8192], P(('groups', 'loans')), parts along dimension 0, may hold values from 0.03 to 0.075
- balance: float32 [8192], P(('groups', 'loans')), parts along dimension 0, may hold values from 0.25 to 4
- loan_term: int32 [8192], P(('groups', 'loans')), parts along dimension 0, may hold values from 180 to 360
- loan_age: int32 [8192], P(('groups', 'loans')), parts along dimension 0, may hold values from 0 to 119
- loan_region: int32 [8192], P(('groups', 'loans')), parts along dimension 0, may hold values from 0 to 415
- loan_deal: int32 [8192], P(('groups', 'loans')), parts along dimension 0, may hold values from 0 to 31, as said below
- region_hpi: float32 [832, 6, 512], P(('groups', 'loans'), None, 'paths'), parts along dimension 0, may hold values from -0.6 to 0.6
- rate_paths: float32 [2, 6, 1024], P(None, None, ('groups', 'paths')), parts along dimension 2, may hold values from 0.01 to 0.08
- deal_owner: int32 [64, 1], P('groups'), parts along dimension 0, may hold values from 0 to 3; in each aligned block of 32 rows (0 to 31, 32 to 63, ...) at most 24 rows name the same one
- tranche_order: int32 [64, 64], P('groups'), parts along dimension 0, may hold values from 0 to 63, each once within a row
- tranche_share: float32 [64, 64], P('groups'), parts along dimension 0, may hold values from 0.2 to 5
- tranche_rate: float32 [64, 64], P('groups'), parts along dimension 0, may hold values from 0.02 to 0.07
Outputs:
- tranche_value: float32 [64, 64], P('groups'), parts along dimension 0
There are 2 independent parts, one for each index of `groups`. A program takes and returns all parts, laid end to end along the dimension named above; an argument that names none is the same for every part. Nothing has to cross between parts.
Inputs may be any that keep to these rules, and one draw needn't show every extreme that they name: `loan_deal`: every deal holds at least one loan. `deal_owner`: no index of loans owns more than 24 deals, and one owns exactly 24. `tranche_order`: each row names every tranche once.
All inputs are finite; a program needn't handle non-finite values.
Results may differ from a plain program's by a relative error of at most 0.0003.
Values sent between devices are 32-bit elements; how exact they have to be, the bound alone decides.
No kernel may reach another device: no remote copies, remote signals or barrier semaphores. Data moves between devices by JAX's collectives and lax.ppermute only.
A program may use at most 64 MiB of HBM per device.

v0:
```python
import jax
import jax.numpy as jnp
from jax import lax
from jax.sharding import PartitionSpec as P

prepay_base = -4.0
incentive = 40.0
default_base = -6.0
price_sens = 12.0
oas_spread = 0.005


def loan_month(held, covar, coupon, rate_month, sched_rate, mortgage_now, hpi_now):
    smm = jax.nn.sigmoid(
        covar[:, 0][None, :] + prepay_base + incentive * (coupon[None, :] - mortgage_now[:, None])
    )
    mdr = jax.nn.sigmoid(covar[:, 1][None, :] + default_base - price_sens * hpi_now)
    interest = held * rate_month[None, :]
    sched = held * sched_rate[None, :]
    lost = mdr * held
    prepaid = smm * (held - sched - lost)
    principal = sched + prepaid + lost
    return (held - principal, principal, interest)


def priority_mask(tranche_order):
    count = tranche_order.shape[1]
    spots = jnp.arange(count, dtype=jnp.int32)
    hits = tranche_order[:, :, None] == spots[None, None, :]
    prio = jnp.sum(jnp.where(hits, spots[None, :, None], 0), axis=1)
    return (prio[:, :, None] < prio[:, None, :]).astype(jnp.float32)


def waterfall(princ, inter, starts, shares, rates, ahead_mask, short, valid):
    steps = princ.shape[2]
    blank = 1.0 - valid
    weights = shares / (jnp.sum(shares, axis=1, keepdims=True) + blank[:, None])
    opening = weights * starts[:, None]
    safe_open = opening + blank[:, None]
    held = jnp.broadcast_to(opening[:, None, :], (princ.shape[0], princ.shape[1], shares.shape[1]))
    decay = jnp.exp(-jnp.cumsum(short + oas_spread, axis=0) / 12.0)
    worth = jnp.zeros_like(held)
    for step in range(steps):
        ahead = jnp.einsum("xpj,xjk->xpk", held, ahead_mask, precision=lax.Precision.HIGHEST)
        paid = jnp.minimum(jnp.maximum(princ[:, :, step, None] - ahead, 0.0), held)
        coupon_due = rates[:, None, :] * held
        denom = jnp.sum(coupon_due, axis=2, keepdims=True) + blank[:, None, None]
        flow = paid + inter[:, :, step, None] * coupon_due / denom
        worth = worth + flow * decay[step][None, :, None]
        held = held - paid
    worth = worth + held * decay[steps - 1][None, :, None]
    return jnp.sum(worth / safe_open[:, None, :], axis=1)


def on_device(
    loan_features,
    hazard_coef,
    coupon,
    balance,
    loan_term,
    loan_age,
    loan_region,
    loan_deal,
    region_hpi,
    rate_paths,
    deal_owner,
    tranche_order,
    tranche_share,
    tranche_rate,
):
    highest = lax.Precision.HIGHEST
    loans_here = coupon.shape[0]
    paths_here = rate_paths.shape[2]
    steps = rate_paths.shape[1]
    deals = deal_owner.shape[0]
    groups = lax.axis_size("loans")
    me_loan = lax.axis_index("loans")
    covar = jnp.dot(loan_features, hazard_coef, preferred_element_type=jnp.float32)
    piece = lax.all_gather(region_hpi, "loans", axis=0, tiled=True)
    rows = piece.shape[0]
    marks = (loan_region[None, :] == lax.iota(jnp.int32, rows)[:, None]).astype(jnp.float32)
    loan_hpi = jnp.einsum("rc,rl->cl", piece.reshape(rows, -1), marks, precision=highest)
    loan_hpi = loan_hpi.reshape(steps, paths_here, loans_here)
    rate_month = coupon / 12.0
    term_left = (loan_term - loan_age).astype(jnp.float32)
    held = jnp.broadcast_to(balance[None, :], (paths_here, loans_here))
    prin_list = []
    int_list = []
    for step in range(steps):
        sched_rate = rate_month / jnp.expm1((term_left - step) * jnp.log1p(rate_month))
        held, principal, interest = loan_month(
            held, covar, coupon, rate_month, sched_rate, rate_paths[1, step], loan_hpi[step]
        )
        prin_list.append(principal)
        int_list.append(interest)
    cash = jnp.stack([jnp.stack(prin_list, 1), jnp.stack(int_list, 1)], 1)
    deal_ids = lax.iota(jnp.int32, deals)
    match = loan_deal[:, None] == deal_ids[None, :]
    onehot_deal = match.astype(jnp.float32)
    totals = lax.psum(jnp.dot(balance, onehot_deal, precision=highest), "loans")
    owners = deal_owner[:, 0]
    order_key = owners * deals + deal_ids
    position = jnp.sum((order_key[None, :] < order_key[:, None]).astype(jnp.int32), axis=1)
    place = (position[None, :] == deal_ids[:, None]).astype(jnp.float32)
    ahead_mask = priority_mask(tranche_order)
    portion = paths_here // groups
    block = cash.reshape(-1, loans_here)
    path_flows = lax.psum_scatter(
        jnp.dot(block, onehot_deal, precision=highest).reshape(
            portion * lax.axis_size("loans"), 2, steps, deals
        ),
        "loans",
        scatter_dimension=0,
        tiled=True,
    )
    flows = path_flows.transpose(3, 0, 1, 2)
    short = lax.dynamic_slice_in_dim(rate_paths[0], me_loan * portion, portion, 1)
    by_deal = waterfall(
        flows[:, :, 0, :],
        flows[:, :, 1, :],
        totals,
        tranche_share,
        tranche_rate,
        ahead_mask,
        short,
        jnp.ones((deals,), jnp.float32),
    )
    ordered = jnp.dot(place, by_deal, precision=highest)
    mine = lax.psum(ordered, "loans")
    total = lax.psum(mine, "paths")
    all_paths = paths_here * lax.axis_size("paths")
    return 100.0 * (total / all_paths - 1.0)


def solution(mesh):
    in_specs = (
        P(("groups", "loans"), None),
        P(),
        P(("groups", "loans")),
        P(("groups", "loans")),
        P(("groups", "loans")),
        P(("groups", "loans")),
        P(("groups", "loans")),
        P(("groups", "loans")),
        P(("groups", "loans"), None, "paths"),
        P(None, None, ("groups", "paths")),
        P("groups", None),
        P("groups", None),
        P("groups", None),
        P("groups", None),
    )
    out_specs = P("groups", None)
    return jax.shard_map(
        on_device, mesh=mesh, in_specs=in_specs, out_specs=out_specs, check_vma=False
    )
```

profile of v0, /device:TPU:0, one launch (start us, length us, event | category | flops | bytes accessed | tf_op | source)
XLA Modules:
  0.0 136.7 jit_solution(10805481417194301331)
XLA Ops:
  6.5 0.7 all-gather.2.cloned.1.call-update
  7.3 0.7 add_bitcast_fusion
  8.6 0.7 slice.140
  9.6 0.8 slice_bitcast_fusion.20
  10.4 0.8 fusion.190
  11.3 0.7 exponential-minus-one_divide_fusion
  12.0 0.7 exponential-minus-one_divide_fusion.1
  13.0 30.8 %all-gather.2.cloned.1.call-done = f32[416,6,128]{2,0,1:T(8,128)} async-done(((f32[104,6,128]{2,0,1:T(8,128)}), f32[416,6,128]{2,0,1:T(8,128)}) %all-gather.2.cloned.1.call-update) | async-done | bytes 1277968 | tf_op jit(solution)/shard_map/all_gather | solution.py:79
  43.8 4.7 %convolution_bitcast_fusion = f32[768,1024]{0,1:T(8,128)S(1)} fusion(s32[1024]{0:T(1024)} %param.20, f32[416,6,128]{2,0,1:T(8,128)} %all-gather.2.cloned.1.call-done), kind=kOutput, calls=%fused_computation.21 | convolution fusion | flops 3926294528 | bytes 4427776 | tf_op jit(solution)/shard_map/rc,rl->cl/dot_general | solution.py:82
  48.5 1.1 bitcast_dynamic-update-slice_fusion.9
  49.6 1.0 bitcast_dynamic-update-slice_fusion.8
  50.6 1.2 bitcast_dynamic-update-slice_fusion.7
  51.8 1.1 bitcast_dynamic-update-slice_fusion.6
  52.9 1.6 %bitcast_dynamic-update-slice_fusion.5 = (f32[128,6,1024]{0,2,1:T(8,128)S(1)}, f32[128,1024]{0,1:T(8,128)S(1)}, f32[128,6,1024]{0,2,1:T(8,128)S(1)}) fusion(f32[128,6,1024]{0,2,1:T(8,128)S(1)} %get-tuple-element.22, f32[768,1024]{0,1:T(8,128)S(1)} %convolution_bitcast_fusion, f32[1024]{0:T(1024)S(1)} %bitcast.124, f32[128]{0:T(128)S(1)} %get-tuple-element.48, ...), kind=kLoop, calls=%fused_computation.138 | loop fusion | flops 7471104 | bytes 3700224
  54.8 1.1 fusion.116
  55.9 6.0 %fusion.5 = f32[128,2,6,32]{3,0,2,1:T(8,128)} fusion(f32[128,1,6,1024]{0,3,2,1:T(8,128)S(1)} %bitcast.112, f32[128,1,6,1024]{0,3,2,1:T(8,128)S(1)} %bitcast.113, s32[1024]{0:T(1024)S(1)} %copy-done.6), kind=kOutput, calls=%fused_computation.5 | convolution fusion | flops 605585408 | bytes 6492160 | tf_op jit(solution)/shard_map/dot_general | solution.py:109
  62.2 10.0 %psum.21 = f32[32]{0:T(128)S(1)} all-reduce(f32[32]{0:T(128)S(1)} %convolution_bitcast_fusion.1), channel_id=1, replica_groups=mesh['groups'=2,'loans'=4,'paths'=4] {'loans'}, use_global_device_ids=true, to_apply=%region_3.4 | all-reduce | flops 32 | bytes 256 | tf_op jit(solution)/shard_map/psum | solution.py:100
  72.8 11.7 %reduce-scatter.2.cloned.1.call-done = f32[32,2,6,32]{3,0,2,1:T(8,128)} async-done(((f32[128,2,6,32]{3,0,2,1:T(8,128)}), f32[32,2,6,32]{3,0,2,1:T(8,128)}) %reduce-scatter.2.cloned.1.call-update) | async-done | bytes 49168 | tf_op jit(solution)/shard_map/reduce_scatter | solution.py:108
  84.5 1.0 slice_bitcast_fusion
  86.3 1.0 fusion.29
  87.3 1.4 subtract_subtract_fusion
  88.7 1.0 fusion.186
  89.6 1.0 fusion.187
  90.6 1.0 fusion.188
  91.6 1.0 fusion.74
  92.6 1.8 %fusion.89 = f32[32,32,64]{2,1,0:T(8,128)S(1)} fusion(f32[32,32,64]{2,1,0:T(8,128)S(1)} %get-tuple-element.63, f32[32,32,64]{2,1,0:T(8,128)S(1)} %get-tuple-element.60, f32[32]{0:T(128)S(1)} %get-tuple-element.57, f32[32,32]{1,0:T(8,128)S(1)} %copy.51, f32[32,64]{1,0:T(8,128)S(1)} %copy-done.5), kind=kOutput, calls=%fused_computation.55 | output fusion | flops 394303 | bytes 798848 | tf_op jit(solution)/shard_map/div | solution.py:48
  94.4 1.8 %fusion.92 = f32[32,32,64]{2,1,0:T(8,128)S(1)} fusion(f32[32,32,64]{2,1,0:T(8,128)S(1)} %get-tuple-element.65, f32[32,32,64]{2,1,0:T(8,128)S(1)} %get-tuple-element.62, f32[32]{0:T(128)S(1)} %get-tuple-element.56, f32[32,32]{1,0:T(8,128)S(1)} %copy.53, f32[32,64]{1,0:T(8,128)S(1)} %copy-done.5), kind=kOutput, calls=%fused_computation.58 | output fusion | flops 394303 | bytes 798848 | tf_op jit(solution)/shard_map/div | solution.py:48
  96.2 1.8 %fusion.95 = f32[32,32,64]{2,1,0:T(8,128)S(1)} fusion(f32[32,32,64]{2,1,0:T(8,128)S(1)} %get-tuple-element.67, f32[32,32,64]{2,1,0:T(8,128)S(1)} %get-tuple-element.64, f32[32]{0:T(128)S(1)} %get-tuple-element.55, f32[32,32]{1,0:T(8,128)S(1)} %copy.55, f32[32,64]{1,0:T(8,128)S(1)} %copy-done.5), kind=kOutput, calls=%fused_computation.61 | output fusion | flops 394303 | bytes 798848 | tf_op jit(solution)/shard_map/div | solution.py:48
  98.1 1.8 %fusion.98 = f32[32,32,64]{2,1,0:T(8,128)S(1)} fusion(f32[32,32,64]{2,1,0:T(8,128)S(1)} %fusion.74, f32[32,32,64]{2,1,0:T(8,128)S(1)} %get-tuple-element.66, f32[32]{0:T(128)S(1)} %get-tuple-element.54, f32[32,32]{1,0:T(8,128)S(1)} %copy.57, f32[32,64]{1,0:T(8,128)S(1)} %copy-done.5), kind=kOutput, calls=%fused_computation.64 | output fusion | flops 394303 | bytes 798848 | tf_op jit(solution)/shard_map/div | solution.py:48
  99.9 2.0 %fusion.189 = f32[32,64]{1,0:T(8,128)S(1)} fusion(f32[32]{0:T(128)S(1)} %get-tuple-element.54, f32[32,32,64]{2,1,0:T(8,128)S(1)} %get-tuple-element.66, f32[32,32,64]{2,1,0:T(8,128)S(1)} %fusion.74, f32[32,32,64]{2,1,0:T(8,128)S(1)} %fusion.98, f32[32,32,64]{2,1,0:T(8,128)S(1)} %fusion.95, f32[32,32,64]{2,1,0:T(8,128)S(1)} %fusion.92, ...), kind=kOutput, calls=%fused_computation.238 | output fusion | flops 1440831 | bytes 2138624 | tf_op jit(solution)/shard_map/div | solution.py:48
  102.1 17.1 %psum.22 = f32[32,64]{1,0:T(8,128)S(1)} all-reduce(f32[32,64]{1,0:T(8,128)S(1)} %fusion.179), channel_id=1, replica_groups=mesh['groups'=2,'loans'=4,'paths'=4] {'loans'}, use_global_device_ids=true, to_apply=%region_13.14 | all-reduce | flops 2048 | bytes 16384 | tf_op jit(solution)/shard_map/psum | solution.py:129
  119.1 10.1 %psum.23 = f32[32,64]{1,0:T(8,128)S(1)} all-reduce(f32[32,64]{1,0:T(8,128)S(1)} %psum.22), channel_id=1, replica_groups=mesh['groups'=2,'loans'=4,'paths'=4] {'paths'}, use_global_device_ids=true, to_apply=%region_14.15 | all-reduce | flops 2048 | bytes 16384 | tf_op jit(solution)/shard_map/psum | solution.py:130
  (46 shorter events, 3.9 us)
Async XLA Ops:
  6.5 3.9 %copy-start = (bf16[1024,128]{1,0:T(8,128)(2,1)S(1)}, bf16[1024,128]{1,0:T(8,128)(2,1)}, u32[]{:S(2)}) copy-start(bf16[1024,128]{1,0:T(8,128)(2,1)} %param.14) | copy-start | bytes 786436
  6.5 41.9 %copy-start.1 = (f32[1024]{0:T(1024)S(1)}, f32[1024]{0:T(1024)}, u32[]{:S(2)}) copy-start(f32[1024]{0:T(1024)} %param.16) | copy-start | bytes 12292
  6.5 42.0 %copy-start.2 = (f32[1024]{0:T(1024)S(1)}, f32[1024]{0:T(1024)}, u32[]{:S(2)}) copy-start(f32[1024]{0:T(1024)} %param.17) | copy-start | bytes 12292
  6.5 37.3 %all-gather.2.cloned.1.call-start = ((), (), s32[]{:S(2)}) async-start(), calls=%async_computation.1 | async-start | bytes 1597440 | tf_op jit(solution)/shard_map/all_gather | solution.py:79
  7.3 77.2 %reduce-scatter.2.cloned.1.call-start = ((), (), s32[]{:S(2)}) async-start(), calls=%async_computation.2 | async-start | bytes 983040 | tf_op jit(solution)/shard_map/reduce_scatter | solution.py:108
  52.9 2.9 %copy-start.6 = (s32[1024]{0:T(1024)S(1)}, s32[1024]{0:T(1024)}, u32[]{:S(2)}) copy-start(s32[1024]{0:T(1024)} %param.21) | copy-start | bytes 12292
  55.9 6.2 %copy-start.3 = (f32[32,64]{1,0:T(8,128)S(1)}, f32[32,64]{1,0:T(8,128)}, u32[]{:S(2)}) copy-start(f32[32,64]{1,0:T(8,128)} %param.26) | copy-start | bytes 24580
  55.9 16.3 %copy-start.4 = (s32[32,64]{1,0:T(8,128)S(1)}, s32[32,64]{1,0:T(8,128)}, u32[]{:S(2)}) copy-start(s32[32,64]{1,0:T(8,128)} %param.25) | copy-start | bytes 24580
  55.9 16.7 %copy-start.5 = (f32[32,64]{1,0:T(8,128)S(1)}, f32[32,64]{1,0:T(8,128)}, u32[]{:S(2)}) copy-start(f32[32,64]{1,0:T(8,128)} %param.27) | copy-start | bytes 24580
Sparse Core Ops, SparseCore 0:
  8.9 34.8 all-gather.1
  62.0 22.3 reduce-scatter.1
where the time goes:
time: 137 us
  waiting for transfers between devices  43.2 us (32%)
  blocking collectives  37.2 us (27%)
  other arithmetic  21 us (15%)
  matrix products  18 us (13%)
  between operations  13.7 us (10%)
  local copies, waits for them, and re-layouts  3.61 us (3%)
    all_gather x1, waiting for transfers between devices, on_device(): piece = lax.all_gather(region_hpi, 'loans', axis=0, tiled=True)  30.8 us
    psum x1, blocking collectives, on_device(): mine = lax.psum(ordered, 'loans')  17.1 us
    reduce_scatter x1, waiting for transfers between devices, on_device(): lax.psum_scatter(jnp.dot(block, onehot_deal, precision=highest).reshape(p...  11.7 us
    psum x1, blocking collectives, on_device(): total = lax.psum(mine, 'paths')  10.1 us
    psum x1, blocking collectives, on_device(): totals = lax.psum(jnp.dot(balance, onehot_deal, precision=highest), 'loans')  10 us
    div x5, other arithmetic, waterfall(): flow = paid + inter[:, :, step, None] * coupon_due / denom  9.33 us
    dot_general x6, matrix products, waterfall(): jnp.einsum('xpj,xjk->xpk', held, ahead_mask, precision=lax.Precision.HIGH...  6.23 us
    unnamed x6, other arithmetic  6.19 us
  transfers between devices with their start and end apart: 2, of which 2 were waited for; matrix products, arithmetic and copies ran while one was open for 5% of the time, Pallas kernels for 0%

commit v1 on v0

v1 whole, which is shorter than its diff:
```python
import functools

import jax
import jax.numpy as jnp
from jax import lax
from jax.experimental import pallas as pl
from jax.experimental.pallas import tpu as pltpu
from jax.sharding import PartitionSpec as P

prepay_base = -4.0
incentive = 40.0
default_base = -6.0
price_sens = 12.0
oas_spread = 0.005
LANES = 128
FIELDS = 7
HIGHEST = lax.Precision.HIGHEST
VMEM_LIMIT = 48 * 1024 * 1024


def up(value, unit):
    return -(-value // unit) * unit


def peer(index, shift, count):
    if count & (count - 1) == 0:
        return jnp.bitwise_xor(index, shift)
    return lax.rem(index + shift, count)


def trade(x, axis, shift, count):
    if count & (count - 1) == 0:
        pairs = [(i, i ^ shift) for i in range(count)]
    else:
        pairs = [(i, (i + shift) % count) for i in range(count)]
    return lax.ppermute(x, axis, pairs)


def sum_over(x, axis):
    count = lax.axis_size(axis)
    if count & (count - 1):
        return lax.psum(x, axis)
    parts = [x] + [trade(x, axis, s, count) for s in range(1, count)]
    while len(parts) > 1:
        parts = [parts[i] + parts[i + 1] for i in range(0, len(parts), 2)]
    return parts[0]


class Plan:
    def __init__(self, count, loans, regions, steps, paths, deals, tranches):
        self.count, self.loans, self.regions, self.steps = count, loans, regions, steps
        self.paths, self.deals, self.tranches = paths, deals, tranches
        self.mine = paths // count
        self.pad = up(self.mine, 16)
        words = steps * self.mine
        self.months_per = LANES // self.mine
        self.full = words // LANES
        self.rem = words - self.full * LANES
        fold = LANES // self.rem if self.rem else 1
        self.fold = fold if regions % fold == 0 else 1
        self.rem_rows = regions // self.fold if self.rem else 0
        self.blocks = self.full + (1 if self.rem else 0)
        self.hpi_rows = up(self.full * regions + self.rem_rows, 8)
        self.loan_rows = loans // LANES
        self.msg_rows = up(self.hpi_rows + FIELDS * self.loan_rows, 8)
        self.depth = up(count * regions, LANES)
        self.groups = max(1, LANES // deals)
        self.rows = self.mine // self.groups
        self.width = self.groups * deals
        self.all_rows = count * self.loan_rows
        self.chunk = 4
        self.lhs_rows = 16 + steps * self.pad


def pack_kernel(plan, feat_ref, coef_ref, coupon_ref, balance_ref, term_ref, age_ref, region_ref, deal_ref, hpi_ref, *outs):
    me = lax.axis_index("loans")
    covar = lax.dot_general(
        coef_ref[...], feat_ref[...], (((0,), (1,)), ((), ())), preferred_element_type=jnp.float32
    )
    base, lr = plan.hpi_rows, plan.loan_rows
    rows0 = jnp.concatenate([covar[0:1, LANES * i : LANES * (i + 1)] for i in range(lr)], axis=0)
    rows1 = jnp.concatenate([covar[1:2, LANES * i : LANES * (i + 1)] for i in range(lr)], axis=0)
    coupon = coupon_ref[...]
    fields = (
        0.5 * (rows0 + prepay_base + incentive * coupon),
        0.5 * (rows1 + default_base),
        coupon,
        (term_ref[...] - age_ref[...]).astype(jnp.float32),
        balance_ref[...],
        region_ref[...].astype(jnp.float32),
        deal_ref[...].astype(jnp.float32),
    )
    regions, mine, per = plan.regions, plan.mine, plan.months_per
    months = [hpi_ref[:, t, :] for t in range(plan.steps)]
    lane = lax.broadcasted_iota(jnp.int32, (regions, LANES), 1)
    for s, out in enumerate(outs):
        start = peer(me, s, plan.count) * mine
        for b in range(plan.blocks):
            block = jnp.zeros((regions, LANES), jnp.float32)
            for t in range(b * per, min((b + 1) * per, plan.steps)):
                spot = (t - b * per) * mine
                moved = pltpu.roll(months[t], lax.rem(spot + LANES - start, LANES), 1)
                block = jnp.where((lane >= spot) & (lane < spot + mine), moved, block)
            if b < plan.full:
                out[b * regions : (b + 1) * regions, :] = block
            else:
                rr = plan.rem_rows
                folded = block[0:rr]
                for i in range(1, plan.fold):
                    folded = folded + pltpu.roll(block[i * rr : (i + 1) * rr], i * plan.rem, 1)
                out[plan.full * regions : plan.full * regions + rr, :] = folded
        used = plan.full * regions + plan.rem_rows
        if used < base:
            out[used:base, :] = jnp.zeros((base - used, LANES), jnp.float32)
        for i, field in enumerate(fields):
            out[base + i * lr : base + (i + 1) * lr, :] = field
        used = base + FIELDS * lr
        if used < plan.msg_rows:
            out[used:, :] = jnp.zeros((plan.msg_rows - used, LANES), jnp.float32)


def deal_kernel(plan, owner_ref, order_ref, share_ref, rate_ref, paths_ref,
                list_out, ends_out, open_out, rate_out, mort_out, disc_out, square, ranks, opens, orders):
    deals, tranches, width = plan.deals, plan.tranches, plan.width
    me = lax.axis_index("loans")
    f32 = jnp.float32
    number = lax.broadcasted_iota(jnp.int32, (deals, 1), 0)
    key = (owner_ref[...] * deals + number).astype(f32)
    row_of = lax.broadcasted_iota(jnp.int32, (deals, deals), 0)
    col_of = lax.broadcasted_iota(jnp.int32, (deals, deals), 1)
    key_row = jnp.sum(jnp.where(row_of == col_of, key, 0.0), axis=0, keepdims=True)
    spot_row = jnp.sum(jnp.where(key < key_row, 1.0, 0.0), axis=0, keepdims=True)
    tall = lax.broadcasted_iota(jnp.int32, (width, deals), 0)
    tall = lax.rem(tall, deals).astype(f32)
    place = jnp.where(tall == spot_row, 1.0, 0.0)
    deal_row = lax.broadcasted_iota(jnp.int32, (width, deals), 1).astype(f32)
    listing = jnp.sum(place * deal_row, axis=1, keepdims=True)
    list_out[...] = jnp.broadcast_to(listing[0:deals], (deals, LANES))

    def listed(table):
        return lax.dot_general(table, place, (((0,), (1,)), ((), ())), precision=HIGHEST, preferred_element_type=f32)

    share = listed(share_ref[...])
    weight = share / jnp.sum(share, axis=0, keepdims=True)
    opens[...] = weight
    open_out[...] = weight
    rate_out[...] = listed(rate_ref[...])
    orders[...] = jnp.floor(listed(order_ref[...].astype(f32)) + 0.5)
    index = lax.broadcasted_iota(jnp.int32, (tranches, width), 0).astype(f32)
    rank = jnp.zeros((tranches, width), f32)
    for j in range(tranches):
        rank = jnp.where(orders[j : j + 1, :] == index, float(j), rank)
    ranks[...] = rank
    ends = jnp.zeros((tranches, width), f32)
    for j in range(tranches):
        ends = ends + jnp.where(ranks[j : j + 1, :] <= rank, opens[j : j + 1, :], 0.0)
    ends_out[...] = ends
    steps = plan.steps
    square[...] = jnp.zeros_like(square)
    square[0:steps, :] = paths_ref[0]
    square[steps : 2 * steps, :] = paths_ref[1]
    turned = jnp.transpose(square[...])
    turned = pltpu.roll(turned, lax.rem(plan.paths - me * plan.mine, plan.paths), 0)
    lane = lax.broadcasted_iota(jnp.int32, (plan.rows, width), 1)
    total = jnp.zeros((plan.mine, 1), f32)
    for t in range(steps):
        mort_out[t * plan.pad : (t + 1) * plan.pad, :] = jnp.broadcast_to(
            (0.5 * incentive) * turned[0 : plan.pad, steps + t : steps + t + 1], (plan.pad, LANES)
        )
        total = total + (turned[0 : plan.mine, t : t + 1] + oas_spread)
        disc = jnp.exp(total / -12.0)
        wide = jnp.zeros((plan.rows, width), f32)
        for g in range(plan.groups):
            part = jnp.broadcast_to(disc[g * plan.rows : (g + 1) * plan.rows], (plan.rows, width))
            wide = jnp.where(lane >= g * plan.deals, part, wide)
        disc_out[t] = wide


def value_kernel(plan, all_paths, *refs):
    count = plan.count
    msgs = refs[:count]
    list_ref, ends_ref, open_ref, rate_ref, mort_ref, disc_ref, out_ref = refs[count : count + 7]
    gather, spots, table, dense, coef, acc = refs[count + 7 :]
    f32, bf16 = jnp.float32, jnp.bfloat16
    me = lax.axis_index("loans")
    regions, steps, pad, mine = plan.regions, plan.steps, plan.pad, plan.mine
    lr, base, ar = plan.loan_rows, plan.hpi_rows, plan.all_rows
    if count * regions < plan.depth:
        gather[count * regions :, :] = jnp.zeros((plan.depth - count * regions, plan.blocks * LANES), f32)
    for s, msg in enumerate(msgs):
        for b in range(plan.full):
            gather[s * regions : (s + 1) * regions, b * LANES : (b + 1) * LANES] = msg[b * regions : (b + 1) * regions, :]
        rr = plan.rem_rows
        for i in range(plan.fold if plan.rem else 0):
            rest = msg[plan.full * regions : plan.full * regions + rr, :]
            if i:
                rest = pltpu.roll(rest, LANES - i * plan.rem, 1)
            gather[s * regions + i * rr : s * regions + (i + 1) * rr, plan.full * LANES :] = rest
        for i in range(FIELDS):
            dense[i, s * lr : (s + 1) * lr, :] = msg[base + i * lr : base + (i + 1) * lr, :]
    if pad > mine:
        spots[...] = jnp.zeros_like(spots)
    for b in range(plan.blocks):
        turned = jnp.transpose(gather[:, b * LANES : (b + 1) * LANES])
        for t in range(b * plan.months_per, min((b + 1) * plan.months_per, steps)):
            spot = (t - b * plan.months_per) * mine
            spots[t * pad : t * pad + mine, :] = (0.5 * price_sens) * turned[spot : spot + mine, :]
    exact = spots[...]
    high = exact.astype(bf16)
    table[0 : steps * pad, :] = high
    table[steps * pad :, :] = (exact - high.astype(f32)).astype(bf16)
    rate = dense[2] / 12.0
    term = dense[3]
    growth = jnp.log1p(rate)
    coef[0] = dense[0]
    coef[1] = dense[1]
    coef[2] = dense[4]
    rate_high = rate.astype(bf16).astype(f32)
    coef[3] = rate_high
    coef[4] = rate - rate_high
    region = dense[5].astype(jnp.int32)
    home = jnp.zeros_like(region)
    for z in range(1, count):
        home = home + jnp.where(region >= z * regions, 1, 0)
    if count & (count - 1) == 0:
        place = jnp.bitwise_xor(home, me)
    else:
        place = lax.rem(me - home + count, count)
    coef[5] = (region + (place - home) * regions).astype(f32)
    coef[6] = dense[6]
    for t in range(steps):
        coef[7 + t] = 1.0 - 2.0 * (rate / (jnp.exp((term - float(t)) * growth) - 1.0))
    acc[...] = jnp.zeros_like(acc)
    listing = list_ref[...]
    depth_of = lax.broadcasted_iota(jnp.int32, (plan.depth, LANES), 0).astype(f32)

    def loans(c, carry):
        marks, weights, lhs = [], [], []
        for j in range(plan.chunk):
            row = c * plan.chunk + j
            marks.append(jnp.where(depth_of == coef[5, pl.ds(row, 1), :], 1.0, 0.0).astype(bf16))
        h = lax.dot_general(
            table[...], jnp.concatenate(marks, axis=1), (((1,), (0,)), ((), ())), preferred_element_type=f32
        )
        h = h[0 : steps * pad] + h[steps * pad :]
        for j in range(plan.chunk):
            row = c * plan.chunk + j

            def at(i):
                return coef[i, pl.ds(row, 1), :]

            first, second = at(0), at(1)
            held = jnp.broadcast_to(at(2), (pad, LANES))
            parts = [jnp.broadcast_to(at(2), (16, LANES))]
            for t in range(steps):
                stay = 1.0 - jnp.tanh(first - mort_ref[t * pad : (t + 1) * pad, :])
                keep = at(7 + t) - jnp.tanh(second - h[t * pad : (t + 1) * pad, j * LANES : (j + 1) * LANES])
                held = held * keep * (0.25 * stay)
                parts.append(held)
            held = jnp.concatenate(parts, axis=0)
            high = held.astype(bf16)
            low = (held - high.astype(f32)).astype(bf16)
            lhs.append(jnp.concatenate([high, low], axis=0))
            hit = listing == at(6)
            kinds = [jnp.where(hit, 1.0, 0.0), jnp.where(hit, at(3), 0.0), jnp.where(hit, at(4), 0.0)]
            if acc.shape[1] > 3 * plan.deals:
                kinds.append(jnp.zeros((acc.shape[1] - 3 * plan.deals, LANES), f32))
            weights.append(jnp.concatenate(kinds, axis=0).astype(bf16))
        acc[...] += lax.dot_general(
            jnp.concatenate(lhs, axis=1),
            jnp.concatenate(weights, axis=1),
            (((1,), (1,)), ((), ())),
            preferred_element_type=f32,
        )
        return carry

    lax.fori_loop(0, ar // plan.chunk, loans, 0)

    deals, width, rows = plan.deals, plan.width, plan.rows
    lane = lax.broadcasted_iota(jnp.int32, (rows, width), 1)
    lr_rows = plan.lhs_rows

    def sums(first_row, kind):
        wide = None
        for g in range(plan.groups):
            at = first_row + g * rows
            part = acc[at : at + rows, :] + acc[lr_rows + at : lr_rows + at + rows, :]
            if plan.groups > 1:
                part = pltpu.roll(part, (g - kind) * deals % width, 1)
                wide = part if g == 0 else jnp.where(lane >= g * deals, part, wide)
            else:
                wide = part[:, kind * deals : (kind + 1) * deals]
        return wide

    def start_sums(kind):
        part = acc[0:16, :] + acc[lr_rows : lr_rows + 16, :]
        part = part[0:rows]
        if plan.groups == 1:
            return part[:, kind * deals : (kind + 1) * deals]
        wide = None
        for g in range(plan.groups):
            moved = pltpu.roll(part, (g - kind) * deals % width, 1)
            wide = moved if g == 0 else jnp.where(lane >= g * deals, moved, wide)
        return wide

    start = start_sums(0)
    inverse = 1.0 / start
    pools = [start] + [sums(16 + t * pad, 0) for t in range(steps)]
    incomes = [start_sums(1) + start_sums(2)]
    incomes += [sums(16 + t * pad, 1) + sums(16 + t * pad, 2) for t in range(steps - 1)]
    paid_by = [jnp.zeros((rows, width), f32)]
    for t in range(steps):
        paid_by.append(paid_by[-1] + jnp.maximum(pools[t] - pools[t + 1], 0.0) * inverse)
    incomes = [disc_ref[t] * (incomes[t] * inverse) for t in range(steps)]
    ends, opening, coupon = ends_ref[...], open_ref[...], rate_ref[...]
    worth = jnp.zeros_like(opening)
    income = jnp.zeros_like(opening)
    for r in range(rows):
        held = jnp.clip(ends - paid_by[0][r : r + 1], 0.0, opening)
        for t in range(steps):
            later = jnp.clip(ends - paid_by[t + 1][r : r + 1], 0.0, opening)
            due = jnp.sum(coupon * held, axis=0, keepdims=True)
            income = income + held * (incomes[t][r : r + 1] / due)
            worth = worth + (held - later) * (disc_ref[t, r : r + 1, :] - 1.0)
            held = later
        worth = worth + held * (disc_ref[steps - 1, r : r + 1, :] - 1.0)
    gain = (worth + coupon * income) / opening * (100.0 / all_paths)
    if plan.groups > 1:
        whole = gain
        for g in range(1, plan.groups):
            whole = whole + pltpu.roll(gain, g * deals, 1)
        gain = whole
    out_ref[...] = jnp.transpose(gain)[0:deals, :]


def on_device(
    loan_features,
    hazard_coef,
    coupon,
    balance,
    loan_term,
    loan_age,
    loan_region,
    loan_deal,
    region_hpi,
    rate_paths,
    deal_owner,
    tranche_order,
    tranche_share,
    tranche_rate,
):
    count = lax.axis_size("loans")
    loans = coupon.shape[0]
    regions, steps, paths = region_hpi.shape
    deals, tranches = tranche_order.shape
    plan = Plan(count, loans, regions, steps, paths, deals, tranches)
    f32 = jnp.float32
    params = pltpu.CompilerParams(vmem_limit_bytes=VMEM_LIMIT)

    def rows(x):
        return x.reshape(plan.loan_rows, LANES)

    with jax.named_scope("pack"):
        msgs = pl.pallas_call(
            functools.partial(pack_kernel, plan),
            out_shape=[jax.ShapeDtypeStruct((plan.msg_rows, LANES), f32)] * count,
            compiler_params=params,
        )(
            loan_features, hazard_coef, rows(coupon), rows(balance), rows(loan_term), rows(loan_age),
            rows(loan_region), rows(loan_deal), region_hpi,
        )
    with jax.named_scope("exchange"):
        got = [msgs[0]] + [trade(msgs[s], "loans", s, count) for s in range(1, count)]
    with jax.named_scope("deals"):
        tables = pl.pallas_call(
            functools.partial(deal_kernel, plan),
            out_shape=[
                jax.ShapeDtypeStruct((deals, LANES), f32),
                jax.ShapeDtypeStruct((tranches, plan.width), f32),
                jax.ShapeDtypeStruct((tranches, plan.width), f32),
                jax.ShapeDtypeStruct((tranches, plan.width), f32),
                jax.ShapeDtypeStruct((steps * plan.pad, LANES), f32),
                jax.ShapeDtypeStruct((steps, plan.rows, plan.width), f32),
            ],
            scratch_shapes=[
                pltpu.VMEM((paths, LANES), f32),
                pltpu.VMEM((tranches, plan.width), f32),
                pltpu.VMEM((tranches, plan.width), f32),
                pltpu.VMEM((tranches, plan.width), f32),
            ],
            compiler_params=params,
            cost_estimate=pl.CostEstimate(flops=4_000_000_000, bytes_accessed=400_000, transcendentals=0),
        )(deal_owner, tranche_order, tranche_share, tranche_rate, rate_paths)
    with jax.named_scope("value"):
        part = pl.pallas_call(
            functools.partial(value_kernel, plan, float(paths * lax.axis_size("paths"))),
            out_shape=jax.ShapeDtypeStruct((deals, tranches), f32),
            scratch_shapes=[
                pltpu.VMEM((plan.depth, plan.blocks * LANES), f32),
                pltpu.VMEM((steps * plan.pad, plan.depth), f32),
                pltpu.VMEM((2 * steps * plan.pad, plan.depth), jnp.bfloat16),
                pltpu.VMEM((FIELDS, plan.all_rows, LANES), f32),
                pltpu.VMEM((7 + steps, plan.all_rows, LANES), f32),
                pltpu.VMEM((2 * plan.lhs_rows, up(3 * deals, LANES)), f32),
            ],
            compiler_params=params,
        )(*got, *tables)
    with jax.named_scope("total"):
        return sum_over(sum_over(part, "loans"), "paths")


def solution(mesh):
    in_specs = (
        P(("groups", "loans"), None),
        P(),
        P(("groups", "loans")),
        P(("groups", "loans")),
        P(("groups", "loans")),
        P(("groups", "loans")),
        P(("groups", "loans")),
        P(("groups", "loans")),
        P(("groups", "loans"), None, "paths"),
        P(None, None, ("groups", "paths")),
        P("groups", None),
        P("groups", None),
        P("groups", None),
        P("groups", None),
    )
    out_specs = P("groups", None)
    return jax.shard_map(
        on_device, mesh=mesh, in_specs=in_specs, out_specs=out_specs, check_vma=False
    )
```

time: 137 us -> 37.7 us (0.28)
  blocking collectives: 37.2 us -> 0 us
  waiting for transfers between devices: 43.2 us -> 14.4 us
  other arithmetic: 21 us -> 0.62 us
  matrix products: 18 us -> 0 us
  between operations: 13.7 us -> 0.15 us
  starting transfers between devices: 0.04 us -> 12 us
  Pallas kernels: 0 us -> 7.68 us
    psum x3 -> x0, blocking collectives: 37.2 us -> none  [the longest x1 17.1 us: on_device(): mine = lax.psum(ordered, 'loans')]
    all_gather x1 -> x0, waiting for transfers between devices: 30.8 us -> none  [on_device(): piece = lax.all_gather(region_hpi, 'loans', axis=0, tiled=True)]
    dot_general x11 -> x0, matrix products: 18 us -> none  [the longest x6 6.23 us: waterfall(): jnp.einsum('xpj,xjk->xpk', held, ahead_mask, precision=lax.Precision.HIGH...]
    ppermute x0 -> x9, waiting for transfers between devices: none -> 14.4 us  [trade(): return lax.ppermute(x, axis, pairs)]
    ppermute x0 -> x9, starting transfers between devices: none -> 12 us  [trade(): return lax.ppermute(x, axis, pairs)]
    reduce_scatter x1 -> x0, waiting for transfers between devices: 11.7 us -> none  [on_device(): lax.psum_scatter(jnp.dot(block, onehot_deal, precision=highest).reshape(p...]
    div x7 -> x0, other arithmetic: 10.8 us -> none  [the longest x5 9.33 us: waterfall(): flow = paid + inter[:, :, step, None] * coupon_due / denom]
    pallas_call x0 -> x3, Pallas kernels: none -> 7.68 us  [the longest x1 5.95 us: on_device(): pl.pallas_call(functools.partial(value_kernel, plan, float(paths * lax.ax...]
  transfers between devices with their start and end apart: 2 -> 9, of which waited for: 2 -> 5; matrix products, arithmetic and copies ran while one was open for 5% -> 0% of each run, Pallas kernels for 0% -> 3%
where the time goes in v1:
time: 37.7 us; the launch traced here: 37.5 us
  waiting for transfers between devices  14.4 us (38%)
  starting transfers between devices  12 us (32%)
  Pallas kernels  7.68 us (20%)
  local copies, waits for them, and re-layouts  2.65 us (7%)
  other arithmetic  0.62 us (2%)
    ppermute x9, waiting for transfers between devices, trade(): return lax.ppermute(x, axis, pairs)  14.4 us
    ppermute x9, starting transfers between devices, trade(): return lax.ppermute(x, axis, pairs)  12 us
    pallas_call x1, Pallas kernels, on_device(): pl.pallas_call(functools.partial(value_kernel, plan, float(paths * lax.ax...  5.95 us
    unnamed x28, local copies, waits for them, and re-layouts  2.65 us
    pallas_call x1, Pallas kernels, on_device(): pl.pallas_call(functools.partial(deal_kernel, plan), out_shape=[jax.Shape...  0.98 us
    pallas_call x1, Pallas kernels, on_device(): pl.pallas_call(functools.partial(pack_kernel, plan), out_shape=[jax.Shape...  0.76 us
  transfers between devices with their start and end apart: 9, of which 5 were waited for; matrix products, arithmetic and copies ran while one was open for 0% of the time, Pallas kernels for 3%

profile of v1, /device:TPU:0, one launch (start us, length us, event | category | flops | bytes accessed | tf_op | source)
XLA Modules:
  0.0 37.5 jit_solution(1960450279715150116)
XLA Ops:
  0.0 0.8 %copy.15.coef_ref = bf16[128,2]{1,0:T(8,128)(2,1)S(1)} copy(bf16[128,2]{0,1:T(2,128)(2,1)} %param.15) | data formatting | bytes 1024 | tf_op args[1]
  0.8 0.0 copy-start.3
  0.8 0.0 copy-start.4
  0.8 0.0 copy-start.5
  0.8 0.0 copy-start.6
  0.8 1.1 %copy.16.hpi_ref = f32[104,6,128]{2,1,0:T(8,128)S(1)} copy(f32[104,6,128]{2,0,1:T(8,128)} %param.22) | data formatting | bytes 638976 | tf_op args[8]
  1.9 0.0 copy-start.2
  1.9 0.0 copy-start.1
  2.0 0.6 %copy-done.2 = f32[1024]{0:T(1024)S(1)} copy-done((f32[1024]{0:T(1024)S(1)}, f32[1024]{0:T(1024)}, u32[]{:S(2)}) %copy-start.2) | copy-done | bytes 4120
  2.6 0.0 copy-done.1
  2.6 0.8 %pack.1 = (f32[216,128]{1,0:T(8,128)S(1)}, f32[216,128]{1,0:T(8,128)S(1)}, f32[216,128]{1,0:T(8,128)S(1)}, f32[216,128]{1,0:T(8,128)S(1)}) custom-call(bf16[1024,128]{1,0:T(8,128)(2,1)S(1)} %copy-done, bf16[128,2]{1,0:T(8,128)(2,1)S(1)} %copy.15.coef_ref, f32[8,128]{1,0:T(8,128)S(1)} %bitcast.6, f32[8,128]{1,0:T(8,128)S(1)} %bitcast.7, ...), custom_call_target="tpu_custom_call" | custom-call | tf_op jit(solution)/shard_map/pack/pallas_call | solution.py:364
  3.4 3.1 %collective-permute-start = (f32[216,128]{1,0:T(8,128)S(1)}, f32[216,128]{1,0:T(8,128)S(1)}, u32[]{:S(2)}, u32[]{:S(2)}) collective-permute-start(f32[216,128]{1,0:T(8,128)S(1)} %get-tuple-element.16), channel_id=1, source_target_pairs={{0,4},{4,0},{8,12},{12,8},{1,5},{5,1},{9,13},{13,9},{2,6},{6,2},{1... | collective-permute-start | bytes 331784 | tf_op jit(solution)/shard_map/exchange/ppermute | solution.py:36
  6.5 2.6 %collective-permute-start.1 = (f32[216,128]{1,0:T(8,128)S(1)}, f32[216,128]{1,0:T(8,128)S(1)}, u32[]{:S(2)}, u32[]{:S(2)}) collective-permute-start(f32[216,128]{1,0:T(8,128)S(1)} %get-tuple-element.17), channel_id=1, source_target_pairs={{0,8},{4,12},{8,0},{12,4},{1,9},{5,13},{9,1},{13,5},{2,10},{6,14},... | collective-permute-start | bytes 331784 | tf_op jit(solution)/shard_map/exchange/ppermute | solution.py:36
  9.1 0.0 collective-permute-start.2
  9.1 0.1 copy.17.owner_ref
  9.2 1.0 %deals.1 = (f32[32,128]{1,0:T(8,128)S(1)}, f32[64,128]{1,0:T(8,128)S(1)}, f32[64,128]{1,0:T(8,128)S(1)}, f32[64,128]{1,0:T(8,128)S(1)}, f32[192,128]{1,0:T(8,128)S(1)}, /*index=5*/f32[6,8,128]{2,1,0:T(8,128)S(1)}) custom-call(s32[32,1]{1,0:T(8,128)S(1)} %copy.17.owner_ref, s32[32,64]{1,0:T(8,128)S(1)} %copy-done.7, f32[32,64]{1,0:T(8,128)S(1)} %copy-done.8, ...), custom_call_target="tpu_custom_call" | custom-call | flops 4000000000 | bytes 400000 | tf_op jit(solution)/shard_map/deals/pallas_call | solution.py:375
  10.2 0.0 collective-permute-done.refs_1_
  10.2 7.6 %collective-permute-done.1.refs_2_ = f32[216,128]{1,0:T(8,128)S(1)} collective-permute-done((f32[216,128]{1,0:T(8,128)S(1)}, f32[216,128]{1,0:T(8,128)S(1)}, u32[]{:S(2)}, u32[]{:S(2)}) %collective-permute-start.1) | collective-permute-done | bytes 110624 | tf_op jit(solution)/shard_map/exchange/ppermute | solution.py:36
  17.8 0.0 collective-permute-done.2.refs_3_
  17.8 5.9 %value.1 = f32[32,64]{1,0:T(8,128)S(1)} custom-call(f32[216,128]{1,0:T(8,128)S(1)} %get-tuple-element.15.refs_0_, f32[216,128]{1,0:T(8,128)S(1)} %collective-permute-done.refs_1_, f32[216,128]{1,0:T(8,128)S(1)} %collective-permute-done.1.refs_2_, f32[216,128]{1,0:T(8,128)S(1)} %collective-permute-done.2.refs_3_, f32[32,128]{1,0:T(8,128)S(1)} %get-tuple-element.19.refs_4_, ...), custom_call_target="tpu_custom_call" | custom-call | tf_op jit(solution)/shard_map/value/pallas_call | solution.py:395
  23.8 2.8 %collective-permute-start.4 = (f32[32,64]{1,0:T(8,128)S(1)}, f32[32,64]{1,0:T(8,128)S(1)}, u32[]{:S(2)}, u32[]{:S(2)}) collective-permute-start(f32[32,64]{1,0:T(8,128)S(1)} %value.1), channel_id=1, source_target_pairs={{0,8},{4,12},{8,0},{12,4},{1,9},{5,13},{9,1},{13,5},{2,10},{6,14},... | collective-permute-start | bytes 24584 | tf_op jit(solution)/shard_map/total/ppermute | solution.py:36
  26.6 1.3 %collective-permute-start.5 = (f32[32,64]{1,0:T(8,128)S(1)}, f32[32,64]{1,0:T(8,128)S(1)}, u32[]{:S(2)}, u32[]{:S(2)}) collective-permute-start(f32[32,64]{1,0:T(8,128)S(1)} %value.1), channel_id=1, source_target_pairs={{0,12},{4,8},{8,4},{12,0},{1,13},{5,9},{9,5},{13,1},{2,14},{6,10},... | collective-permute-start | bytes 24584 | tf_op jit(solution)/shard_map/total/ppermute | solution.py:36
  27.9 0.0 collective-permute-start.3
  27.9 0.5 %collective-permute-done.4 = f32[32,64]{1,0:T(8,128)S(1)} collective-permute-done((f32[32,64]{1,0:T(8,128)S(1)}, f32[32,64]{1,0:T(8,128)S(1)}, u32[]{:S(2)}, u32[]{:S(2)}) %collective-permute-start.4) | collective-permute-done | bytes 8224 | tf_op jit(solution)/shard_map/total/ppermute | solution.py:36
  28.5 3.7 %collective-permute-done.5 = f32[32,64]{1,0:T(8,128)S(1)} collective-permute-done((f32[32,64]{1,0:T(8,128)S(1)}, f32[32,64]{1,0:T(8,128)S(1)}, u32[]{:S(2)}, u32[]{:S(2)}) %collective-permute-start.5) | collective-permute-done | bytes 8224 | tf_op jit(solution)/shard_map/total/ppermute | solution.py:36
  32.1 0.0 collective-permute-done.3
  32.2 1.6 %collective-permute-start.7 = (f32[32,64]{1,0:T(8,128)S(1)}, f32[32,64]{1,0:T(8,128)S(1)}, u32[]{:S(2)}, u32[]{:S(2)}) collective-permute-start(f32[32,64]{1,0:T(8,128)S(1)} %add_add_fusion.1), channel_id=1, source_target_pairs={{0,2},{1,3},{2,0},{3,1},{4,6},{5,7},{6,4},{7,5},{8,10},{9,11},{10,... | collective-permute-start | bytes 24584 | tf_op jit(solution)/shard_map/total/ppermute | solution.py:36
  33.7 0.0 collective-permute-start.8
  33.7 0.6 %collective-permute-start.6 = (f32[32,64]{1,0:T(8,128)S(1)}, f32[32,64]{1,0:T(8,128)S(1)}, u32[]{:S(2)}, u32[]{:S(2)}) collective-permute-start(f32[32,64]{1,0:T(8,128)S(1)} %add_add_fusion.1), channel_id=1, source_target_pairs={{0,1},{1,0},{2,3},{3,2},{4,5},{5,4},{6,7},{7,6},{8,9},{9,8},{10,11... | collective-permute-start | bytes 24584 | tf_op jit(solution)/shard_map/total/ppermute | solution.py:36
  34.4 1.6 %collective-permute-done.7 = f32[32,64]{1,0:T(8,128)S(1)} collective-permute-done((f32[32,64]{1,0:T(8,128)S(1)}, f32[32,64]{1,0:T(8,128)S(1)}, u32[]{:S(2)}, u32[]{:S(2)}) %collective-permute-start.7) | collective-permute-done | bytes 8224 | tf_op jit(solution)/shard_map/total/ppermute | solution.py:36
  36.0 0.9 %collective-permute-done.8 = f32[32,64]{1,0:T(8,128)S(1)} collective-permute-done((f32[32,64]{1,0:T(8,128)S(1)}, f32[32,64]{1,0:T(8,128)S(1)}, u32[]{:S(2)}, u32[]{:S(2)}) %collective-permute-start.8) | collective-permute-done | bytes 8224 | tf_op jit(solution)/shard_map/total/ppermute | solution.py:36
  36.9 0.6 %add_add_fusion = f32[32,64]{1,0:T(8,128)} fusion(f32[32,64]{1,0:T(8,128)S(1)} %collective-permute-done.7, f32[32,64]{1,0:T(8,128)S(1)} %collective-permute-done.8, f32[32,64]{1,0:T(8,128)S(1)} %add_add_fusion.1, f32[32,64]{1,0:T(8,128)S(1)} %collective-permute-done.6), kind=kLoop, calls=%fused_computation | loop fusion | flops 6144 | bytes 40960 | tf_op jit(solution)/shard_map/total/add | solution.py:45
  (19 shorter events, 0.0 us)
Async XLA Ops:
  0.8 1.2 %copy-start = (bf16[1024,128]{1,0:T(8,128)(2,1)S(1)}, bf16[1024,128]{1,0:T(8,128)(2,1)}, u32[]{:S(2)}) copy-start(bf16[1024,128]{1,0:T(8,128)(2,1)} %feat_ref.1) | copy-start | bytes 786436
  0.8 1.2 %copy-start.3 = (s32[1024]{0:T(1024)S(1)}, s32[1024]{0:T(1024)}, u32[]{:S(2)}) copy-start(s32[1024]{0:T(1024)} %param.18) | copy-start | bytes 12292
  0.8 1.2 %copy-start.4 = (s32[1024]{0:T(1024)S(1)}, s32[1024]{0:T(1024)}, u32[]{:S(2)}) copy-start(s32[1024]{0:T(1024)} %param.19) | copy-start | bytes 12292
  0.8 1.2 %copy-start.5 = (s32[1024]{0:T(1024)S(1)}, s32[1024]{0:T(1024)}, u32[]{:S(2)}) copy-start(s32[1024]{0:T(1024)} %param.20) | copy-start | bytes 12292
  0.8 1.2 %copy-start.6 = (s32[1024]{0:T(1024)S(1)}, s32[1024]{0:T(1024)}, u32[]{:S(2)}) copy-start(s32[1024]{0:T(1024)} %param.21) | copy-start | bytes 12292
  1.9 0.7 %copy-start.2 = (f32[1024]{0:T(1024)S(1)}, f32[1024]{0:T(1024)}, u32[]{:S(2)}) copy-start(f32[1024]{0:T(1024)} %param.17) | copy-start | bytes 12292
  1.9 0.7 %copy-start.1 = (f32[1024]{0:T(1024)S(1)}, f32[1024]{0:T(1024)}, u32[]{:S(2)}) copy-start(f32[1024]{0:T(1024)} %param.16) | copy-start | bytes 12292
  2.6 6.6 %copy-start.10 = (f32[2,6,128]{2,0,1:T(2,128)S(1)}, f32[2,6,128]{2,0,1:T(2,128)}, u32[]{:S(2)}) copy-start(f32[2,6,128]{2,0,1:T(2,128)} %param.23) | copy-start | bytes 18436
  2.6 6.6 %copy-start.9 = (f32[32,64]{1,0:T(8,128)S(1)}, f32[32,64]{1,0:T(8,128)}, u32[]{:S(2)}) copy-start(f32[32,64]{1,0:T(8,128)} %rate_ref.1) | copy-start | bytes 24580
  3.4 6.8 %collective-permute-start = (f32[216,128]{1,0:T(8,128)S(1)}, f32[216,128]{1,0:T(8,128)S(1)}, u32[]{:S(2)}, u32[]{:S(2)}) collective-permute-start(f32[216,128]{1,0:T(8,128)S(1)} %get-tuple-element.16), channel_id=1, source_target_pairs={{0,4},{4,0},{8,12},{12,8},{1,5},{5,1},{9,13},{13,9},{2,6},{6,2},{1... | collective-permute-start | bytes 331784 | tf_op jit(solution)/shard_map/exchange/ppermute | solution.py:36
  6.5 2.6 %copy-start.11 = (s32[32,1]{0,1:T(1,128)S(1)}, s32[32,1]{0,1:T(1,128)}, u32[]{:S(2)}) copy-start(s32[32,1]{0,1:T(1,128)} %param.24) | copy-start | bytes 388
  6.5 2.7 %copy-start.7 = (s32[32,64]{1,0:T(8,128)S(1)}, s32[32,64]{1,0:T(8,128)}, u32[]{:S(2)}) copy-start(s32[32,64]{1,0:T(8,128)} %order_ref.1) | copy-start | bytes 24580
  6.5 2.7 %copy-start.8 = (f32[32,64]{1,0:T(8,128)S(1)}, f32[32,64]{1,0:T(8,128)}, u32[]{:S(2)}) copy-start(f32[32,64]{1,0:T(8,128)} %share_ref.1) | copy-start | bytes 24580
  6.5 11.3 %collective-permute-start.1 = (f32[216,128]{1,0:T(8,128)S(1)}, f32[216,128]{1,0:T(8,128)S(1)}, u32[]{:S(2)}, u32[]{:S(2)}) collective-permute-start(f32[216,128]{1,0:T(8,128)S(1)} %get-tuple-element.17), channel_id=1, source_target_pairs={{0,8},{4,12},{8,0},{12,4},{1,9},{5,13},{9,1},{13,5},{2,10},{6,14},... | collective-permute-start | bytes 331784 | tf_op jit(solution)/shard_map/exchange/ppermute | solution.py:36
  9.1 8.8 %collective-permute-start.2 = (f32[216,128]{1,0:T(8,128)S(1)}, f32[216,128]{1,0:T(8,128)S(1)}, u32[]{:S(2)}, u32[]{:S(2)}) collective-permute-start(f32[216,128]{1,0:T(8,128)S(1)} %get-tuple-element.18), channel_id=1, source_target_pairs={{0,12},{4,8},{8,4},{12,0},{1,13},{5,9},{9,5},{13,1},{2,14},{6,10},... | collective-permute-start | bytes 331784 | tf_op jit(solution)/shard_map/exchange/ppermute | solution.py:36
  23.8 4.7 %collective-permute-start.4 = (f32[32,64]{1,0:T(8,128)S(1)}, f32[32,64]{1,0:T(8,128)S(1)}, u32[]{:S(2)}, u32[]{:S(2)}) collective-permute-start(f32[32,64]{1,0:T(8,128)S(1)} %value.1), channel_id=1, source_target_pairs={{0,8},{4,12},{8,0},{12,4},{1,9},{5,13},{9,1},{13,5},{2,10},{6,14},... | collective-permute-start | bytes 24584 | tf_op jit(solution)/shard_map/total/ppermute | solution.py:36
  26.6 5.5 %collective-permute-start.5 = (f32[32,64]{1,0:T(8,128)S(1)}, f32[32,64]{1,0:T(8,128)S(1)}, u32[]{:S(2)}, u32[]{:S(2)}) collective-permute-start(f32[32,64]{1,0:T(8,128)S(1)} %value.1), channel_id=1, source_target_pairs={{0,12},{4,8},{8,4},{12,0},{1,13},{5,9},{9,5},{13,1},{2,14},{6,10},... | collective-permute-start | bytes 24584 | tf_op jit(solution)/shard_map/total/ppermute | solution.py:36
  27.9 4.2 %collective-permute-start.3 = (f32[32,64]{1,0:T(8,128)S(1)}, f32[32,64]{1,0:T(8,128)S(1)}, u32[]{:S(2)}, u32[]{:S(2)}) collective-permute-start(f32[32,64]{1,0:T(8,128)S(1)} %value.1), channel_id=1, source_target_pairs={{0,4},{4,0},{8,12},{12,8},{1,5},{5,1},{9,13},{13,9},{2,6},{6,2},{1... | collective-permute-start | bytes 24584 | tf_op jit(solution)/shard_map/total/ppermute | solution.py:36
  32.2 3.8 %collective-permute-start.7 = (f32[32,64]{1,0:T(8,128)S(1)}, f32[32,64]{1,0:T(8,128)S(1)}, u32[]{:S(2)}, u32[]{:S(2)}) collective-permute-start(f32[32,64]{1,0:T(8,128)S(1)} %add_add_fusion.1), channel_id=1, source_target_pairs={{0,2},{1,3},{2,0},{3,1},{4,6},{5,7},{6,4},{7,5},{8,10},{9,11},{10,... | collective-permute-start | bytes 24584 | tf_op jit(solution)/shard_map/total/ppermute | solution.py:36
  33.7 3.2 %collective-permute-start.8 = (f32[32,64]{1,0:T(8,128)S(1)}, f32[32,64]{1,0:T(8,128)S(1)}, u32[]{:S(2)}, u32[]{:S(2)}) collective-permute-start(f32[32,64]{1,0:T(8,128)S(1)} %add_add_fusion.1), channel_id=1, source_target_pairs={{0,3},{1,2},{2,1},{3,0},{4,7},{5,6},{6,5},{7,4},{8,11},{9,10},{10,... | collective-permute-start | bytes 24584 | tf_op jit(solution)/shard_map/total/ppermute | solution.py:36
  33.7 3.2 %collective-permute-start.6 = (f32[32,64]{1,0:T(8,128)S(1)}, f32[32,64]{1,0:T(8,128)S(1)}, u32[]{:S(2)}, u32[]{:S(2)}) collective-permute-start(f32[32,64]{1,0:T(8,128)S(1)} %add_add_fusion.1), channel_id=1, source_target_pairs={{0,1},{1,0},{2,3},{3,2},{4,5},{5,4},{6,7},{7,6},{8,9},{9,8},{10,11... | collective-permute-start | bytes 24584 | tf_op jit(solution)/shard_map/total/ppermute | solution.py:36

commit v2 on v1

--- a/solution.py
+++ b/solution.py
@@ -68,14 +68,24 @@
         self.rows = self.mine // self.groups
         self.width = self.groups * deals
         self.all_rows = count * self.loan_rows
-        self.chunk = 4
+        self.chunk = 16
         self.lhs_rows = 16 + steps * self.pad
-
-
-def pack_kernel(plan, feat_ref, coef_ref, coupon_ref, balance_ref, term_ref, age_ref, region_ref, deal_ref, hpi_ref, *outs):
+        self.order = [0,3,2,1] if count == 4 else list(range(count))
+
+
+def pack_kernel(plan, *refs):
     me = lax.axis_index("loans")
+    outs = refs[9 : 9 + plan.count]
+    here = refs[9 + plan.count : -1]
+    sems = refs[-1]
+    copies = [pltpu.make_async_copy(refs[i], here[i], sems.at[i]) for i in range(9)]
+    for copy in copies[::-1]:
+        copy.start()
+    for copy in copies:
+        copy.wait()
+    feat_ref, coef_ref, coupon_ref, balance_ref, term_ref, age_ref, region_ref, deal_ref, hpi_ref = here
     covar = lax.dot_general(
-        coef_ref[...], feat_ref[...], (((0,), (1,)), ((), ())), preferred_element_type=jnp.float32
+        coef_ref[...], feat_ref[...], (((1,), (1,)), ((), ())), preferred_element_type=jnp.float32
     )
     base, lr = plan.hpi_rows, plan.loan_rows
     rows0 = jnp.concatenate([covar[0:1, LANES * i : LANES * (i + 1)] for i in range(lr)], axis=0)
@@ -91,7 +101,7 @@
         deal_ref[...].astype(jnp.float32),
     )
     regions, mine, per = plan.regions, plan.mine, plan.months_per
-    months = [hpi_ref[:, t, :] for t in range(plan.steps)]
+    months = [hpi_ref[t] for t in range(plan.steps)]
     lane = lax.broadcasted_iota(jnp.int32, (regions, LANES), 1)
     for s, out in enumerate(outs):
         start = peer(me, s, plan.count) * mine
@@ -178,7 +188,7 @@
 
 def value_kernel(plan, all_paths, *refs):
     count = plan.count
-    msgs = refs[:count]
+    msgs = {s: refs[i] for i, s in enumerate(plan.order)}
     list_ref, ends_ref, open_ref, rate_ref, mort_ref, disc_ref, out_ref = refs[count : count + 7]
     gather, spots, table, dense, coef, acc = refs[count + 7 :]
     f32, bf16 = jnp.float32, jnp.bfloat16
@@ -187,7 +197,7 @@
     lr, base, ar = plan.loan_rows, plan.hpi_rows, plan.all_rows
     if count * regions < plan.depth:
         gather[count * regions :, :] = jnp.zeros((plan.depth - count * regions, plan.blocks * LANES), f32)
-    for s, msg in enumerate(msgs):
+    for s, msg in msgs.items():
         for b in range(plan.full):
             gather[s * regions : (s + 1) * regions, b * LANES : (b + 1) * LANES] = msg[b * regions : (b + 1) * regions, :]
         rr = plan.rem_rows
@@ -232,13 +242,13 @@
         coef[7 + t] = 1.0 - 2.0 * (rate / (jnp.exp((term - float(t)) * growth) - 1.0))
     acc[...] = jnp.zeros_like(acc)
     listing = list_ref[...]
-    depth_of = lax.broadcasted_iota(jnp.int32, (plan.depth, LANES), 0).astype(f32)
+    depth_of = lax.broadcasted_iota(jnp.int16, (plan.depth, LANES), 0)
 
     def loans(c, carry):
         marks, weights, lhs = [], [], []
         for j in range(plan.chunk):
             row = c * plan.chunk + j
-            marks.append(jnp.where(depth_of == coef[5, pl.ds(row, 1), :], 1.0, 0.0).astype(bf16))
+            marks.append(jnp.where(depth_of == coef[5, pl.ds(row, 1), :].astype(jnp.int32).astype(jnp.int16), jnp.array(1.0,bf16), jnp.array(0.0,bf16)))
         h = lax.dot_general(
             table[...], jnp.concatenate(marks, axis=1), (((1,), (0,)), ((), ())), preferred_element_type=f32
         )
@@ -360,17 +370,20 @@
     def rows(x):
         return x.reshape(plan.loan_rows, LANES)
 
+    given = (
+        loan_features, hazard_coef.T, rows(coupon), rows(balance), rows(loan_term), rows(loan_age),
+        rows(loan_region), rows(loan_deal), region_hpi.transpose(1, 0, 2),
+    )
     with jax.named_scope("pack"):
         msgs = pl.pallas_call(
             functools.partial(pack_kernel, plan),
             out_shape=[jax.ShapeDtypeStruct((plan.msg_rows, LANES), f32)] * count,
-            compiler_params=params,
-        )(
-            loan_features, hazard_coef, rows(coupon), rows(balance), rows(loan_term), rows(loan_age),
-            rows(loan_region), rows(loan_deal), region_hpi,
-        )
+            in_specs=[pl.BlockSpec(memory_space=pltpu.HBM)] * len(given),
+            scratch_shapes=[pltpu.VMEM(x.shape, x.dtype) for x in given] + [pltpu.SemaphoreType.DMA((len(given),))],
+            compiler_params=pltpu.CompilerParams(vmem_limit_bytes=56 * 1024 * 1024),
+        )(*given)
     with jax.named_scope("exchange"):
-        got = [msgs[0]] + [trade(msgs[s], "loans", s, count) for s in range(1, count)]
+        got = [trade(msgs[s], "loans", s, count) if s else msgs[s] for s in plan.order]
     with jax.named_scope("deals"):
         tables = pl.pallas_call(
             functools.partial(deal_kernel, plan),

time: 37.7 us -> 33.2 us (0.88)
  local copies, waits for them, and re-layouts: 2.65 us -> 0.11 us
  waiting for transfers between devices: 14.4 us -> 13.1 us
  starting transfers between devices: 12 us -> 11.5 us
    unnamed x28 -> x14, local copies, waits for them, and re-layouts: 2.65 us -> 0.11 us
    pallas_call x1, Pallas kernels: 5.95 us -> 4.05 us  [on_device(): pl.pallas_call(functools.partial(value_kernel, plan, float(paths * lax.ax...]
    pallas_call x1, Pallas kernels: 0.76 us -> 2.58 us  [on_device(): pl.pallas_call(functools.partial(pack_kernel, plan), out_shape=[jax.Shape...]
    ppermute x9, waiting for transfers between devices: 14.4 us -> 13.1 us  [trade(): return lax.ppermute(x, axis, pairs)]
    ppermute x9, starting transfers between devices: 12 us -> 11.5 us  [trade(): return lax.ppermute(x, axis, pairs)]
  transfers between devices with their start and end apart: 9 -> 9, of which waited for: 5 -> 7; matrix products, arithmetic and copies ran while one was open for 0% -> 0% of each run, Pallas kernels for 3% -> 3%
where the time goes in v2:
time: 33.2 us; the launch traced here: 33 us
  waiting for transfers between devices  13.1 us (39%)
  starting transfers between devices  11.5 us (35%)
  Pallas kernels  7.61 us (23%)
  other arithmetic  0.62 us (2%)
    ppermute x9, waiting for transfers between devices, trade(): return lax.ppermute(x, axis, pairs)  13.1 us
    ppermute x9, starting transfers between devices, trade(): return lax.ppermute(x, axis, pairs)  11.5 us
    pallas_call x1, Pallas kernels, on_device(): pl.pallas_call(functools.partial(value_kernel, plan, float(paths * lax.ax...  4.05 us
    pallas_call x1, Pallas kernels, on_device(): pl.pallas_call(functools.partial(pack_kernel, plan), out_shape=[jax.Shape...  2.58 us
    pallas_call x1, Pallas kernels, on_device(): pl.pallas_call(functools.partial(deal_kernel, plan), out_shape=[jax.Shape...  0.98 us
  transfers between devices with their start and end apart: 9, of which 7 were waited for; matrix products, arithmetic and copies ran while one was open for 0% of the time, Pallas kernels for 3%

profile of v2, /device:TPU:0, one launch (start us, length us, event | category | flops | bytes accessed | tf_op | source)
XLA Modules:
  0.0 33.0 jit_solution(1756547127996632804)
XLA Ops:
  0.0 0.0 copy-start.4
  0.0 0.0 copy-start.3
  0.0 2.6 %pack.1 = (f32[216,128]{1,0:T(8,128)}, f32[216,128]{1,0:T(8,128)}, f32[216,128]{1,0:T(8,128)}, f32[216,128]{1,0:T(8,128)}) custom-call(bf16[1024,128]{1,0:T(8,128)(2,1)} %refs_0_.1, bf16[2,128]{1,0:T(2,128)(2,1)} %bitcast.15, f32[8,128]{1,0:T(8,128)} %bitcast.9, f32[8,128]{1,0:T(8,128)} %bitcast.10, s32[8,128]{1,0:T(8,128)} %bitcast.11, s32[8,128]{1,0:T(8,128)} %bitcast.12, ...), custom_call_target="tpu_custom_call" | custom-call | tf_op jit(solution)/shard_map/pack/pallas_call | solution.py:378
  2.6 5.1 %collective-permute-start = (f32[216,128]{1,0:T(8,128)}, f32[216,128]{1,0:T(8,128)S(1)}, u32[]{:S(2)}, u32[]{:S(2)}) collective-permute-start(f32[216,128]{1,0:T(8,128)} %get-tuple-element.16), channel_id=1, source_target_pairs={{0,12},{4,8},{8,4},{12,0},{1,13},{5,9},{9,5},{13,1},{2,14},{6,10},... | collective-permute-start | bytes 331784 | tf_op jit(solution)/shard_map/exchange/ppermute | solution.py:36
  7.7 0.0 collective-permute-start.1
  7.7 0.7 %collective-permute-start.2 = (f32[216,128]{1,0:T(8,128)}, f32[216,128]{1,0:T(8,128)S(1)}, u32[]{:S(2)}, u32[]{:S(2)}) collective-permute-start(f32[216,128]{1,0:T(8,128)} %get-tuple-element.18), channel_id=1, source_target_pairs={{0,4},{4,0},{8,12},{12,8},{1,5},{5,1},{9,13},{13,9},{2,6},{6,2},{1... | collective-permute-start | bytes 331784 | tf_op jit(solution)/shard_map/exchange/ppermute | solution.py:36
  8.4 0.0 copy-done.5
  8.4 0.1 copy.15.owner_ref
  8.5 0.0 copy-done.4
  8.5 0.0 copy-done.3
  8.5 0.0 copy-done.1
  8.5 0.0 copy-done.2
  8.5 0.0 copy-start
  8.5 1.0 %deals.1 = (f32[32,128]{1,0:T(8,128)S(1)}, f32[64,128]{1,0:T(8,128)S(1)}, f32[64,128]{1,0:T(8,128)S(1)}, f32[64,128]{1,0:T(8,128)S(1)}, f32[192,128]{1,0:T(8,128)S(1)}, /*index=5*/f32[6,8,128]{2,1,0:T(8,128)S(1)}) custom-call(s32[32,1]{1,0:T(8,128)S(1)} %copy.15.owner_ref, s32[32,64]{1,0:T(8,128)S(1)} %copy-done.1, f32[32,64]{1,0:T(8,128)S(1)} %copy-done.2, ...), custom_call_target="tpu_custom_call" | custom-call | flops 4000000000 | bytes 400000 | tf_op jit(solution)/shard_map/deals/pallas_call | solution.py:388
  9.5 2.4 %collective-permute-done.refs_1_ = f32[216,128]{1,0:T(8,128)S(1)} collective-permute-done((f32[216,128]{1,0:T(8,128)}, f32[216,128]{1,0:T(8,128)S(1)}, u32[]{:S(2)}, u32[]{:S(2)}) %collective-permute-start) | collective-permute-done | bytes 110624 | tf_op jit(solution)/shard_map/exchange/ppermute | solution.py:36
  11.9 5.3 %collective-permute-done.1.refs_2_ = f32[216,128]{1,0:T(8,128)S(1)} collective-permute-done((f32[216,128]{1,0:T(8,128)}, f32[216,128]{1,0:T(8,128)S(1)}, u32[]{:S(2)}, u32[]{:S(2)}) %collective-permute-start.1) | collective-permute-done | bytes 110624 | tf_op jit(solution)/shard_map/exchange/ppermute | solution.py:36
  17.2 0.0 collective-permute-done.2.refs_3_
  17.2 0.0 copy-done
  17.2 4.0 %value.1 = f32[32,64]{1,0:T(8,128)S(1)} custom-call(f32[216,128]{1,0:T(8,128)S(1)} %copy-done, f32[216,128]{1,0:T(8,128)S(1)} %collective-permute-done.refs_1_, f32[216,128]{1,0:T(8,128)S(1)} %collective-permute-done.1.refs_2_, f32[216,128]{1,0:T(8,128)S(1)} %collective-permute-done.2.refs_3_, f32[32,128]{1,0:T(8,128)S(1)} %get-tuple-element.19.refs_4_, ...), custom_call_target="tpu_custom_call" | custom-call | tf_op jit(solution)/shard_map/value/pallas_call | solution.py:408
  21.3 0.4 %collective-permute-start.4 = (f32[32,64]{1,0:T(8,128)S(1)}, f32[32,64]{1,0:T(8,128)S(1)}, u32[]{:S(2)}, u32[]{:S(2)}) collective-permute-start(f32[32,64]{1,0:T(8,128)S(1)} %value.1), channel_id=1, source_target_pairs={{0,8},{4,12},{8,0},{12,4},{1,9},{5,13},{9,1},{13,5},{2,10},{6,14},... | collective-permute-start | bytes 24584 | tf_op jit(solution)/shard_map/total/ppermute | solution.py:36
  21.7 2.3 %collective-permute-start.5 = (f32[32,64]{1,0:T(8,128)S(1)}, f32[32,64]{1,0:T(8,128)S(1)}, u32[]{:S(2)}, u32[]{:S(2)}) collective-permute-start(f32[32,64]{1,0:T(8,128)S(1)} %value.1), channel_id=1, source_target_pairs={{0,12},{4,8},{8,4},{12,0},{1,13},{5,9},{9,5},{13,1},{2,14},{6,10},... | collective-permute-start | bytes 24584 | tf_op jit(solution)/shard_map/total/ppermute | solution.py:36
  23.9 0.9 %collective-permute-start.3 = (f32[32,64]{1,0:T(8,128)S(1)}, f32[32,64]{1,0:T(8,128)S(1)}, u32[]{:S(2)}, u32[]{:S(2)}) collective-permute-start(f32[32,64]{1,0:T(8,128)S(1)} %value.1), channel_id=1, source_target_pairs={{0,4},{4,0},{8,12},{12,8},{1,5},{5,1},{9,13},{13,9},{2,6},{6,2},{1... | collective-permute-start | bytes 24584 | tf_op jit(solution)/shard_map/total/ppermute | solution.py:36
  24.8 1.1 %collective-permute-done.4 = f32[32,64]{1,0:T(8,128)S(1)} collective-permute-done((f32[32,64]{1,0:T(8,128)S(1)}, f32[32,64]{1,0:T(8,128)S(1)}, u32[]{:S(2)}, u32[]{:S(2)}) %collective-permute-start.4) | collective-permute-done | bytes 8224 | tf_op jit(solution)/shard_map/total/ppermute | solution.py:36
  26.0 1.3 %collective-permute-done.5 = f32[32,64]{1,0:T(8,128)S(1)} collective-permute-done((f32[32,64]{1,0:T(8,128)S(1)}, f32[32,64]{1,0:T(8,128)S(1)}, u32[]{:S(2)}, u32[]{:S(2)}) %collective-permute-start.5) | collective-permute-done | bytes 8224 | tf_op jit(solution)/shard_map/total/ppermute | solution.py:36
  27.2 0.5 %collective-permute-done.3 = f32[32,64]{1,0:T(8,128)S(1)} collective-permute-done((f32[32,64]{1,0:T(8,128)S(1)}, f32[32,64]{1,0:T(8,128)S(1)}, u32[]{:S(2)}, u32[]{:S(2)}) %collective-permute-start.3) | collective-permute-done | bytes 8224 | tf_op jit(solution)/shard_map/total/ppermute | solution.py:36
  27.7 1.6 %collective-permute-start.7 = (f32[32,64]{1,0:T(8,128)S(1)}, f32[32,64]{1,0:T(8,128)S(1)}, u32[]{:S(2)}, u32[]{:S(2)}) collective-permute-start(f32[32,64]{1,0:T(8,128)S(1)} %add_add_fusion.1), channel_id=1, source_target_pairs={{0,2},{1,3},{2,0},{3,1},{4,6},{5,7},{6,4},{7,5},{8,10},{9,11},{10,... | collective-permute-start | bytes 24584 | tf_op jit(solution)/shard_map/total/ppermute | solution.py:36
  29.2 0.0 collective-permute-start.8
  29.2 0.6 %collective-permute-start.6 = (f32[32,64]{1,0:T(8,128)S(1)}, f32[32,64]{1,0:T(8,128)S(1)}, u32[]{:S(2)}, u32[]{:S(2)}) collective-permute-start(f32[32,64]{1,0:T(8,128)S(1)} %add_add_fusion.1), channel_id=1, source_target_pairs={{0,1},{1,0},{2,3},{3,2},{4,5},{5,4},{6,7},{7,6},{8,9},{9,8},{10,11... | collective-permute-start | bytes 24584 | tf_op jit(solution)/shard_map/total/ppermute | solution.py:36
  29.9 1.6 %collective-permute-done.7 = f32[32,64]{1,0:T(8,128)S(1)} collective-permute-done((f32[32,64]{1,0:T(8,128)S(1)}, f32[32,64]{1,0:T(8,128)S(1)}, u32[]{:S(2)}, u32[]{:S(2)}) %collective-permute-start.7) | collective-permute-done | bytes 8224 | tf_op jit(solution)/shard_map/total/ppermute | solution.py:36
  31.5 0.9 %collective-permute-done.8 = f32[32,64]{1,0:T(8,128)S(1)} collective-permute-done((f32[32,64]{1,0:T(8,128)S(1)}, f32[32,64]{1,0:T(8,128)S(1)}, u32[]{:S(2)}, u32[]{:S(2)}) %collective-permute-start.8) | collective-permute-done | bytes 8224 | tf_op jit(solution)/shard_map/total/ppermute | solution.py:36
  32.4 0.0 collective-permute-done.6
  32.4 0.6 %add_add_fusion = f32[32,64]{1,0:T(8,128)} fusion(f32[32,64]{1,0:T(8,128)S(1)} %collective-permute-done.7, f32[32,64]{1,0:T(8,128)S(1)} %collective-permute-done.8, f32[32,64]{1,0:T(8,128)S(1)} %add_add_fusion.1, f32[32,64]{1,0:T(8,128)S(1)} %collective-permute-done.6), kind=kLoop, calls=%fused_computation | loop fusion | flops 6144 | bytes 40960 | tf_op jit(solution)/shard_map/total/add | solution.py:45
  (5 shorter events, 0.0 us)
Async XLA Ops:
  0.0 8.5 %copy-start.4 = (f32[2,6,128]{2,0,1:T(2,128)S(1)}, f32[2,6,128]{2,0,1:T(2,128)}, u32[]{:S(2)}) copy-start(f32[2,6,128]{2,0,1:T(2,128)} %param.23) | copy-start | bytes 18436
  0.0 8.5 %copy-start.3 = (f32[32,64]{1,0:T(8,128)S(1)}, f32[32,64]{1,0:T(8,128)}, u32[]{:S(2)}) copy-start(f32[32,64]{1,0:T(8,128)} %rate_ref.1) | copy-start | bytes 24580
  2.6 9.3 %collective-permute-start = (f32[216,128]{1,0:T(8,128)}, f32[216,128]{1,0:T(8,128)S(1)}, u32[]{:S(2)}, u32[]{:S(2)}) collective-permute-start(f32[216,128]{1,0:T(8,128)} %get-tuple-element.16), channel_id=1, source_target_pairs={{0,12},{4,8},{8,4},{12,0},{1,13},{5,9},{9,5},{13,1},{2,14},{6,10},... | collective-permute-start | bytes 331784 | tf_op jit(solution)/shard_map/exchange/ppermute | solution.py:36
  7.7 0.7 %copy-start.5 = (s32[32,1]{0,1:T(1,128)S(1)}, s32[32,1]{0,1:T(1,128)}, u32[]{:S(2)}) copy-start(s32[32,1]{0,1:T(1,128)} %param.24) | copy-start | bytes 388
  7.7 0.8 %copy-start.1 = (s32[32,64]{1,0:T(8,128)S(1)}, s32[32,64]{1,0:T(8,128)}, u32[]{:S(2)}) copy-start(s32[32,64]{1,0:T(8,128)} %order_ref.1) | copy-start | bytes 24580
  7.7 0.8 %copy-start.2 = (f32[32,64]{1,0:T(8,128)S(1)}, f32[32,64]{1,0:T(8,128)}, u32[]{:S(2)}) copy-start(f32[32,64]{1,0:T(8,128)} %share_ref.1) | copy-start | bytes 24580
  7.7 9.5 %collective-permute-start.1 = (f32[216,128]{1,0:T(8,128)}, f32[216,128]{1,0:T(8,128)S(1)}, u32[]{:S(2)}, u32[]{:S(2)}) collective-permute-start(f32[216,128]{1,0:T(8,128)} %get-tuple-element.17), channel_id=1, source_target_pairs={{0,8},{4,12},{8,0},{12,4},{1,9},{5,13},{9,1},{13,5},{2,10},{6,14},... | collective-permute-start | bytes 331784 | tf_op jit(solution)/shard_map/exchange/ppermute | solution.py:36
  7.7 9.5 %collective-permute-start.2 = (f32[216,128]{1,0:T(8,128)}, f32[216,128]{1,0:T(8,128)S(1)}, u32[]{:S(2)}, u32[]{:S(2)}) collective-permute-start(f32[216,128]{1,0:T(8,128)} %get-tuple-element.18), channel_id=1, source_target_pairs={{0,4},{4,0},{8,12},{12,8},{1,5},{5,1},{9,13},{13,9},{2,6},{6,2},{1... | collective-permute-start | bytes 331784 | tf_op jit(solution)/shard_map/exchange/ppermute | solution.py:36
  8.5 8.7 %copy-start = (f32[216,128]{1,0:T(8,128)S(1)}, f32[216,128]{1,0:T(8,128)}, u32[]{:S(2)}) copy-start(f32[216,128]{1,0:T(8,128)} %get-tuple-element.15.refs_0_) | copy-start | bytes 331780
  21.3 4.7 %collective-permute-start.4 = (f32[32,64]{1,0:T(8,128)S(1)}, f32[32,64]{1,0:T(8,128)S(1)}, u32[]{:S(2)}, u32[]{:S(2)}) collective-permute-start(f32[32,64]{1,0:T(8,128)S(1)} %value.1), channel_id=1, source_target_pairs={{0,8},{4,12},{8,0},{12,4},{1,9},{5,13},{9,1},{13,5},{2,10},{6,14},... | collective-permute-start | bytes 24584 | tf_op jit(solution)/shard_map/total/ppermute | solution.py:36
  21.7 5.5 %collective-permute-start.5 = (f32[32,64]{1,0:T(8,128)S(1)}, f32[32,64]{1,0:T(8,128)S(1)}, u32[]{:S(2)}, u32[]{:S(2)}) collective-permute-start(f32[32,64]{1,0:T(8,128)S(1)} %value.1), channel_id=1, source_target_pairs={{0,12},{4,8},{8,4},{12,0},{1,13},{5,9},{9,5},{13,1},{2,14},{6,10},... | collective-permute-start | bytes 24584 | tf_op jit(solution)/shard_map/total/ppermute | solution.py:36
  23.9 3.7 %collective-permute-start.3 = (f32[32,64]{1,0:T(8,128)S(1)}, f32[32,64]{1,0:T(8,128)S(1)}, u32[]{:S(2)}, u32[]{:S(2)}) collective-permute-start(f32[32,64]{1,0:T(8,128)S(1)} %value.1), channel_id=1, source_target_pairs={{0,4},{4,0},{8,12},{12,8},{1,5},{5,1},{9,13},{13,9},{2,6},{6,2},{1... | collective-permute-start | bytes 24584 | tf_op jit(solution)/shard_map/total/ppermute | solution.py:36
  27.7 3.8 %collective-permute-start.7 = (f32[32,64]{1,0:T(8,128)S(1)}, f32[32,64]{1,0:T(8,128)S(1)}, u32[]{:S(2)}, u32[]{:S(2)}) collective-permute-start(f32[32,64]{1,0:T(8,128)S(1)} %add_add_fusion.1), channel_id=1, source_target_pairs={{0,2},{1,3},{2,0},{3,1},{4,6},{5,7},{6,4},{7,5},{8,10},{9,11},{10,... | collective-permute-start | bytes 24584 | tf_op jit(solution)/shard_map/total/ppermute | solution.py:36
  29.2 3.2 %collective-permute-start.8 = (f32[32,64]{1,0:T(8,128)S(1)}, f32[32,64]{1,0:T(8,128)S(1)}, u32[]{:S(2)}, u32[]{:S(2)}) collective-permute-start(f32[32,64]{1,0:T(8,128)S(1)} %add_add_fusion.1), channel_id=1, source_target_pairs={{0,3},{1,2},{2,1},{3,0},{4,7},{5,6},{6,5},{7,4},{8,11},{9,10},{10,... | collective-permute-start | bytes 24584 | tf_op jit(solution)/shard_map/total/ppermute | solution.py:36
  29.2 3.2 %collective-permute-start.6 = (f32[32,64]{1,0:T(8,128)S(1)}, f32[32,64]{1,0:T(8,128)S(1)}, u32[]{:S(2)}, u32[]{:S(2)}) collective-permute-start(f32[32,64]{1,0:T(8,128)S(1)} %add_add_fusion.1), channel_id=1, source_target_pairs={{0,1},{1,0},{2,3},{3,2},{4,5},{5,4},{6,7},{7,6},{8,9},{9,8},{10,11... | collective-permute-start | bytes 24584 | tf_op jit(solution)/shard_map/total/ppermute | solution.py:36

commit v3 on v2

v3 whole, which is shorter than its diff:
```python
import functools

import jax
import jax.numpy as jnp
from jax import lax
from jax.experimental import pallas as pl
from jax.experimental.pallas import tpu as pltpu
from jax.sharding import PartitionSpec as P

prepay_base = -4.0
incentive = 40.0
default_base = -6.0
price_sens = 12.0
oas_spread = 0.005
LANES = 128
FIELDS = 7
EARLY = 2
HIGHEST = lax.Precision.HIGHEST
VMEM_LIMIT = 40 * 1024 * 1024
PACK_LIMIT = 56 * 1024 * 1024


def up(value, unit):
    return -(-value // unit) * unit


def peer(index, shift, count):
    if count & (count - 1) == 0:
        return jnp.bitwise_xor(index, shift)
    return lax.rem(index + shift, count)


def trade(x, axis, shift, count):
    if count & (count - 1) == 0:
        pairs = [(i, i ^ shift) for i in range(count)]
    else:
        pairs = [(i, (i + shift) % count) for i in range(count)]
    return lax.ppermute(x, axis, pairs)


def sum_over(x, axis):
    count = lax.axis_size(axis)
    if count & (count - 1):
        return lax.psum(x, axis)
    parts = [x] + [trade(x, axis, s, count) for s in range(1, count)]
    while len(parts) > 1:
        parts = [parts[i] + parts[i + 1] for i in range(0, len(parts), 2)]
    return parts[0]


class Plan:
    def __init__(self, count, sides, loans, regions, steps, paths, deals, tranches):
        self.count, self.loans, self.regions, self.steps = count, loans, regions, steps
        self.paths, self.deals, self.tranches = paths, deals, tranches
        self.mine = paths // count
        self.pad = up(self.mine, 16)
        most = LANES // self.mine
        early = min(EARLY, steps, most)
        late = steps - early
        per = min(late, most) if late else 0
        self.early = tuple(range(early))
        self.late = tuple(range(early, steps))
        self.blocks = [self.late[i : i + per] for i in range(0, late, per)] if late else []
        self.early_rows = self.packed_rows(early)
        self.block_rows = [self.packed_rows(len(months)) for months in self.blocks]
        self.halves = 2 if sides % 2 == 0 else 1
        self.loan_rows = loans // LANES
        self.half_rows = self.loan_rows // self.halves
        self.first_rows = up(self.early_rows + FIELDS * self.half_rows, 8)
        self.late_rows = up(sum(self.block_rows), 8)
        self.depth = up(count * regions, LANES)
        self.groups = max(1, LANES // deals)
        self.rows = self.mine // self.groups
        self.width = self.groups * deals
        self.all_rows = count * self.loan_rows
        self.chunk = 16
        self.sum_width = up(3 * deals, LANES)
        self.order = tuple(range(count))[::-1]
        fold = LANES // tranches if LANES % tranches == 0 else 1
        self.out_fold = fold if deals % (8 * fold) == 0 else 1

    def folds(self, months):
        used = months * self.mine
        if 2 * used == LANES and self.regions % 2 == 0:
            return "halves"
        if used + self.mine == LANES and self.regions % (months + 1) == 0:
            return "spare"
        return "plain"

    def packed_rows(self, months):
        kind = self.folds(months)
        if kind == "halves":
            return self.regions // 2
        if kind == "spare":
            return self.regions // (months + 1) * months
        return self.regions


def fetch(sources, targets, sems):
    copies = [pltpu.make_async_copy(a, b, sems.at[i]) for i, (a, b) in enumerate(zip(sources, targets))]
    for copy in copies:
        copy.start()
    return copies


def lane_block(plan, months, start):
    lane = lax.broadcasted_iota(jnp.int32, (plan.regions, LANES), 1)
    block = jnp.zeros((plan.regions, LANES), jnp.float32)
    for i, month in enumerate(months):
        spot = i * plan.mine
        moved = pltpu.roll(month, lax.rem(spot + LANES - start, LANES), 1)
        block = jnp.where((lane >= spot) & (lane < spot + plan.mine), moved, block)
    count, kind = len(months), plan.folds(len(months))
    if kind == "halves":
        rows = plan.regions // 2
        return block[0:rows] + pltpu.roll(block[rows:], LANES // 2, 1)
    if kind == "spare":
        rows = plan.regions // (count + 1)
        last = block[count * rows :]
        moved = [pltpu.roll(last, (count - i) * plan.mine, 1) for i in range(count)]
        lane = lax.broadcasted_iota(jnp.int32, (count * rows, LANES), 1)
        return jnp.where(lane < count * plan.mine, block[0 : count * rows], jnp.concatenate(moved, axis=0))
    return block


def unfold(plan, count, packed):
    kind = plan.folds(count)
    if kind == "halves":
        return jnp.concatenate([packed, pltpu.roll(packed, LANES // 2, 1)], axis=0)
    if kind == "spare":
        rows = plan.regions // (count + 1)
        lane = lax.broadcasted_iota(jnp.int32, (rows, LANES), 1)
        last = jnp.zeros((rows, LANES), jnp.float32)
        for i in range(count):
            moved = pltpu.roll(packed[i * rows : (i + 1) * rows], (i + 1) * plan.mine, 1)
            last = jnp.where((lane >= i * plan.mine) & (lane < (i + 1) * plan.mine), moved, last)
        return jnp.concatenate([packed, last], axis=0)
    return packed


def first_kernel(plan, *refs):
    me = lax.axis_index("loans")
    sent = plan.count * (2 if plan.late else 1)
    outs, late_outs = refs[9 : 9 + plan.count], refs[9 + plan.count : 9 + sent]
    here = refs[9 + sent : -1]
    sems = refs[-1]
    side = lax.rem(lax.axis_index("paths"), plan.halves)
    lots = plan.half_rows * LANES
    sources = list(refs[:9])
    sources[1] = refs[1].at[pl.ds(side * lots, lots)]
    copies = fetch(sources, here, sems)
    hpi_ref, feat_ref, coef_ref, coupon_ref, balance_ref, term_ref, age_ref, region_ref, deal_ref = here
    copies[0].wait()
    rows, hr = plan.early_rows, plan.half_rows
    for s, out in zip(plan.order, outs):
        out[0:rows, :] = lane_block(plan, [hpi_ref[t] for t in plan.early], peer(me, s, plan.count) * plan.mine)
    for s, out in zip(plan.order, late_outs):
        at = 0
        for months, size in zip(plan.blocks, plan.block_rows):
            out[at : at + size, :] = lane_block(
                plan, [hpi_ref[t] for t in months], peer(me, s, plan.count) * plan.mine
            )
            at += size
        if at < plan.late_rows:
            out[at:, :] = jnp.zeros((plan.late_rows - at, LANES), jnp.float32)
    for copy in copies[1:]:
        copy.wait()
    covar = lax.dot_general(
        coef_ref[...], feat_ref[...], (((1,), (1,)), ((), ())), preferred_element_type=jnp.float32
    )
    rows0 = jnp.concatenate([covar[0:1, LANES * i : LANES * (i + 1)] for i in range(hr)], axis=0)
    rows1 = jnp.concatenate([covar[1:2, LANES * i : LANES * (i + 1)] for i in range(hr)], axis=0)

    def share(x):
        if plan.halves == 1:
            return x
        return pltpu.roll(x, lax.rem(plan.loan_rows - side * hr, plan.loan_rows), 0)[0:hr]

    coupon = share(coupon_ref[...])
    fields = (
        0.5 * (rows0 + prepay_base + incentive * coupon),
        0.5 * (rows1 + default_base),
        coupon,
        share((term_ref[...] - age_ref[...]).astype(jnp.float32)),
        share(balance_ref[...]),
        share(region_ref[...].astype(jnp.float32)),
        share(deal_ref[...].astype(jnp.float32)),
    )
    used = rows + FIELDS * hr
    for out in outs:
        for i, field in enumerate(fields):
            out[rows + i * hr : rows + (i + 1) * hr, :] = field
        if used < plan.first_rows:
            out[used:, :] = jnp.zeros((plan.first_rows - used, LANES), jnp.float32)


def deal_kernel(plan, *refs):
    list_out, ends_out, open_out, rate_out, mort_out, disc_out = refs[5:11]
    square, ranks, opens, orders = refs[11:15]
    owner_ref, order_ref, share_ref, rate_ref, paths_ref = refs[:5]
    deals, tranches, width = plan.deals, plan.tranches, plan.width
    me = lax.axis_index("loans")
    f32 = jnp.float32
    number = lax.broadcasted_iota(jnp.int32, (1, deals), 1)
    key_row = (owner_ref[...] * deals + number).astype(f32)
    row_of = lax.broadcasted_iota(jnp.int32, (deals, deals), 0)
    col_of = lax.broadcasted_iota(jnp.int32, (deals, deals), 1)
    key = jnp.sum(jnp.where(row_of == col_of, key_row, 0.0), axis=1, keepdims=True)
    spot_row = jnp.sum(jnp.where(key < key_row, 1.0, 0.0), axis=0, keepdims=True)
    tall = lax.broadcasted_iota(jnp.int32, (width, deals), 0)
    tall = lax.rem(tall, deals).astype(f32)
    place = jnp.where(tall == spot_row, 1.0, 0.0)
    deal_row = lax.broadcasted_iota(jnp.int32, (width, deals), 1).astype(f32)
    listing = jnp.sum(place * deal_row, axis=1, keepdims=True)
    list_out[...] = jnp.broadcast_to(listing[0:deals], (deals, LANES))

    def listed(table):
        return lax.dot_general(table, place, (((0,), (1,)), ((), ())), precision=HIGHEST, preferred_element_type=f32)

    share = listed(share_ref[...])
    weight = share / jnp.sum(share, axis=0, keepdims=True)
    opens[...] = weight
    open_out[...] = weight
    rate_out[...] = listed(rate_ref[...])
    orders[...] = jnp.floor(listed(order_ref[...].astype(f32)) + 0.5)
    index = lax.broadcasted_iota(jnp.int32, (tranches, width), 0).astype(f32)
    rank = jnp.zeros((tranches, width), f32)
    for j in range(tranches):
        rank = jnp.where(orders[j : j + 1, :] == index, float(j), rank)
    ranks[...] = rank
    ends = jnp.zeros((tranches, width), f32)
    for j in range(tranches):
        ends = ends + jnp.where(ranks[j : j + 1, :] <= rank, opens[j : j + 1, :], 0.0)
    ends_out[...] = ends
    steps = plan.steps
    square[...] = jnp.zeros_like(square)
    for t in range(steps):
        square[2 * t : 2 * t + 2, :] = paths_ref[t]
    turned = jnp.transpose(square[...])
    turned = pltpu.roll(turned, lax.rem(plan.paths - me * plan.mine, plan.paths), 0)
    lane = lax.broadcasted_iota(jnp.int32, (plan.rows, width), 1)
    total = jnp.zeros((plan.mine, 1), f32)
    for t in range(steps):
        mort_out[t * plan.pad : (t + 1) * plan.pad, :] = jnp.broadcast_to(
            (0.5 * incentive) * turned[0 : plan.pad, 2 * t + 1 : 2 * t + 2], (plan.pad, LANES)
        )
        total = total + (turned[0 : plan.mine, 2 * t : 2 * t + 1] + oas_spread)
        disc = jnp.exp(total / -12.0)
        wide = jnp.zeros((plan.rows, width), f32)
        for g in range(plan.groups):
            part = jnp.broadcast_to(disc[g * plan.rows : (g + 1) * plan.rows], (plan.rows, width))
            wide = jnp.where(lane >= g * plan.deals, part, wide)
        disc_out[t] = wide


def fill_table(plan, table, gather, spots, months, spot_row):
    turned = jnp.transpose(gather)
    for i in range(len(months)):
        spots[spot_row + i * plan.pad : spot_row + i * plan.pad + plan.mine, :] = (0.5 * price_sens) * turned[
            i * plan.mine : (i + 1) * plan.mine, :
        ]


def split(table, exact):
    rows = exact.shape[0]
    high = exact.astype(jnp.bfloat16)
    table[0:rows, :] = high
    table[rows:, :] = (exact - high.astype(jnp.float32)).astype(jnp.bfloat16)


def sort_kernel(plan, *refs):
    count, regions, rows, hr = plan.count, plan.regions, plan.early_rows, plan.half_rows
    msgs = {s: refs[i] for i, s in enumerate(plan.order)}
    half_out, table, gather, spots = refs[count:]
    if count * regions < plan.depth:
        gather[count * regions :, :] = jnp.zeros((plan.depth - count * regions, LANES), jnp.float32)
    for s, msg in msgs.items():
        gather[s * regions : (s + 1) * regions, :] = unfold(plan, len(plan.early), msg[0:rows, :])
        for i in range(FIELDS):
            half_out[(i * count + s) * hr : (i * count + s + 1) * hr, :] = msg[rows + i * hr : rows + (i + 1) * hr, :]
    if plan.pad > plan.mine:
        spots[...] = jnp.zeros_like(spots)
    fill_table(plan, table, gather[...], spots, plan.early, 0)
    split(table, spots[...])


def loan_months(plan, months, first, table, coef, listing, mort_ref, state_in, state_out, acc):
    f32, bf16 = jnp.float32, jnp.bfloat16
    pad = plan.pad
    rows = len(months) * pad
    depth_of = lax.broadcasted_iota(jnp.int16, (plan.depth, LANES), 0)
    one, zero = jnp.array(1.0, bf16), jnp.array(0.0, bf16)
    acc[...] = jnp.zeros_like(acc)

    def loans(c, carry):
        marks, weights, lhs = [], [], []
        for j in range(plan.chunk):
            spot = coef[5, pl.ds(c * plan.chunk + j, 1), :].astype(jnp.int32).astype(jnp.int16)
            marks.append(jnp.where(depth_of == spot, one, zero))
        h = lax.dot_general(
            table[...], jnp.concatenate(marks, axis=1), (((1,), (0,)), ((), ())), preferred_element_type=f32
        )
        h = h[0:rows] + h[rows:]
        for j in range(plan.chunk):
            row = c * plan.chunk + j

            def at(i):
                return coef[i, pl.ds(row, 1), :]

            score, default = at(0), at(1)
            if first:
                held = jnp.broadcast_to(at(2), (pad, LANES))
                parts = [jnp.broadcast_to(at(2), (16, LANES))]
            else:
                held = state_in[row]
                parts = []
            for i, t in enumerate(months):
                stay = 1.0 - jnp.tanh(score - mort_ref[t * pad : (t + 1) * pad, :])
                keep = at(7 + t) - jnp.tanh(default - h[i * pad : (i + 1) * pad, j * LANES : (j + 1) * LANES])
                held = held * keep * (0.25 * stay)
                parts.append(held)
            if state_out is not None:
                state_out[row] = held
            held = jnp.concatenate(parts, axis=0)
            high = held.astype(bf16)
            low = (held - high.astype(f32)).astype(bf16)
            lhs.append(jnp.concatenate([high, low], axis=0))
            hit = listing == at(6)
            kinds = [jnp.where(hit, 1.0, 0.0), jnp.where(hit, at(3), 0.0), jnp.where(hit, at(4), 0.0)]
            if plan.sum_width > 3 * plan.deals:
                kinds.append(jnp.zeros((plan.sum_width - 3 * plan.deals, LANES), f32))
            weights.append(jnp.concatenate(kinds, axis=0).astype(bf16))
        acc[...] += lax.dot_general(
            jnp.concatenate(lhs, axis=1),
            jnp.concatenate(weights, axis=1),
            (((1,), (1,)), ((), ())),
            preferred_element_type=f32,
        )
        return carry

    lax.fori_loop(0, plan.all_rows // plan.chunk, loans, 0)


def early_kernel(plan, *refs):
    halves = refs[: plan.halves]
    table, list_ref, mort_ref, coef, state, acc = refs[plan.halves :]
    f32, bf16 = jnp.float32, jnp.bfloat16
    me = lax.axis_index("loans")
    each = plan.count * plan.half_rows
    count, regions = plan.count, plan.regions

    def dense(i):
        return jnp.concatenate([half[i * each : (i + 1) * each, :] for half in halves], axis=0)

    rate = dense(2) / 12.0
    term = dense(3)
    growth = jnp.log1p(rate)
    coef[0] = dense(0)
    coef[1] = dense(1)
    coef[2] = dense(4)
    rate_high = rate.astype(bf16).astype(f32)
    coef[3] = rate_high
    coef[4] = rate - rate_high
    region = dense(5).astype(jnp.int32)
    home = jnp.zeros_like(region)
    for z in range(1, count):
        home = home + jnp.where(region >= z * regions, 1, 0)
    if count & (count - 1) == 0:
        place = jnp.bitwise_xor(home, me)
    else:
        place = lax.rem(me - home + count, count)
    coef[5] = (region + (place - home) * regions).astype(f32)
    coef[6] = dense(6)
    for t in range(plan.steps):
        coef[7 + t] = 1.0 - 2.0 * (rate / (jnp.exp((term - float(t)) * growth) - 1.0))
    loan_months(plan, plan.early, True, table, coef, list_ref[...], mort_ref, None, state, acc)


def value_kernel(plan, all_paths, *refs):
    f32 = jnp.float32
    sent = plan.count if plan.late else 0
    msgs = {s: refs[i] for i, s in enumerate(plan.order[:sent])}
    coef, state, acc_early, list_ref, ends_ref, open_ref, rate_ref, mort_ref, disc_ref, out_ref = refs[sent : sent + 10]
    regions, steps, pad = plan.regions, plan.steps, plan.pad
    if plan.late:
        table, gather, spots, acc = refs[sent + 10 :]
        used = plan.count * regions
        if used < plan.depth:
            gather[used:, :] = jnp.zeros((plan.depth - used, gather.shape[1]), f32)
        if pad > plan.mine:
            spots[...] = jnp.zeros_like(spots)
        at, month = 0, 0
        for months, size in zip(plan.blocks, plan.block_rows):
            for s, msg in msgs.items():
                gather[s * regions : (s + 1) * regions, :] = unfold(plan, len(months), msg[at : at + size, :])
            fill_table(plan, table, gather[...], spots, months, month * pad)
            at, month = at + size, month + len(months)
        split(table, spots[...])
        loan_months(plan, plan.late, False, table, coef, list_ref[...], mort_ref, state, None, acc)

    deals, width, rows = plan.deals, plan.width, plan.rows
    lane = lax.broadcasted_iota(jnp.int32, (rows, width), 1)
    early_rows, late_rows = 16 + len(plan.early) * pad, len(plan.late) * pad

    def sums(t, kind):
        wide = None
        for g in range(plan.groups):
            if t < len(plan.early):
                at = 16 + t * pad + g * rows
                part = acc_early[at : at + rows, :] + acc_early[early_rows + at : early_rows + at + rows, :]
            else:
                at = (t - len(plan.early)) * pad + g * rows
                part = acc[at : at + rows, :] + acc[late_rows + at : late_rows + at + rows, :]
            if plan.groups > 1:
                part = pltpu.roll(part, (g - kind) * deals % width, 1)
                wide = part if g == 0 else jnp.where(lane >= g * deals, part, wide)
            else:
                wide = part[:, kind * deals : (kind + 1) * deals]
        return wide

    def start_sums(kind):
        part = acc_early[0:16, :] + acc_early[early_rows : early_rows + 16, :]
        part = part[0:rows]
        if plan.groups == 1:
            return part[:, kind * deals : (kind + 1) * deals]
        wide = None
        for g in range(plan.groups):
            moved = pltpu.roll(part, (g - kind) * deals % width, 1)
            wide = moved if g == 0 else jnp.where(lane >= g * deals, moved, wide)
        return wide

    start = start_sums(0)
    inverse = 1.0 / start
    pools = [start] + [sums(t, 0) for t in range(steps)]
    incomes = [start_sums(1) + start_sums(2)]
    incomes += [sums(t, 1) + sums(t, 2) for t in range(steps - 1)]
    paid_by = [jnp.zeros((rows, width), f32)]
    for t in range(steps):
        paid_by.append(paid_by[-1] + jnp.maximum(pools[t] - pools[t + 1], 0.0) * inverse)
    incomes = [disc_ref[t] * (incomes[t] * inverse) for t in range(steps)]
    ends, opening, coupon = ends_ref[...], open_ref[...], rate_ref[...]
    worth = jnp.zeros_like(opening)
    income = jnp.zeros_like(opening)
    for r in range(rows):
        held = jnp.clip(ends - paid_by[0][r : r + 1], 0.0, opening)
        for t in range(steps):
            later = jnp.clip(ends - paid_by[t + 1][r : r + 1], 0.0, opening)
            due = jnp.sum(coupon * held, axis=0, keepdims=True)
            income = income + held * (incomes[t][r : r + 1] / due)
            worth = worth + (held - later) * (disc_ref[t, r : r + 1, :] - 1.0)
            held = later
        worth = worth + held * (disc_ref[steps - 1, r : r + 1, :] - 1.0)
    gain = (worth + coupon * income) / opening * (100.0 / all_paths)
    if plan.groups > 1:
        whole = gain
        for g in range(1, plan.groups):
            whole = whole + pltpu.roll(gain, g * deals, 1)
        gain = whole
    listed = jnp.transpose(gain)[0:deals, :]
    part = deals // plan.out_fold
    out_ref[...] = jnp.concatenate([listed[i * part : (i + 1) * part] for i in range(plan.out_fold)], axis=1)


def on_device(
    loan_features,
    hazard_coef,
    coupon,
    balance,
    loan_term,
    loan_age,
    loan_region,
    loan_deal,
    region_hpi,
    rate_paths,
    deal_owner,
    tranche_order,
    tranche_share,
    tranche_rate,
):
    count = lax.axis_size("loans")
    sides = lax.axis_size("paths")
    loans = coupon.shape[0]
    regions, steps, paths = region_hpi.shape
    deals, tranches = tranche_order.shape
    plan = Plan(count, sides, loans, regions, steps, paths, deals, tranches)
    f32, bf16 = jnp.float32, jnp.bfloat16
    params = pltpu.CompilerParams(vmem_limit_bytes=VMEM_LIMIT)
    whole = pltpu.CompilerParams(vmem_limit_bytes=PACK_LIMIT)
    early, late = len(plan.early), len(plan.late)

    def shape(*dims, dtype=f32):
        return jax.ShapeDtypeStruct(dims, dtype)

    def cost(microseconds):
        return pl.CostEstimate(flops=int(microseconds * 1e9), bytes_accessed=100_000, transcendentals=0)

    def rows(x):
        return x.reshape(plan.loan_rows, LANES)

    by_month = region_hpi.transpose(1, 0, 2)
    given = (
        by_month, loan_features, hazard_coef.T, rows(coupon), rows(balance), rows(loan_term), rows(loan_age),
        rows(loan_region), rows(loan_deal),
    )
    here = [x.shape for x in given]
    here[1] = (plan.half_rows * LANES,) + here[1][1:]
    with jax.named_scope("pack_first"):
        msgs = pl.pallas_call(
            functools.partial(first_kernel, plan),
            out_shape=[pltpu.VMEM((plan.first_rows, LANES), f32)] * count
            + [pltpu.VMEM((plan.late_rows, LANES), f32)] * (count if late else 0),
            in_specs=[pl.BlockSpec(memory_space=pltpu.HBM)] * len(given),
            scratch_shapes=[pltpu.VMEM(dims, x.dtype) for dims, x in zip(here, given)]
            + [pltpu.SemaphoreType.DMA((len(given),))],
            compiler_params=params,
            cost_estimate=cost(1),
        )(*[pltpu.with_memory_space_constraint(x, pltpu.HBM) for x in given])
    with jax.named_scope("exchange_first"):
        got = [trade(msg, "loans", s, count) if s else msg for s, msg in zip(plan.order, msgs[:count])]
    if late:
        with jax.named_scope("exchange_late"):
            late_got = [trade(msg, "loans", s, count) if s else msg for s, msg in zip(plan.order, msgs[count:])]
    else:
        late_got = []
    with jax.named_scope("deals"):
        held = (deal_owner.T, tranche_order, tranche_share, tranche_rate, rate_paths.transpose(1, 0, 2))
        listing, ends, opening, rates, mort, disc = pl.pallas_call(
            functools.partial(deal_kernel, plan),
            out_shape=[
                shape(deals, LANES),
                shape(tranches, plan.width),
                shape(tranches, plan.width),
                shape(tranches, plan.width),
                shape(steps * plan.pad, LANES),
                shape(steps, plan.rows, plan.width),
            ],
            scratch_shapes=[
                pltpu.VMEM((paths, LANES), f32),
                pltpu.VMEM((tranches, plan.width), f32),
                pltpu.VMEM((tranches, plan.width), f32),
                pltpu.VMEM((tranches, plan.width), f32),
            ],
            compiler_params=params,
            cost_estimate=cost(1),
        )(*held)
    with jax.named_scope("sort"):
        half, table = pl.pallas_call(
            functools.partial(sort_kernel, plan),
            out_shape=[
                shape(FIELDS * count * plan.half_rows, LANES),
                shape(2 * early * plan.pad, plan.depth, dtype=bf16),
            ],
            scratch_shapes=[pltpu.VMEM((plan.depth, LANES), f32), pltpu.VMEM((early * plan.pad, plan.depth), f32)],
            compiler_params=params,
            cost_estimate=cost(0.5),
        )(*got)
    with jax.named_scope("share"):
        halves = [half]
        if plan.halves == 2:
            halves.append(lax.ppermute(half, "paths", [(i, i ^ 1) for i in range(sides)]))
    with jax.named_scope("early_months"):
        coef, state, acc = pl.pallas_call(
            functools.partial(early_kernel, plan),
            out_shape=[
                shape(7 + steps, plan.all_rows, LANES),
                shape(plan.all_rows, plan.pad, LANES),
                shape(2 * (16 + early * plan.pad), plan.sum_width),
            ],
            compiler_params=params,
            cost_estimate=cost(2),
        )(*halves, table, listing, mort)
    scratch = [
        pltpu.VMEM((2 * late * plan.pad, plan.depth), bf16),
        pltpu.VMEM((plan.depth, LANES), f32),
        pltpu.VMEM((late * plan.pad, plan.depth), f32),
        pltpu.VMEM((2 * late * plan.pad, plan.sum_width), f32),
    ]
    with jax.named_scope("value"):
        part = pl.pallas_call(
            functools.partial(value_kernel, plan, float(paths * sides)),
            out_shape=shape(deals // plan.out_fold, plan.out_fold * tranches),
            scratch_shapes=scratch if late else [],
            compiler_params=params,
            cost_estimate=cost(3),
        )(*late_got, coef, state, acc, listing, ends, opening, rates, mort, disc)
    with jax.named_scope("total"):
        total = sum_over(sum_over(part, "loans"), "paths")
        return jnp.concatenate(
            [total[:, i * tranches : (i + 1) * tranches] for i in range(plan.out_fold)], axis=0
        )


def solution(mesh):
    in_specs = (
        P(("groups", "loans"), None),
        P(),
        P(("groups", "loans")),
        P(("groups", "loans")),
        P(("groups", "loans")),
        P(("groups", "loans")),
        P(("groups", "loans")),
        P(("groups", "loans")),
        P(("groups", "loans"), None, "paths"),
        P(None, None, ("groups", "paths")),
        P("groups", None),
        P("groups", None),
        P("groups", None),
        P("groups", None),
    )
    out_specs = P("groups", None)
    return jax.shard_map(
        on_device, mesh=mesh, in_specs=in_specs, out_specs=out_specs, check_vma=False
    )
```

time: 33.2 us -> 31.6 us (0.952)
  waiting for transfers between devices: 13.1 us -> 5.9 us
  starting transfers between devices: 11.5 us -> 16.6 us
  local copies, waits for them, and re-layouts: 0.11 us -> 0.73 us
    ppermute x9 -> x12, waiting for transfers between devices: 13.1 us -> 5.9 us  [trade(): return lax.ppermute(x, axis, pairs)]
    ppermute x9 -> x12, starting transfers between devices: 11.5 us -> 16.5 us  [trade(): return lax.ppermute(x, axis, pairs)]
    concatenate x0 -> x1, other arithmetic: none -> 0.61 us  [on_device(): jnp.concatenate([total[:, i * tranches:(i + 1) * tranches] for i in range...]
    add x2, other arithmetic: 0.62 us -> 0.01 us  [sum_over(): parts = [parts[i] + parts[i + 1] for i in range(0, len(parts), 2)]]
    unnamed x14 -> x10, local copies, waits for them, and re-layouts: 0.11 us -> 0.66 us
    pallas_call x3 -> x5, Pallas kernels: 7.61 us -> 7.43 us  [the longest x1 3.05 us: on_device(): pl.pallas_call(functools.partial(value_kernel, plan, float(paths * sides)...]
  transfers between devices with their start and end apart: 9 -> 13, of which waited for: 7 -> 5; matrix products, arithmetic and copies ran while one was open for 0% -> 0% of each run, Pallas kernels for 3% -> 8%
where the time goes in v3:
time: 31.6 us; the launch traced here: 31.4 us
  starting transfers between devices  16.6 us (53%)
  Pallas kernels  7.43 us (24%)
  waiting for transfers between devices  5.9 us (19%)
  local copies, waits for them, and re-layouts  0.73 us (2%)
  other arithmetic  0.62 us (2%)
    ppermute x12, starting transfers between devices, trade(): return lax.ppermute(x, axis, pairs)  16.5 us
    ppermute x12, waiting for transfers between devices, trade(): return lax.ppermute(x, axis, pairs)  5.9 us
    pallas_call x1, Pallas kernels, on_device(): pl.pallas_call(functools.partial(value_kernel, plan, float(paths * sides)...  3.05 us
    pallas_call x1, Pallas kernels, on_device(): pl.pallas_call(functools.partial(first_kernel, plan), out_shape=[pltpu.VM...  1.83 us
    pallas_call x1, Pallas kernels, on_device(): pl.pallas_call(functools.partial(early_kernel, plan), out_shape=[shape(7...  1.38 us
    pallas_call x1, Pallas kernels, on_device(): pl.pallas_call(functools.partial(deal_kernel, plan), out_shape=[shape(dea...  0.97 us
    unnamed x10, local copies, waits for them, and re-layouts  0.66 us
  transfers between devices with their start and end apart: 13, of which 5 were waited for; matrix products, arithmetic and copies ran while one was open for 0% of the time, Pallas kernels for 8%

profile of v3, /device:TPU:0, one launch (start us, length us, event | category | flops | bytes accessed | tf_op | source)
XLA Modules:
  0.0 31.4 jit_solution(7606091621959947794)
XLA Ops:
  0.0 1.8 %pack_first.1 = (f32[80,128]{1,0:T(8,128)S(1)}, f32[80,128]{1,0:T(8,128)S(1)}, f32[80,128]{1,0:T(8,128)S(1)}, f32[80,128]{1,0:T(8,128)S(1)}, f32[104,128]{1,0:T(...) custom-call(f32[6,104,128]{2,1,0:T(8,128)} %bitcast.12, ...), custom_call_target="tpu_custom_call" | custom-call | flops 1000000000 | bytes 100000 | tf_op jit(solution)/shard_map/pack_first/pallas_call | solution.py:508
  1.8 5.1 %collective-permute-start.3 = (f32[80,128]{1,0:T(8,128)S(1)}, f32[80,128]{1,0:T(8,128)S(1)}, u32[]{:S(2)}, u32[]{:S(2)}) collective-permute-start(f32[80,128]{1,0:T(8,128)S(1)} %get-tuple-element.28), channel_id=1, source_target_pairs={{0,12},{4,8},{8,4},{12,0},{1,13},{5,9},{9,5},{13,1},{2,14},{6,10},... | collective-permute-start | bytes 122888 | tf_op jit(solution)/shard_map/exchange_first/ppermute | solution.py:38
  7.0 0.0 collective-permute-start.4
  7.0 0.6 %collective-permute-start.5 = (f32[80,128]{1,0:T(8,128)S(1)}, f32[80,128]{1,0:T(8,128)S(1)}, u32[]{:S(2)}, u32[]{:S(2)}) collective-permute-start(f32[80,128]{1,0:T(8,128)S(1)} %get-tuple-element.30), channel_id=1, source_target_pairs={{0,4},{4,0},{8,12},{12,8},{1,5},{5,1},{9,13},{13,9},{2,6},{6,2},{1... | collective-permute-start | bytes 122888 | tf_op jit(solution)/shard_map/exchange_first/ppermute | solution.py:38
  7.6 3.7 %collective-permute-start = (f32[104,128]{1,0:T(8,128)S(1)}, f32[104,128]{1,0:T(8,128)S(1)}, u32[]{:S(2)}, u32[]{:S(2)}) collective-permute-start(f32[104,128]{1,0:T(8,128)S(1)} %get-tuple-element.24), channel_id=1, source_target_pairs={{0,12},{4,8},{8,4},{12,0},{1,13},{5,9},{9,5},{13,1},{2,14},{6,10},... | collective-permute-start | bytes 159752 | tf_op jit(solution)/shard_map/exchange_late/ppermute | solution.py:38
  11.3 0.0 collective-permute-start.1
  11.3 0.0 collective-permute-done.3.refs_0_
  11.3 0.6 %collective-permute-start.2 = (f32[104,128]{1,0:T(8,128)S(1)}, f32[104,128]{1,0:T(8,128)S(1)}, u32[]{:S(2)}, u32[]{:S(2)}) collective-permute-start(f32[104,128]{1,0:T(8,128)S(1)} %get-tuple-element.26), channel_id=1, source_target_pairs={{0,4},{4,0},{8,12},{12,8},{1,5},{5,1},{9,13},{13,9},{2,6},{6,2},{1... | collective-permute-start | bytes 159752 | tf_op jit(solution)/shard_map/exchange_late/ppermute | solution.py:38
  12.0 1.1 %collective-permute-done.4.refs_1_ = f32[80,128]{1,0:T(8,128)S(1)} collective-permute-done((f32[80,128]{1,0:T(8,128)S(1)}, f32[80,128]{1,0:T(8,128)S(1)}, u32[]{:S(2)}, u32[]{:S(2)}) %collective-permute-start.4) | collective-permute-done | bytes 40992 | tf_op jit(solution)/shard_map/exchange_first/ppermute | solution.py:38
  13.1 0.0 collective-permute-done.5.refs_2_
  13.1 0.0 copy-start.3
  13.1 0.2 sort.1
  13.3 0.1 collective-permute-start.6
  13.4 0.0 copy-start.4
  13.4 0.4 %copy-done = s32[32,64]{1,0:T(8,128)S(1)} copy-done((s32[32,64]{1,0:T(8,128)S(1)}, s32[32,64]{1,0:T(8,128)}, u32[]{:S(2)}) %copy-start) | copy-done | bytes 8216
  13.8 0.0 copy-done.1
  13.8 0.0 copy-done.2
  13.8 0.2 copy-done.4
  14.0 1.0 %deals.1 = (f32[32,128]{1,0:T(8,128)S(1)}, f32[64,128]{1,0:T(8,128)S(1)}, f32[64,128]{1,0:T(8,128)S(1)}, f32[64,128]{1,0:T(8,128)S(1)}, f32[192,128]{1,0:T(8,128)S(1)}, /*index=5*/f32[6,8,128]{2,1,0:T(8,128)S(1)}) custom-call(s32[1,32]{1,0:T(1,128)S(1)} %bitcast.11, s32[32,64]{1,0:T(8,128)S(1)} %copy-done, f32[32,64]{1,0:T(8,128)S(1)} %copy-done.1, ...), custom_call_target="tpu_custom_call" | custom-call | flops 1000000000 | bytes 100000 | tf_op jit(solution)/shard_map/deals/pallas_call | solution.py:527
  15.0 1.4 %early_months.1 = (f32[13,32,128]{2,1,0:T(8,128)S(1)}, f32[32,32,128]{2,1,0:T(8,128)S(1)}, f32[160,128]{1,0:T(8,128)S(1)}) custom-call(f32[112,128]{1,0:T(8,128)S(1)} %get-tuple-element.32.refs_0_, f32[112,128]{1,0:T(8,128)S(1)} %collective-permute-done.6.refs_1_, bf16[128,512]{1,0:T(8,128)(2,1)S(1)} %get-tuple-element.33.refs_2_, ...), custom_call_target="tpu_custom_call" | custom-call | flops 2000000000 | bytes 100000 | tf_op jit(solution)/shard_map/early_months/pallas_call | solution.py:562
  16.5 3.0 %value.1 = f32[16,128]{1,0:T(8,128)S(1)} custom-call(f32[104,128]{1,0:T(8,128)S(1)} %collective-permute-done.refs_0_, f32[104,128]{1,0:T(8,128)S(1)} %collective-permute-done.1.refs_1_, f32[104,128]{1,0:T(8,128)S(1)} %collective-permute-done.2.refs_2_, f32[104,128]{1,0:T(8,128)S(1)} %get-tuple-element.27.refs_3_, ...), custom_call_target="tpu_custom_call" | custom-call | flops 3000000000 | bytes 100000 | tf_op jit(solution)/shard_map/value/pallas_call | solution.py:579
  19.5 2.7 %collective-permute-start.9 = (f32[16,128]{1,0:T(8,128)S(1)}, f32[16,128]{1,0:T(8,128)S(1)}, u32[]{:S(2)}, u32[]{:S(2)}) collective-permute-start(f32[16,128]{1,0:T(8,128)S(1)} %value.1), channel_id=1, source_target_pairs={{0,12},{4,8},{8,4},{12,0},{1,13},{5,9},{9,5},{13,1},{2,14},{6,10},... | collective-permute-start | bytes 24584 | tf_op jit(solution)/shard_map/total/ppermute | solution.py:38
  22.3 1.7 %collective-permute-start.7 = (f32[16,128]{1,0:T(8,128)S(1)}, f32[16,128]{1,0:T(8,128)S(1)}, u32[]{:S(2)}, u32[]{:S(2)}) collective-permute-start(f32[16,128]{1,0:T(8,128)S(1)} %value.1), channel_id=1, source_target_pairs={{0,4},{4,0},{8,12},{12,8},{1,5},{5,1},{9,13},{13,9},{2,6},{6,2},{1... | collective-permute-start | bytes 24584 | tf_op jit(solution)/shard_map/total/ppermute | solution.py:38
  24.0 1.1 %collective-permute-done.9 = f32[16,128]{1,0:T(8,128)S(1)} collective-permute-done((f32[16,128]{1,0:T(8,128)S(1)}, f32[16,128]{1,0:T(8,128)S(1)}, u32[]{:S(2)}, u32[]{:S(2)}) %collective-permute-start.9) | collective-permute-done | bytes 8224 | tf_op jit(solution)/shard_map/total/ppermute | solution.py:38
  25.0 1.8 %collective-permute-done.8 = f32[16,128]{1,0:T(8,128)S(1)} collective-permute-done((f32[16,128]{1,0:T(8,128)S(1)}, f32[16,128]{1,0:T(8,128)S(1)}, u32[]{:S(2)}, u32[]{:S(2)}) %collective-permute-start.8) | collective-permute-done | bytes 8224 | tf_op jit(solution)/shard_map/total/ppermute | solution.py:38
  26.8 0.2 collective-permute-start.12
  27.1 1.4 %collective-permute-start.11 = (f32[16,128]{1,0:T(8,128)S(1)}, f32[16,128]{1,0:T(8,128)S(1)}, u32[]{:S(2)}, u32[]{:S(2)}) collective-permute-start(f32[16,128]{1,0:T(8,128)S(1)} %add_add_fusion.1), channel_id=1, source_target_pairs={{0,2},{1,3},{2,0},{3,1},{4,6},{5,7},{6,4},{7,5},{8,10},{9,11},{10,... | collective-permute-start | bytes 24584 | tf_op jit(solution)/shard_map/total/ppermute | solution.py:38
  28.4 0.3 collective-permute-start.10
  28.7 1.3 %collective-permute-done.12 = f32[16,128]{1,0:T(8,128)S(1)} collective-permute-done((f32[16,128]{1,0:T(8,128)S(1)}, f32[16,128]{1,0:T(8,128)S(1)}, u32[]{:S(2)}, u32[]{:S(2)}) %collective-permute-start.12) | collective-permute-done | bytes 8224 | tf_op jit(solution)/shard_map/total/ppermute | solution.py:38
  30.0 0.7 %collective-permute-done.11 = f32[16,128]{1,0:T(8,128)S(1)} collective-permute-done((f32[16,128]{1,0:T(8,128)S(1)}, f32[16,128]{1,0:T(8,128)S(1)}, u32[]{:S(2)}, u32[]{:S(2)}) %collective-permute-start.11) | collective-permute-done | bytes 8224 | tf_op jit(solution)/shard_map/total/ppermute | solution.py:38
  30.7 0.1 fusion
  30.8 0.6 %pad_maximum_fusion = f32[32,64]{1,0:T(8,128)} fusion(f32[16,64]{1,0:T(8,128)S(1)} %get-tuple-element.44, f32[16,64]{1,0:T(8,128)S(1)} %get-tuple-element.43), kind=kLoop, calls=%fused_computation | loop fusion | flops 2048 | bytes 16384 | tf_op jit(solution)/shard_map/total/concatenate | solution.py:588
  (13 shorter events, 0.0 us)
Async XLA Ops:
  1.8 9.5 %collective-permute-start.3 = (f32[80,128]{1,0:T(8,128)S(1)}, f32[80,128]{1,0:T(8,128)S(1)}, u32[]{:S(2)}, u32[]{:S(2)}) collective-permute-start(f32[80,128]{1,0:T(8,128)S(1)} %get-tuple-element.28), channel_id=1, source_target_pairs={{0,12},{4,8},{8,4},{12,0},{1,13},{5,9},{9,5},{13,1},{2,14},{6,10},... | collective-permute-start | bytes 122888 | tf_op jit(solution)/shard_map/exchange_first/ppermute | solution.py:38
  7.0 6.1 %collective-permute-start.4 = (f32[80,128]{1,0:T(8,128)S(1)}, f32[80,128]{1,0:T(8,128)S(1)}, u32[]{:S(2)}, u32[]{:S(2)}) collective-permute-start(f32[80,128]{1,0:T(8,128)S(1)} %get-tuple-element.29), channel_id=1, source_target_pairs={{0,8},{4,12},{8,0},{12,4},{1,9},{5,13},{9,1},{13,5},{2,10},{6,14},... | collective-permute-start | bytes 122888 | tf_op jit(solution)/shard_map/exchange_first/ppermute | solution.py:38
  7.0 6.1 %collective-permute-start.5 = (f32[80,128]{1,0:T(8,128)S(1)}, f32[80,128]{1,0:T(8,128)S(1)}, u32[]{:S(2)}, u32[]{:S(2)}) collective-permute-start(f32[80,128]{1,0:T(8,128)S(1)} %get-tuple-element.30), channel_id=1, source_target_pairs={{0,4},{4,0},{8,12},{12,8},{1,5},{5,1},{9,13},{13,9},{2,6},{6,2},{1... | collective-permute-start | bytes 122888 | tf_op jit(solution)/shard_map/exchange_first/ppermute | solution.py:38
  7.6 8.8 %collective-permute-start = (f32[104,128]{1,0:T(8,128)S(1)}, f32[104,128]{1,0:T(8,128)S(1)}, u32[]{:S(2)}, u32[]{:S(2)}) collective-permute-start(f32[104,128]{1,0:T(8,128)S(1)} %get-tuple-element.24), channel_id=1, source_target_pairs={{0,12},{4,8},{8,4},{12,0},{1,13},{5,9},{9,5},{13,1},{2,14},{6,10},... | collective-permute-start | bytes 159752 | tf_op jit(solution)/shard_map/exchange_late/ppermute | solution.py:38
  11.3 5.1 %collective-permute-start.1 = (f32[104,128]{1,0:T(8,128)S(1)}, f32[104,128]{1,0:T(8,128)S(1)}, u32[]{:S(2)}, u32[]{:S(2)}) collective-permute-start(f32[104,128]{1,0:T(8,128)S(1)} %get-tuple-element.25), channel_id=1, source_target_pairs={{0,8},{4,12},{8,0},{12,4},{1,9},{5,13},{9,1},{13,5},{2,10},{6,14},... | collective-permute-start | bytes 159752 | tf_op jit(solution)/shard_map/exchange_late/ppermute | solution.py:38
  11.3 5.1 %collective-permute-start.2 = (f32[104,128]{1,0:T(8,128)S(1)}, f32[104,128]{1,0:T(8,128)S(1)}, u32[]{:S(2)}, u32[]{:S(2)}) collective-permute-start(f32[104,128]{1,0:T(8,128)S(1)} %get-tuple-element.26), channel_id=1, source_target_pairs={{0,4},{4,0},{8,12},{12,8},{1,5},{5,1},{9,13},{13,9},{2,6},{6,2},{1... | collective-permute-start | bytes 159752 | tf_op jit(solution)/shard_map/exchange_late/ppermute | solution.py:38
  13.1 0.7 %copy-start = (s32[32,64]{1,0:T(8,128)S(1)}, s32[32,64]{1,0:T(8,128)}, u32[]{:S(2)}) copy-start(s32[32,64]{1,0:T(8,128)} %refs_1_.3) | copy-start | bytes 24580
  13.1 0.7 %copy-start.1 = (f32[32,64]{1,0:T(8,128)S(1)}, f32[32,64]{1,0:T(8,128)}, u32[]{:S(2)}) copy-start(f32[32,64]{1,0:T(8,128)} %refs_2_.1) | copy-start | bytes 24580
  13.1 0.7 %copy-start.2 = (f32[32,64]{1,0:T(8,128)S(1)}, f32[32,64]{1,0:T(8,128)}, u32[]{:S(2)}) copy-start(f32[32,64]{1,0:T(8,128)} %refs_3_.1) | copy-start | bytes 24580
  13.1 0.7 %copy-start.3 = (f32[2,6,128]{2,0,1:T(2,128)S(1)}, f32[2,6,128]{2,0,1:T(2,128)}, u32[]{:S(2)}) copy-start(f32[2,6,128]{2,0,1:T(2,128)} %param.23) | copy-start | bytes 18436
  13.3 1.7 %collective-permute-start.6 = (f32[112,128]{1,0:T(8,128)S(1)}, f32[112,128]{1,0:T(8,128)S(1)}, u32[]{:S(2)}, u32[]{:S(2)}) collective-permute-start(f32[112,128]{1,0:T(8,128)S(1)} %get-tuple-element.32.refs_0_), channel_id=1, source_target_pairs={{0,1},{1,0},{2,3},{3,2},{4,5},{5,4},{6,7},{7,6},{8,9},{9,8},{10,11... | collective-permute-start | bytes 172040 | tf_op jit(solution)/shard_map/share/ppermute | solution.py:560
  13.4 0.7 %copy-start.4 = (s32[32,1]{0,1:T(1,128)S(1)}, s32[32,1]{0,1:T(1,128)}, u32[]{:S(2)}) copy-start(s32[32,1]{0,1:T(1,128)} %param.24) | copy-start | bytes 388
  19.5 5.5 %collective-permute-start.9 = (f32[16,128]{1,0:T(8,128)S(1)}, f32[16,128]{1,0:T(8,128)S(1)}, u32[]{:S(2)}, u32[]{:S(2)}) collective-permute-start(f32[16,128]{1,0:T(8,128)S(1)} %value.1), channel_id=1, source_target_pairs={{0,12},{4,8},{8,4},{12,0},{1,13},{5,9},{9,5},{13,1},{2,14},{6,10},... | collective-permute-start | bytes 24584 | tf_op jit(solution)/shard_map/total/ppermute | solution.py:38
  22.3 4.5 %collective-permute-start.8 = (f32[16,128]{1,0:T(8,128)S(1)}, f32[16,128]{1,0:T(8,128)S(1)}, u32[]{:S(2)}, u32[]{:S(2)}) collective-permute-start(f32[16,128]{1,0:T(8,128)S(1)} %value.1), channel_id=1, source_target_pairs={{0,8},{4,12},{8,0},{12,4},{1,9},{5,13},{9,1},{13,5},{2,10},{6,14},... | collective-permute-start | bytes 24584 | tf_op jit(solution)/shard_map/total/ppermute | solution.py:38
  22.3 4.5 %collective-permute-start.7 = (f32[16,128]{1,0:T(8,128)S(1)}, f32[16,128]{1,0:T(8,128)S(1)}, u32[]{:S(2)}, u32[]{:S(2)}) collective-permute-start(f32[16,128]{1,0:T(8,128)S(1)} %value.1), channel_id=1, source_target_pairs={{0,4},{4,0},{8,12},{12,8},{1,5},{5,1},{9,13},{13,9},{2,6},{6,2},{1... | collective-permute-start | bytes 24584 | tf_op jit(solution)/shard_map/total/ppermute | solution.py:38
  26.8 3.2 %collective-permute-start.12 = (f32[16,128]{1,0:T(8,128)S(1)}, f32[16,128]{1,0:T(8,128)S(1)}, u32[]{:S(2)}, u32[]{:S(2)}) collective-permute-start(f32[16,128]{1,0:T(8,128)S(1)} %add_add_fusion.1), channel_id=1, source_target_pairs={{0,3},{1,2},{2,1},{3,0},{4,7},{5,6},{6,5},{7,4},{8,11},{9,10},{10,... | collective-permute-start | bytes 24584 | tf_op jit(solution)/shard_map/total/ppermute | solution.py:38
  27.1 3.7 %collective-permute-start.11 = (f32[16,128]{1,0:T(8,128)S(1)}, f32[16,128]{1,0:T(8,128)S(1)}, u32[]{:S(2)}, u32[]{:S(2)}) collective-permute-start(f32[16,128]{1,0:T(8,128)S(1)} %add_add_fusion.1), channel_id=1, source_target_pairs={{0,2},{1,3},{2,0},{3,1},{4,6},{5,7},{6,4},{7,5},{8,10},{9,11},{10,... | collective-permute-start | bytes 24584 | tf_op jit(solution)/shard_map/total/ppermute | solution.py:38
  28.4 2.3 %collective-permute-start.10 = (f32[16,128]{1,0:T(8,128)S(1)}, f32[16,128]{1,0:T(8,128)S(1)}, u32[]{:S(2)}, u32[]{:S(2)}) collective-permute-start(f32[16,128]{1,0:T(8,128)S(1)} %add_add_fusion.1), channel_id=1, source_target_pairs={{0,1},{1,0},{2,3},{3,2},{4,5},{5,4},{6,7},{7,6},{8,9},{9,8},{10,11... | collective-permute-start | bytes 24584 | tf_op jit(solution)/shard_map/total/ppermute | solution.py:38

commit v4 on v3

--- a/solution.py
+++ b/solution.py
@@ -14,10 +14,9 @@
 oas_spread = 0.005
 LANES = 128
 FIELDS = 7
-EARLY = 2
+PASSED = 5
 HIGHEST = lax.Precision.HIGHEST
 VMEM_LIMIT = 40 * 1024 * 1024
-PACK_LIMIT = 56 * 1024 * 1024
 
 
 def up(value, unit):
@@ -55,24 +54,20 @@
         self.mine = paths // count
         self.pad = up(self.mine, 16)
         most = LANES // self.mine
-        early = min(EARLY, steps, most)
-        late = steps - early
-        per = min(late, most) if late else 0
-        self.early = tuple(range(early))
-        self.late = tuple(range(early, steps))
-        self.blocks = [self.late[i : i + per] for i in range(0, late, per)] if late else []
-        self.early_rows = self.packed_rows(early)
+        first = steps % most or most
+        spots = [0] + list(range(first, steps + 1, most))
+        self.blocks = [tuple(range(a, b)) for a, b in zip(spots, spots[1:])]
         self.block_rows = [self.packed_rows(len(months)) for months in self.blocks]
         self.halves = 2 if sides % 2 == 0 else 1
         self.loan_rows = loans // LANES
         self.half_rows = self.loan_rows // self.halves
-        self.first_rows = up(self.early_rows + FIELDS * self.half_rows, 8)
-        self.late_rows = up(sum(self.block_rows), 8)
+        self.hpi_rows = sum(self.block_rows)
+        self.msg_rows = up(self.hpi_rows + FIELDS * self.half_rows, 8)
         self.depth = up(count * regions, LANES)
         self.groups = max(1, LANES // deals)
         self.rows = self.mine // self.groups
         self.width = self.groups * deals
-        self.all_rows = count * self.loan_rows
+        self.all_rows = count * self.half_rows
         self.chunk = 16
         self.sum_width = up(3 * deals, LANES)
         self.order = tuple(range(count))[::-1]
@@ -138,31 +133,27 @@
     return packed
 
 
-def first_kernel(plan, *refs):
+def pack_kernel(plan, *refs):
     me = lax.axis_index("loans")
-    sent = plan.count * (2 if plan.late else 1)
-    outs, late_outs = refs[9 : 9 + plan.count], refs[9 + plan.count : 9 + sent]
-    here = refs[9 + sent : -1]
-    sems = refs[-1]
+    given, passed = refs[:9], refs[9 : 9 + PASSED]
+    refs = refs[9 + PASSED :]
+    outs, kept, here, sems, pass_sems = refs[: plan.count], refs[plan.count : plan.count + PASSED], refs[plan.count + PASSED : -2], refs[-2], refs[-1]
     side = lax.rem(lax.axis_index("paths"), plan.halves)
     lots = plan.half_rows * LANES
-    sources = list(refs[:9])
-    sources[1] = refs[1].at[pl.ds(side * lots, lots)]
+    sources = list(given)
+    sources[1] = given[1].at[pl.ds(side * lots, lots)]
     copies = fetch(sources, here, sems)
+    passing = fetch(passed, kept, pass_sems)
     hpi_ref, feat_ref, coef_ref, coupon_ref, balance_ref, term_ref, age_ref, region_ref, deal_ref = here
     copies[0].wait()
-    rows, hr = plan.early_rows, plan.half_rows
+    rows, hr = plan.hpi_rows, plan.half_rows
     for s, out in zip(plan.order, outs):
-        out[0:rows, :] = lane_block(plan, [hpi_ref[t] for t in plan.early], peer(me, s, plan.count) * plan.mine)
-    for s, out in zip(plan.order, late_outs):
         at = 0
         for months, size in zip(plan.blocks, plan.block_rows):
             out[at : at + size, :] = lane_block(
                 plan, [hpi_ref[t] for t in months], peer(me, s, plan.count) * plan.mine
             )
             at += size
-        if at < plan.late_rows:
-            out[at:, :] = jnp.zeros((plan.late_rows - at, LANES), jnp.float32)
     for copy in copies[1:]:
         copy.wait()
     covar = lax.dot_general(
@@ -190,29 +181,33 @@
     for out in outs:
         for i, field in enumerate(fields):
             out[rows + i * hr : rows + (i + 1) * hr, :] = field
-        if used < plan.first_rows:
-            out[used:, :] = jnp.zeros((plan.first_rows - used, LANES), jnp.float32)
-
-
-def deal_kernel(plan, *refs):
-    list_out, ends_out, open_out, rate_out, mort_out, disc_out = refs[5:11]
-    square, ranks, opens, orders = refs[11:15]
-    owner_ref, order_ref, share_ref, rate_ref, paths_ref = refs[:5]
-    deals, tranches, width = plan.deals, plan.tranches, plan.width
-    me = lax.axis_index("loans")
-    f32 = jnp.float32
+        if used < plan.msg_rows:
+            out[used:, :] = jnp.zeros((plan.msg_rows - used, LANES), jnp.float32)
+    for copy in passing:
+        copy.wait()
+
+
+def list_deals(plan, owner, tall):
+    deals, f32 = plan.deals, jnp.float32
     number = lax.broadcasted_iota(jnp.int32, (1, deals), 1)
-    key_row = (owner_ref[...] * deals + number).astype(f32)
+    key_row = (owner * deals + number).astype(f32)
     row_of = lax.broadcasted_iota(jnp.int32, (deals, deals), 0)
     col_of = lax.broadcasted_iota(jnp.int32, (deals, deals), 1)
     key = jnp.sum(jnp.where(row_of == col_of, key_row, 0.0), axis=1, keepdims=True)
     spot_row = jnp.sum(jnp.where(key < key_row, 1.0, 0.0), axis=0, keepdims=True)
-    tall = lax.broadcasted_iota(jnp.int32, (width, deals), 0)
-    tall = lax.rem(tall, deals).astype(f32)
-    place = jnp.where(tall == spot_row, 1.0, 0.0)
-    deal_row = lax.broadcasted_iota(jnp.int32, (width, deals), 1).astype(f32)
-    listing = jnp.sum(place * deal_row, axis=1, keepdims=True)
-    list_out[...] = jnp.broadcast_to(listing[0:deals], (deals, LANES))
+    spot = lax.rem(lax.broadcasted_iota(jnp.int32, (tall, deals), 0), deals).astype(f32)
+    place = jnp.where(spot == spot_row, 1.0, 0.0)
+    deal_row = lax.broadcasted_iota(jnp.int32, (tall, deals), 1).astype(f32)
+    return place, jnp.sum(place * deal_row, axis=1, keepdims=True)
+
+
+def deal_kernel(plan, owner_ref, order_ref, share_ref, rate_ref, paths_ref, list_out, ends_out, open_out, rate_out,
+                mort_out, disc_out, square, ranks, opens, orders):
+    me = lax.axis_index("loans")
+    tranches, width, steps = plan.tranches, plan.width, plan.steps
+    f32 = jnp.float32
+    place, listing = list_deals(plan, owner_ref[...], width)
+    list_out[...] = jnp.broadcast_to(listing[0 : plan.deals], (plan.deals, LANES))
 
     def listed(table):
         return lax.dot_general(table, place, (((0,), (1,)), ((), ())), precision=HIGHEST, preferred_element_type=f32)
@@ -232,12 +227,10 @@
     for j in range(tranches):
         ends = ends + jnp.where(ranks[j : j + 1, :] <= rank, opens[j : j + 1, :], 0.0)
     ends_out[...] = ends
-    steps = plan.steps
     square[...] = jnp.zeros_like(square)
     for t in range(steps):
         square[2 * t : 2 * t + 2, :] = paths_ref[t]
-    turned = jnp.transpose(square[...])
-    turned = pltpu.roll(turned, lax.rem(plan.paths - me * plan.mine, plan.paths), 0)
+    turned = pltpu.roll(jnp.transpose(square[...]), lax.rem(plan.paths - me * plan.mine, plan.paths), 0)
     lane = lax.broadcasted_iota(jnp.int32, (plan.rows, width), 1)
     total = jnp.zeros((plan.mine, 1), f32)
     for t in range(steps):
@@ -253,44 +246,45 @@
         disc_out[t] = wide
 
 
-def fill_table(plan, table, gather, spots, months, spot_row):
-    turned = jnp.transpose(gather)
-    for i in range(len(months)):
-        spots[spot_row + i * plan.pad : spot_row + i * plan.pad + plan.mine, :] = (0.5 * price_sens) * turned[
+def fill_table(plan, spots, gathered, months):
+    turned = jnp.transpose(gathered)
+    for i, t in enumerate(months):
+        spots[t * plan.pad : t * plan.pad + plan.mine, :] = (0.5 * price_sens) * turned[
             i * plan.mine : (i + 1) * plan.mine, :
         ]
 
 
-def split(table, exact):
-    rows = exact.shape[0]
-    high = exact.astype(jnp.bfloat16)
-    table[0:rows, :] = high
-    table[rows:, :] = (exact - high.astype(jnp.float32)).astype(jnp.bfloat16)
-
-
 def sort_kernel(plan, *refs):
-    count, regions, rows, hr = plan.count, plan.regions, plan.early_rows, plan.half_rows
+    count, regions, rows, hr = plan.count, plan.regions, plan.hpi_rows, plan.half_rows
     msgs = {s: refs[i] for i, s in enumerate(plan.order)}
     half_out, table, gather, spots = refs[count:]
-    if count * regions < plan.depth:
-        gather[count * regions :, :] = jnp.zeros((plan.depth - count * regions, LANES), jnp.float32)
     for s, msg in msgs.items():
-        gather[s * regions : (s + 1) * regions, :] = unfold(plan, len(plan.early), msg[0:rows, :])
         for i in range(FIELDS):
             half_out[(i * count + s) * hr : (i * count + s + 1) * hr, :] = msg[rows + i * hr : rows + (i + 1) * hr, :]
+    if count * regions < plan.depth:
+        gather[count * regions :, :] = jnp.zeros((plan.depth - count * regions, gather.shape[1]), jnp.float32)
     if plan.pad > plan.mine:
         spots[...] = jnp.zeros_like(spots)
-    fill_table(plan, table, gather[...], spots, plan.early, 0)
-    split(table, spots[...])
-
-
-def loan_months(plan, months, first, table, coef, listing, mort_ref, state_in, state_out, acc):
+    at = 0
+    for b, (months, size) in enumerate(zip(plan.blocks, plan.block_rows)):
+        lanes = slice(b * LANES, (b + 1) * LANES)
+        for s, msg in msgs.items():
+            gather[s * regions : (s + 1) * regions, lanes] = unfold(plan, len(months), msg[at : at + size, :])
+        fill_table(plan, spots, gather[:, lanes], months)
+        at += size
+    exact = spots[...]
+    high = exact.astype(jnp.bfloat16)
+    table[0 : exact.shape[0], :] = high
+    table[exact.shape[0] :, :] = (exact - high.astype(jnp.float32)).astype(jnp.bfloat16)
+
+
+def loan_months(plan, table, coef, listing, mort_ref, acc):
     f32, bf16 = jnp.float32, jnp.bfloat16
     pad = plan.pad
-    rows = len(months) * pad
+    rows = plan.steps * pad
+    acc[...] = jnp.zeros_like(acc)
     depth_of = lax.broadcasted_iota(jnp.int16, (plan.depth, LANES), 0)
     one, zero = jnp.array(1.0, bf16), jnp.array(0.0, bf16)
-    acc[...] = jnp.zeros_like(acc)
 
     def loans(c, carry):
         marks, weights, lhs = [], [], []
@@ -308,19 +302,13 @@
                 return coef[i, pl.ds(row, 1), :]
 
             score, default = at(0), at(1)
-            if first:
-                held = jnp.broadcast_to(at(2), (pad, LANES))
-                parts = [jnp.broadcast_to(at(2), (16, LANES))]
-            else:
-                held = state_in[row]
-                parts = []
-            for i, t in enumerate(months):
+            held = jnp.broadcast_to(at(2), (pad, LANES))
+            parts = [jnp.broadcast_to(at(2), (16, LANES))]
+            for t in range(plan.steps):
                 stay = 1.0 - jnp.tanh(score - mort_ref[t * pad : (t + 1) * pad, :])
-                keep = at(7 + t) - jnp.tanh(default - h[i * pad : (i + 1) * pad, j * LANES : (j + 1) * LANES])
+                keep = at(7 + t) - jnp.tanh(default - h[t * pad : (t + 1) * pad, j * LANES : (j + 1) * LANES])
                 held = held * keep * (0.25 * stay)
                 parts.append(held)
-            if state_out is not None:
-                state_out[row] = held
             held = jnp.concatenate(parts, axis=0)
             high = held.astype(bf16)
             low = (held - high.astype(f32)).astype(bf16)
@@ -338,19 +326,17 @@
         )
         return carry
 
-    lax.fori_loop(0, plan.all_rows // plan.chunk, loans, 0)
-
-
-def early_kernel(plan, *refs):
-    halves = refs[: plan.halves]
-    table, list_ref, mort_ref, coef, state, acc = refs[plan.halves :]
+    lax.fori_loop(0, plan.count * plan.half_rows // plan.chunk, loans, 0)
+
+
+def loan_values(plan, half, coef):
     f32, bf16 = jnp.float32, jnp.bfloat16
     me = lax.axis_index("loans")
     each = plan.count * plan.half_rows
     count, regions = plan.count, plan.regions
 
     def dense(i):
-        return jnp.concatenate([half[i * each : (i + 1) * each, :] for half in halves], axis=0)
+        return half[i * each : (i + 1) * each, :]
 
     rate = dense(2) / 12.0
     term = dense(3)
@@ -373,44 +359,32 @@
     coef[6] = dense(6)
     for t in range(plan.steps):
         coef[7 + t] = 1.0 - 2.0 * (rate / (jnp.exp((term - float(t)) * growth) - 1.0))
-    loan_months(plan, plan.early, True, table, coef, list_ref[...], mort_ref, None, state, acc)
+
+
+def half_kernel(plan, half, table, list_ref, mort_ref, acc, coef):
+    loan_values(plan, half, coef)
+    loan_months(plan, table, coef, list_ref[...], mort_ref, acc)
 
 
 def value_kernel(plan, all_paths, *refs):
     f32 = jnp.float32
-    sent = plan.count if plan.late else 0
-    msgs = {s: refs[i] for i, s in enumerate(plan.order[:sent])}
-    coef, state, acc_early, list_ref, ends_ref, open_ref, rate_ref, mort_ref, disc_ref, out_ref = refs[sent : sent + 10]
-    regions, steps, pad = plan.regions, plan.steps, plan.pad
-    if plan.late:
-        table, gather, spots, acc = refs[sent + 10 :]
-        used = plan.count * regions
-        if used < plan.depth:
-            gather[used:, :] = jnp.zeros((plan.depth - used, gather.shape[1]), f32)
-        if pad > plan.mine:
-            spots[...] = jnp.zeros_like(spots)
-        at, month = 0, 0
-        for months, size in zip(plan.blocks, plan.block_rows):
-            for s, msg in msgs.items():
-                gather[s * regions : (s + 1) * regions, :] = unfold(plan, len(months), msg[at : at + size, :])
-            fill_table(plan, table, gather[...], spots, months, month * pad)
-            at, month = at + size, month + len(months)
-        split(table, spots[...])
-        loan_months(plan, plan.late, False, table, coef, list_ref[...], mort_ref, state, None, acc)
-
+    other = refs[: plan.halves - 1]
+    half, table, list_ref, ends_ref, open_ref, rate_ref, mort_ref, disc_ref, out_ref, acc, coef = refs[plan.halves - 1 :]
+    loan_values(plan, half, coef)
+    loan_months(plan, table, coef, list_ref[...], mort_ref, acc)
+    sum_rows = 16 + plan.steps * plan.pad
+    pool = acc[0:sum_rows, :] + acc[sum_rows:, :]
+    for part in other:
+        pool = pool + (part[0:sum_rows, :] + part[sum_rows:, :])
+    pad, steps = plan.pad, plan.steps
     deals, width, rows = plan.deals, plan.width, plan.rows
     lane = lax.broadcasted_iota(jnp.int32, (rows, width), 1)
-    early_rows, late_rows = 16 + len(plan.early) * pad, len(plan.late) * pad
 
     def sums(t, kind):
         wide = None
         for g in range(plan.groups):
-            if t < len(plan.early):
-                at = 16 + t * pad + g * rows
-                part = acc_early[at : at + rows, :] + acc_early[early_rows + at : early_rows + at + rows, :]
-            else:
-                at = (t - len(plan.early)) * pad + g * rows
-                part = acc[at : at + rows, :] + acc[late_rows + at : late_rows + at + rows, :]
+            at = 16 + t * pad + g * rows
+            part = pool[at : at + rows]
             if plan.groups > 1:
                 part = pltpu.roll(part, (g - kind) * deals % width, 1)
                 wide = part if g == 0 else jnp.where(lane >= g * deals, part, wide)
@@ -419,8 +393,7 @@
         return wide
 
     def start_sums(kind):
-        part = acc_early[0:16, :] + acc_early[early_rows : early_rows + 16, :]
-        part = part[0:rows]
+        part = pool[0:rows]
         if plan.groups == 1:
             return part[:, kind * deals : (kind + 1) * deals]
         wide = None
@@ -485,8 +458,6 @@
     plan = Plan(count, sides, loans, regions, steps, paths, deals, tranches)
     f32, bf16 = jnp.float32, jnp.bfloat16
     params = pltpu.CompilerParams(vmem_limit_bytes=VMEM_LIMIT)
-    whole = pltpu.CompilerParams(vmem_limit_bytes=PACK_LIMIT)
-    early, late = len(plan.early), len(plan.late)
 
     def shape(*dims, dtype=f32):
         return jax.ShapeDtypeStruct(dims, dtype)
@@ -502,55 +473,51 @@
         by_month, loan_features, hazard_coef.T, rows(coupon), rows(balance), rows(loan_term), rows(loan_age),
         rows(loan_region), rows(loan_deal),
     )
+    passed = (deal_owner.T, tranche_order, tranche_share, tranche_rate, rate_paths.transpose(1, 0, 2))
     here = [x.shape for x in given]
     here[1] = (plan.half_rows * LANES,) + here[1][1:]
-    with jax.named_scope("pack_first"):
+    with jax.named_scope("pack"):
         msgs = pl.pallas_call(
-            functools.partial(first_kernel, plan),
-            out_shape=[pltpu.VMEM((plan.first_rows, LANES), f32)] * count
-            + [pltpu.VMEM((plan.late_rows, LANES), f32)] * (count if late else 0),
-            in_specs=[pl.BlockSpec(memory_space=pltpu.HBM)] * len(given),
+            functools.partial(pack_kernel, plan),
+            out_shape=[pltpu.VMEM((plan.msg_rows, LANES), f32)] * count
+            + [pltpu.VMEM(x.shape, x.dtype) for x in passed],
+            in_specs=[pl.BlockSpec(memory_space=pltpu.HBM)] * (len(given) + PASSED),
             scratch_shapes=[pltpu.VMEM(dims, x.dtype) for dims, x in zip(here, given)]
-            + [pltpu.SemaphoreType.DMA((len(given),))],
+            + [pltpu.SemaphoreType.DMA((len(given),)), pltpu.SemaphoreType.DMA((PASSED,))],
             compiler_params=params,
             cost_estimate=cost(1),
-        )(*[pltpu.with_memory_space_constraint(x, pltpu.HBM) for x in given])
-    with jax.named_scope("exchange_first"):
-        got = [trade(msg, "loans", s, count) if s else msg for s, msg in zip(plan.order, msgs[:count])]
-    if late:
-        with jax.named_scope("exchange_late"):
-            late_got = [trade(msg, "loans", s, count) if s else msg for s, msg in zip(plan.order, msgs[count:])]
-    else:
-        late_got = []
+        )(*[pltpu.with_memory_space_constraint(x, pltpu.HBM) for x in given + passed])
+    msgs, kept = msgs[:count], msgs[count:]
+    with jax.named_scope("exchange"):
+        got = [trade(msg, "loans", s, count) if s else msg for s, msg in zip(plan.order, msgs)]
     with jax.named_scope("deals"):
-        held = (deal_owner.T, tranche_order, tranche_share, tranche_rate, rate_paths.transpose(1, 0, 2))
+        table_shape = (tranches, plan.width)
         listing, ends, opening, rates, mort, disc = pl.pallas_call(
             functools.partial(deal_kernel, plan),
             out_shape=[
                 shape(deals, LANES),
-                shape(tranches, plan.width),
-                shape(tranches, plan.width),
-                shape(tranches, plan.width),
+                shape(*table_shape),
+                shape(*table_shape),
+                shape(*table_shape),
                 shape(steps * plan.pad, LANES),
                 shape(steps, plan.rows, plan.width),
             ],
-            scratch_shapes=[
-                pltpu.VMEM((paths, LANES), f32),
-                pltpu.VMEM((tranches, plan.width), f32),
-                pltpu.VMEM((tranches, plan.width), f32),
-                pltpu.VMEM((tranches, plan.width), f32),
-            ],
+            scratch_shapes=[pltpu.VMEM((paths, LANES), f32)] + [pltpu.VMEM(table_shape, f32)] * 3,
             compiler_params=params,
             cost_estimate=cost(1),
-        )(*held)
+        )(*kept)
+        got[-1], listing = lax.optimization_barrier((got[-1], listing))
     with jax.named_scope("sort"):
         half, table = pl.pallas_call(
             functools.partial(sort_kernel, plan),
             out_shape=[
-                shape(FIELDS * count * plan.half_rows, LANES),
-                shape(2 * early * plan.pad, plan.depth, dtype=bf16),
+                shape(FIELDS * plan.all_rows, LANES),
+                shape(2 * steps * plan.pad, plan.depth, dtype=bf16),
             ],
-            scratch_shapes=[pltpu.VMEM((plan.depth, LANES), f32), pltpu.VMEM((early * plan.pad, plan.depth), f32)],
+            scratch_shapes=[
+                pltpu.VMEM((plan.depth, len(plan.blocks) * LANES), f32),
+                pltpu.VMEM((steps * plan.pad, plan.depth), f32),
+            ],
             compiler_params=params,
             cost_estimate=cost(0.5),
         )(*got)
@@ -558,31 +525,28 @@
         halves = [half]
         if plan.halves == 2:
             halves.append(lax.ppermute(half, "paths", [(i, i ^ 1) for i in range(sides)]))
-    with jax.named_scope("early_months"):
-        coef, state, acc = pl.pallas_call(
-            functools.partial(early_kernel, plan),
-            out_shape=[
-                shape(7 + steps, plan.all_rows, LANES),
-                shape(plan.all_rows, plan.pad, LANES),
-                shape(2 * (16 + early * plan.pad), plan.sum_width),
-            ],
-            compiler_params=params,
-            cost_estimate=cost(2),
-        )(*halves, table, listing, mort)
-    scratch = [
-        pltpu.VMEM((2 * late * plan.pad, plan.depth), bf16),
-        pltpu.VMEM((plan.depth, LANES), f32),
-        pltpu.VMEM((late * plan.pad, plan.depth), f32),
-        pltpu.VMEM((2 * late * plan.pad, plan.sum_width), f32),
-    ]
+    sums = (2 * (16 + steps * plan.pad), plan.sum_width)
+    coef = pltpu.VMEM((7 + steps, plan.all_rows, LANES), f32)
+    other = []
+    for side in halves[:-1]:
+        with jax.named_scope("half"):
+            other.append(
+                pl.pallas_call(
+                    functools.partial(half_kernel, plan),
+                    out_shape=shape(*sums),
+                    scratch_shapes=[coef],
+                    compiler_params=params,
+                    cost_estimate=cost(2),
+                )(side, table, listing, mort)
+            )
     with jax.named_scope("value"):
         part = pl.pallas_call(
             functools.partial(value_kernel, plan, float(paths * sides)),
             out_shape=shape(deals // plan.out_fold, plan.out_fold * tranches),
-            scratch_shapes=scratch if late else [],
+            scratch_shapes=[pltpu.VMEM(sums, f32), coef],
             compiler_params=params,
             cost_estimate=cost(3),
-        )(*late_got, coef, state, acc, listing, ends, opening, rates, mort, disc)
+        )(*other, halves[-1], table, listing, ends, opening, rates, mort, disc)
     with jax.named_scope("total"):
         total = sum_over(sum_over(part, "loans"), "paths")
         return jnp.concatenate(

time: 31.6 us -> 31.1 us (0.984)
  waiting for transfers between devices: 5.9 us -> 11 us
  starting transfers between devices: 16.6 us -> 12.2 us
  local copies, waits for them, and re-layouts: 0.73 us -> 0.07 us
  Pallas kernels: 7.43 us -> 7.07 us
    ppermute x12 -> x9, waiting for transfers between devices: 5.9 us -> 11 us  [trade(): return lax.ppermute(x, axis, pairs)]
    ppermute x12 -> x9, starting transfers between devices: 16.5 us -> 12.1 us  [trade(): return lax.ppermute(x, axis, pairs)]
    pallas_call x1, Pallas kernels: 3.05 us -> 2.35 us  [on_device(): pl.pallas_call(functools.partial(value_kernel, plan, float(paths * sides)...]
    unnamed x10 -> x0, local copies, waits for them, and re-layouts: 0.66 us -> none
  transfers between devices with their start and end apart: 13 -> 10, of which waited for: 5 -> 6; matrix products, arithmetic and copies ran while one was open for 0% -> 0% of each run, Pallas kernels for 8% -> 8%
where the time goes in v4:
time: 31.1 us; the launch traced here: 31 us
  starting transfers between devices  12.2 us (39%)
  waiting for transfers between devices  11 us (35%)
  Pallas kernels  7.07 us (23%)
  other arithmetic  0.62 us (2%)
    ppermute x9, starting transfers between devices, trade(): return lax.ppermute(x, axis, pairs)  12.1 us
    ppermute x9, waiting for transfers between devices, trade(): return lax.ppermute(x, axis, pairs)  11 us
    pallas_call x1, Pallas kernels, on_device(): pl.pallas_call(functools.partial(value_kernel, plan, float(paths * sides)...  2.35 us
    pallas_call x1, Pallas kernels, on_device(): pl.pallas_call(functools.partial(pack_kernel, plan), out_shape=[pltpu.VME...  1.91 us
    pallas_call x1, Pallas kernels, on_device(): pl.pallas_call(functools.partial(half_kernel, plan), out_shape=shape(*sum...  1.55 us
    pallas_call x1, Pallas kernels, on_device(): pl.pallas_call(functools.partial(deal_kernel, plan), out_shape=[shape(dea...  0.97 us
  transfers between devices with their start and end apart: 10, of which 6 were waited for; matrix products, arithmetic and copies ran while one was open for 0% of the time, Pallas kernels for 8%

profile of v4, /device:TPU:0, one launch (start us, length us, event | category | flops | bytes accessed | tf_op | source)
XLA Modules:
  0.0 31.0 jit_solution(13448051051007316714)
XLA Ops:
  0.0 1.9 %pack.1 = (f32[184,128]{1,0:T(8,128)S(1)}, f32[184,128]{1,0:T(8,128)S(1)}, f32[184,128]{1,0:T(8,128)S(1)}, f32[184,128]{1,0:T(8,128)S(1)}, s32[1,32]{1,0:T(1,128...) custom-call(f32[6,104,128]{2,1,0:T(8,128)} %bitcast.10, ...), custom_call_target="tpu_custom_call" | custom-call | flops 1000000000 | bytes 100000 | tf_op jit(solution)/shard_map/pack/pallas_call | solution.py:480
  1.9 5.1 %collective-permute-start = (f32[184,128]{1,0:T(8,128)S(1)}, f32[184,128]{1,0:T(8,128)S(1)}, u32[]{:S(2)}, u32[]{:S(2)}) collective-permute-start(f32[184,128]{1,0:T(8,128)S(1)} %get-tuple-element.24), channel_id=1, source_target_pairs={{0,12},{4,8},{8,4},{12,0},{1,13},{5,9},{9,5},{13,1},{2,14},{6,10},... | collective-permute-start | bytes 282632 | tf_op jit(solution)/shard_map/exchange/ppermute | solution.py:37
  7.0 0.0 collective-permute-start.1
  7.0 0.6 %collective-permute-start.2 = (f32[184,128]{1,0:T(8,128)S(1)}, f32[184,128]{1,0:T(8,128)S(1)}, u32[]{:S(2)}, u32[]{:S(2)}) collective-permute-start(f32[184,128]{1,0:T(8,128)S(1)} %get-tuple-element.26), channel_id=1, source_target_pairs={{0,4},{4,0},{8,12},{12,8},{1,5},{5,1},{9,13},{13,9},{2,6},{6,2},{1... | collective-permute-start | bytes 282632 | tf_op jit(solution)/shard_map/exchange/ppermute | solution.py:37
  7.7 1.0 %deals.1 = (f32[32,128]{1,0:T(8,128)S(1)}, f32[64,128]{1,0:T(8,128)S(1)}, f32[64,128]{1,0:T(8,128)S(1)}, f32[64,128]{1,0:T(8,128)S(1)}, f32[192,128]{1,0:T(8,128)S(1)}, /*index=5*/f32[6,8,128]{2,1,0:T(8,128)S(1)}) custom-call(s32[1,32]{1,0:T(1,128)S(1)} %get-tuple-element.28.owner_ref, s32[32,64]{1,0:T(8,128)S(1)} %get-tuple-element.29.order_ref, ...), custom_call_target="tpu_custom_call" | custom-call | flops 1000000000 | bytes 100000 | tf_op jit(solution)/shard_map/deals/pallas_call | solution.py:495
  8.7 1.9 %collective-permute-done.refs_0_ = f32[184,128]{1,0:T(8,128)S(1)} collective-permute-done((f32[184,128]{1,0:T(8,128)S(1)}, f32[184,128]{1,0:T(8,128)S(1)}, u32[]{:S(2)}, u32[]{:S(2)}) %collective-permute-start) | collective-permute-done | bytes 94240 | tf_op jit(solution)/shard_map/exchange/ppermute | solution.py:37
  10.6 4.4 %collective-permute-done.1.refs_1_ = f32[184,128]{1,0:T(8,128)S(1)} collective-permute-done((f32[184,128]{1,0:T(8,128)S(1)}, f32[184,128]{1,0:T(8,128)S(1)}, u32[]{:S(2)}, u32[]{:S(2)}) %collective-permute-start.1) | collective-permute-done | bytes 94240 | tf_op jit(solution)/shard_map/exchange/ppermute | solution.py:37
  15.0 0.0 collective-permute-done.2.refs_2_
  15.0 0.3 sort.1
  15.2 0.1 collective-permute-start.3
  15.3 1.5 %half.1.refs_0_ = f32[416,128]{1,0:T(8,128)S(1)} custom-call(f32[112,128]{1,0:T(8,128)S(1)} %get-tuple-element.35.half, bf16[384,512]{1,0:T(8,128)(2,1)S(1)} %get-tuple-element.36.table.refs_2_, f32[32,128]{1,0:T(8,128)S(1)} %get-tuple-element.37.list_ref.refs_3_, f32[192,128]{1,0:T(8,128)S(1)} %get-tuple-element.38.mort_ref.refs_7_), custom_call_target="tpu_custom_call" | custom-call | flops 2000000000 | bytes 100000 | tf_op jit(solution)/shard_map/half/pallas_call | solution.py:534
  16.9 0.0 collective-permute-done.3.refs_1_
  16.9 2.3 %value.1 = f32[16,128]{1,0:T(8,128)S(1)} custom-call(f32[416,128]{1,0:T(8,128)S(1)} %half.1.refs_0_, f32[112,128]{1,0:T(8,128)S(1)} %collective-permute-done.3.refs_1_, bf16[384,512]{1,0:T(8,128)(2,1)S(1)} %get-tuple-element.36.table.refs_2_, f32[32,128]{1,0:T(8,128)S(1)} %get-tuple-element.37.list_ref.refs_3_, f32[64,128]{1,0:T(8,128)S(1)} %get-tuple-element.39.refs_4_, ...), custom_call_target="tpu_custom_call" | custom-call | flops 3000000000 | bytes 100000 | tf_op jit(solution)/shard_map/value/pallas_call | solution.py:543
  19.2 2.6 %collective-permute-start.6 = (f32[16,128]{1,0:T(8,128)S(1)}, f32[16,128]{1,0:T(8,128)S(1)}, u32[]{:S(2)}, u32[]{:S(2)}) collective-permute-start(f32[16,128]{1,0:T(8,128)S(1)} %value.1), channel_id=1, source_target_pairs={{0,12},{4,8},{8,4},{12,0},{1,13},{5,9},{9,5},{13,1},{2,14},{6,10},... | collective-permute-start | bytes 24584 | tf_op jit(solution)/shard_map/total/ppermute | solution.py:37
  21.9 0.0 collective-permute-start.5
  21.9 1.8 %collective-permute-start.4 = (f32[16,128]{1,0:T(8,128)S(1)}, f32[16,128]{1,0:T(8,128)S(1)}, u32[]{:S(2)}, u32[]{:S(2)}) collective-permute-start(f32[16,128]{1,0:T(8,128)S(1)} %value.1), channel_id=1, source_target_pairs={{0,4},{4,0},{8,12},{12,8},{1,5},{5,1},{9,13},{13,9},{2,6},{6,2},{1... | collective-permute-start | bytes 24584 | tf_op jit(solution)/shard_map/total/ppermute | solution.py:37
  23.7 1.1 %collective-permute-done.6 = f32[16,128]{1,0:T(8,128)S(1)} collective-permute-done((f32[16,128]{1,0:T(8,128)S(1)}, f32[16,128]{1,0:T(8,128)S(1)}, u32[]{:S(2)}, u32[]{:S(2)}) %collective-permute-start.6) | collective-permute-done | bytes 8224 | tf_op jit(solution)/shard_map/total/ppermute | solution.py:37
  24.8 1.6 %collective-permute-done.5 = f32[16,128]{1,0:T(8,128)S(1)} collective-permute-done((f32[16,128]{1,0:T(8,128)S(1)}, f32[16,128]{1,0:T(8,128)S(1)}, u32[]{:S(2)}, u32[]{:S(2)}) %collective-permute-start.5) | collective-permute-done | bytes 8224 | tf_op jit(solution)/shard_map/total/ppermute | solution.py:37
  26.4 0.0 collective-permute-done.4
  26.4 0.2 collective-permute-start.9
  26.7 1.4 %collective-permute-start.8 = (f32[16,128]{1,0:T(8,128)S(1)}, f32[16,128]{1,0:T(8,128)S(1)}, u32[]{:S(2)}, u32[]{:S(2)}) collective-permute-start(f32[16,128]{1,0:T(8,128)S(1)} %add_add_fusion.1), channel_id=1, source_target_pairs={{0,2},{1,3},{2,0},{3,1},{4,6},{5,7},{6,4},{7,5},{8,10},{9,11},{10,... | collective-permute-start | bytes 24584 | tf_op jit(solution)/shard_map/total/ppermute | solution.py:37
  28.1 0.3 collective-permute-start.7
  28.4 1.3 %collective-permute-done.9 = f32[16,128]{1,0:T(8,128)S(1)} collective-permute-done((f32[16,128]{1,0:T(8,128)S(1)}, f32[16,128]{1,0:T(8,128)S(1)}, u32[]{:S(2)}, u32[]{:S(2)}) %collective-permute-start.9) | collective-permute-done | bytes 8224 | tf_op jit(solution)/shard_map/total/ppermute | solution.py:37
  29.6 0.7 %collective-permute-done.8 = f32[16,128]{1,0:T(8,128)S(1)} collective-permute-done((f32[16,128]{1,0:T(8,128)S(1)}, f32[16,128]{1,0:T(8,128)S(1)}, u32[]{:S(2)}, u32[]{:S(2)}) %collective-permute-start.8) | collective-permute-done | bytes 8224 | tf_op jit(solution)/shard_map/total/ppermute | solution.py:37
  30.3 0.0 collective-permute-done.7
  30.3 0.1 fusion
  30.4 0.6 %pad_maximum_fusion = f32[32,64]{1,0:T(8,128)} fusion(f32[16,64]{1,0:T(8,128)S(1)} %get-tuple-element.44, f32[16,64]{1,0:T(8,128)S(1)} %get-tuple-element.43), kind=kLoop, calls=%fused_computation | loop fusion | flops 2048 | bytes 16384 | tf_op jit(solution)/shard_map/total/concatenate | solution.py:552
  (2 shorter events, 0.0 us)
Async XLA Ops:
  1.9 8.6 %collective-permute-start = (f32[184,128]{1,0:T(8,128)S(1)}, f32[184,128]{1,0:T(8,128)S(1)}, u32[]{:S(2)}, u32[]{:S(2)}) collective-permute-start(f32[184,128]{1,0:T(8,128)S(1)} %get-tuple-element.24), channel_id=1, source_target_pairs={{0,12},{4,8},{8,4},{12,0},{1,13},{5,9},{9,5},{13,1},{2,14},{6,10},... | collective-permute-start | bytes 282632 | tf_op jit(solution)/shard_map/exchange/ppermute | solution.py:37
  7.0 7.9 %collective-permute-start.1 = (f32[184,128]{1,0:T(8,128)S(1)}, f32[184,128]{1,0:T(8,128)S(1)}, u32[]{:S(2)}, u32[]{:S(2)}) collective-permute-start(f32[184,128]{1,0:T(8,128)S(1)} %get-tuple-element.25), channel_id=1, source_target_pairs={{0,8},{4,12},{8,0},{12,4},{1,9},{5,13},{9,1},{13,5},{2,10},{6,14},... | collective-permute-start | bytes 282632 | tf_op jit(solution)/shard_map/exchange/ppermute | solution.py:37
  7.0 7.9 %collective-permute-start.2 = (f32[184,128]{1,0:T(8,128)S(1)}, f32[184,128]{1,0:T(8,128)S(1)}, u32[]{:S(2)}, u32[]{:S(2)}) collective-permute-start(f32[184,128]{1,0:T(8,128)S(1)} %get-tuple-element.26), channel_id=1, source_target_pairs={{0,4},{4,0},{8,12},{12,8},{1,5},{5,1},{9,13},{13,9},{2,6},{6,2},{1... | collective-permute-start | bytes 282632 | tf_op jit(solution)/shard_map/exchange/ppermute | solution.py:37
  15.2 1.6 %collective-permute-start.3 = (f32[112,128]{1,0:T(8,128)S(1)}, f32[112,128]{1,0:T(8,128)S(1)}, u32[]{:S(2)}, u32[]{:S(2)}) collective-permute-start(f32[112,128]{1,0:T(8,128)S(1)} %get-tuple-element.35.half), channel_id=1, source_target_pairs={{0,1},{1,0},{2,3},{3,2},{4,5},{5,4},{6,7},{7,6},{8,9},{9,8},{10,11... | collective-permute-start | bytes 172040 | tf_op jit(solution)/shard_map/share/ppermute | solution.py:527
  19.2 5.5 %collective-permute-start.6 = (f32[16,128]{1,0:T(8,128)S(1)}, f32[16,128]{1,0:T(8,128)S(1)}, u32[]{:S(2)}, u32[]{:S(2)}) collective-permute-start(f32[16,128]{1,0:T(8,128)S(1)} %value.1), channel_id=1, source_target_pairs={{0,12},{4,8},{8,4},{12,0},{1,13},{5,9},{9,5},{13,1},{2,14},{6,10},... | collective-permute-start | bytes 24584 | tf_op jit(solution)/shard_map/total/ppermute | solution.py:37
  21.9 4.5 %collective-permute-start.5 = (f32[16,128]{1,0:T(8,128)S(1)}, f32[16,128]{1,0:T(8,128)S(1)}, u32[]{:S(2)}, u32[]{:S(2)}) collective-permute-start(f32[16,128]{1,0:T(8,128)S(1)} %value.1), channel_id=1, source_target_pairs={{0,8},{4,12},{8,0},{12,4},{1,9},{5,13},{9,1},{13,5},{2,10},{6,14},... | collective-permute-start | bytes 24584 | tf_op jit(solution)/shard_map/total/ppermute | solution.py:37
  21.9 4.5 %collective-permute-start.4 = (f32[16,128]{1,0:T(8,128)S(1)}, f32[16,128]{1,0:T(8,128)S(1)}, u32[]{:S(2)}, u32[]{:S(2)}) collective-permute-start(f32[16,128]{1,0:T(8,128)S(1)} %value.1), channel_id=1, source_target_pairs={{0,4},{4,0},{8,12},{12,8},{1,5},{5,1},{9,13},{13,9},{2,6},{6,2},{1... | collective-permute-start | bytes 24584 | tf_op jit(solution)/shard_map/total/ppermute | solution.py:37
  26.4 3.2 %collective-permute-start.9 = (f32[16,128]{1,0:T(8,128)S(1)}, f32[16,128]{1,0:T(8,128)S(1)}, u32[]{:S(2)}, u32[]{:S(2)}) collective-permute-start(f32[16,128]{1,0:T(8,128)S(1)} %add_add_fusion.1), channel_id=1, source_target_pairs={{0,3},{1,2},{2,1},{3,0},{4,7},{5,6},{6,5},{7,4},{8,11},{9,10},{10,... | collective-permute-start | bytes 24584 | tf_op jit(solution)/shard_map/total/ppermute | solution.py:37
  26.7 3.7 %collective-permute-start.8 = (f32[16,128]{1,0:T(8,128)S(1)}, f32[16,128]{1,0:T(8,128)S(1)}, u32[]{:S(2)}, u32[]{:S(2)}) collective-permute-start(f32[16,128]{1,0:T(8,128)S(1)} %add_add_fusion.1), channel_id=1, source_target_pairs={{0,2},{1,3},{2,0},{3,1},{4,6},{5,7},{6,4},{7,5},{8,10},{9,11},{10,... | collective-permute-start | bytes 24584 | tf_op jit(solution)/shard_map/total/ppermute | solution.py:37
  28.1 2.2 %collective-permute-start.7 = (f32[16,128]{1,0:T(8,128)S(1)}, f32[16,128]{1,0:T(8,128)S(1)}, u32[]{:S(2)}, u32[]{:S(2)}) collective-permute-start(f32[16,128]{1,0:T(8,128)S(1)} %add_add_fusion.1), channel_id=1, source_target_pairs={{0,1},{1,0},{2,3},{3,2},{4,5},{5,4},{6,7},{7,6},{8,9},{9,8},{10,11... | collective-permute-start | bytes 24584 | tf_op jit(solution)/shard_map/total/ppermute | solution.py:37

commit v5 on v4

--- a/solution.py
+++ b/solution.py
@@ -78,16 +78,12 @@
         used = months * self.mine
         if 2 * used == LANES and self.regions % 2 == 0:
             return "halves"
-        if used + self.mine == LANES and self.regions % (months + 1) == 0:
-            return "spare"
         return "plain"
 
     def packed_rows(self, months):
         kind = self.folds(months)
         if kind == "halves":
             return self.regions // 2
-        if kind == "spare":
-            return self.regions // (months + 1) * months
         return self.regions
 
 
@@ -98,23 +94,20 @@
     return copies
 
 
-def lane_block(plan, months, start):
-    lane = lax.broadcasted_iota(jnp.int32, (plan.regions, LANES), 1)
+def turned_months(plan, months):
+    return [pltpu.roll(month, i * plan.mine, 1) if i else month for i, month in enumerate(months)]
+
+
+def lane_block(plan, moved, target):
+    places = LANES // plan.mine
+    lane = lax.broadcasted_iota(jnp.int32, (1, LANES), 1)
     block = jnp.zeros((plan.regions, LANES), jnp.float32)
-    for i, month in enumerate(months):
-        spot = i * plan.mine
-        moved = pltpu.roll(month, lax.rem(spot + LANES - start, LANES), 1)
-        block = jnp.where((lane >= spot) & (lane < spot + plan.mine), moved, block)
-    count, kind = len(months), plan.folds(len(months))
-    if kind == "halves":
+    for i, month in enumerate(moved):
+        start = lax.rem(target + i, places) * plan.mine
+        block = jnp.where((lane >= start) & (lane < start + plan.mine), month, block)
+    if plan.folds(len(moved)) == "halves":
         rows = plan.regions // 2
         return block[0:rows] + pltpu.roll(block[rows:], LANES // 2, 1)
-    if kind == "spare":
-        rows = plan.regions // (count + 1)
-        last = block[count * rows :]
-        moved = [pltpu.roll(last, (count - i) * plan.mine, 1) for i in range(count)]
-        lane = lax.broadcasted_iota(jnp.int32, (count * rows, LANES), 1)
-        return jnp.where(lane < count * plan.mine, block[0 : count * rows], jnp.concatenate(moved, axis=0))
     return block
 
 
@@ -122,38 +115,39 @@
     kind = plan.folds(count)
     if kind == "halves":
         return jnp.concatenate([packed, pltpu.roll(packed, LANES // 2, 1)], axis=0)
-    if kind == "spare":
-        rows = plan.regions // (count + 1)
-        lane = lax.broadcasted_iota(jnp.int32, (rows, LANES), 1)
-        last = jnp.zeros((rows, LANES), jnp.float32)
-        for i in range(count):
-            moved = pltpu.roll(packed[i * rows : (i + 1) * rows], (i + 1) * plan.mine, 1)
-            last = jnp.where((lane >= i * plan.mine) & (lane < (i + 1) * plan.mine), moved, last)
-        return jnp.concatenate([packed, last], axis=0)
     return packed
 
 
-def pack_kernel(plan, *refs):
+def write_homes(plan, hpi_ref, targets):
     me = lax.axis_index("loans")
-    given, passed = refs[:9], refs[9 : 9 + PASSED]
-    refs = refs[9 + PASSED :]
-    outs, kept, here, sems, pass_sems = refs[: plan.count], refs[plan.count : plan.count + PASSED], refs[plan.count + PASSED : -2], refs[-2], refs[-1]
+    at = 0
+    for months, size in zip(plan.blocks, plan.block_rows):
+        moved = turned_months(plan, [hpi_ref[t] for t in months])
+        for out, s in targets:
+            out[at : at + size, :] = lane_block(plan, moved, peer(me, s, plan.count))
+        at += size
+
+
+def write_loans(plan, out, fields):
+    size = FIELDS * plan.half_rows
+    out[plan.hpi_rows : plan.hpi_rows + size, :] = fields
+    used = plan.hpi_rows + size
+    if used < plan.msg_rows:
+        out[used:, :] = jnp.zeros((plan.msg_rows - used, LANES), jnp.float32)
+
+
+def far_kernel(plan, *refs):
+    given, passed, refs = refs[:9], refs[9 : 9 + PASSED], refs[9 + PASSED :]
+    out, fields_out, hpi_ref, refs = refs[0], refs[1], refs[2], refs[3:]
+    kept, here, sems, pass_sems = refs[:PASSED], refs[PASSED:-2], refs[-2], refs[-1]
     side = lax.rem(lax.axis_index("paths"), plan.halves)
     lots = plan.half_rows * LANES
     sources = list(given)
     sources[1] = given[1].at[pl.ds(side * lots, lots)]
-    copies = fetch(sources, here, sems)
+    copies = fetch(sources, (hpi_ref, *here), sems)
     passing = fetch(passed, kept, pass_sems)
-    hpi_ref, feat_ref, coef_ref, coupon_ref, balance_ref, term_ref, age_ref, region_ref, deal_ref = here
-    copies[0].wait()
-    rows, hr = plan.hpi_rows, plan.half_rows
-    for s, out in zip(plan.order, outs):
-        at = 0
-        for months, size in zip(plan.blocks, plan.block_rows):
-            out[at : at + size, :] = lane_block(
-                plan, [hpi_ref[t] for t in months], peer(me, s, plan.count) * plan.mine
-            )
-            at += size
+    feat_ref, coef_ref, coupon_ref, balance_ref, term_ref, age_ref, region_ref, deal_ref = here
+    hr = plan.half_rows
     for copy in copies[1:]:
         copy.wait()
     covar = lax.dot_general(
@@ -177,14 +171,19 @@
         share(region_ref[...].astype(jnp.float32)),
         share(deal_ref[...].astype(jnp.float32)),
     )
-    used = rows + FIELDS * hr
-    for out in outs:
-        for i, field in enumerate(fields):
-            out[rows + i * hr : rows + (i + 1) * hr, :] = field
-        if used < plan.msg_rows:
-            out[used:, :] = jnp.zeros((plan.msg_rows - used, LANES), jnp.float32)
+    for i, field in enumerate(fields):
+        fields_out[i * hr : (i + 1) * hr, :] = field
+    copies[0].wait()
+    write_homes(plan, hpi_ref, [(out, plan.order[0])])
+    write_loans(plan, out, fields_out[...])
     for copy in passing:
         copy.wait()
+
+
+def near_kernel(plan, hpi_ref, fields_ref, *outs):
+    write_homes(plan, hpi_ref, list(zip(outs, plan.order[1:])))
+    for out in outs:
+        write_loans(plan, out, fields_ref[...])
 
 
 def list_deals(plan, owner, tall):
@@ -246,18 +245,27 @@
         disc_out[t] = wide
 
 
-def fill_table(plan, spots, gathered, months):
+def fill_table(plan, spots, turn, gathered, months):
+    me = lax.axis_index("loans")
+    mine, places = plan.mine, LANES // plan.mine
     turned = jnp.transpose(gathered)
+    whole = mine % 8 == 0
+    if whole:
+        turn[...] = turned
+    else:
+        turned = pltpu.roll(turned, lax.rem(LANES - me * mine, LANES), 0)
     for i, t in enumerate(months):
-        spots[t * plan.pad : t * plan.pad + plan.mine, :] = (0.5 * price_sens) * turned[
-            i * plan.mine : (i + 1) * plan.mine, :
-        ]
+        if whole:
+            part = turn[pl.ds(pl.multiple_of(lax.rem(me + i, places) * mine, 8), mine), :]
+        else:
+            part = turned[i * mine : (i + 1) * mine, :]
+        spots[t * plan.pad : t * plan.pad + mine, :] = (0.5 * price_sens) * part
 
 
 def sort_kernel(plan, *refs):
     count, regions, rows, hr = plan.count, plan.regions, plan.hpi_rows, plan.half_rows
     msgs = {s: refs[i] for i, s in enumerate(plan.order)}
-    half_out, table, gather, spots = refs[count:]
+    half_out, table, gather, spots, turn = refs[count:]
     for s, msg in msgs.items():
         for i in range(FIELDS):
             half_out[(i * count + s) * hr : (i * count + s + 1) * hr, :] = msg[rows + i * hr : rows + (i + 1) * hr, :]
@@ -270,7 +278,7 @@
         lanes = slice(b * LANES, (b + 1) * LANES)
         for s, msg in msgs.items():
             gather[s * regions : (s + 1) * regions, lanes] = unfold(plan, len(months), msg[at : at + size, :])
-        fill_table(plan, spots, gather[:, lanes], months)
+        fill_table(plan, spots, turn, gather[:, lanes], months)
         at += size
     exact = spots[...]
     high = exact.astype(jnp.bfloat16)
@@ -476,20 +484,32 @@
     passed = (deal_owner.T, tranche_order, tranche_share, tranche_rate, rate_paths.transpose(1, 0, 2))
     here = [x.shape for x in given]
     here[1] = (plan.half_rows * LANES,) + here[1][1:]
-    with jax.named_scope("pack"):
-        msgs = pl.pallas_call(
-            functools.partial(pack_kernel, plan),
-            out_shape=[pltpu.VMEM((plan.msg_rows, LANES), f32)] * count
+    with jax.named_scope("pack_far"):
+        msg, fields, homes, *kept = pl.pallas_call(
+            functools.partial(far_kernel, plan),
+            out_shape=[
+                pltpu.VMEM((plan.msg_rows, LANES), f32),
+                pltpu.VMEM((FIELDS * plan.half_rows, LANES), f32),
+                pltpu.VMEM(given[0].shape, f32),
+            ]
             + [pltpu.VMEM(x.shape, x.dtype) for x in passed],
             in_specs=[pl.BlockSpec(memory_space=pltpu.HBM)] * (len(given) + PASSED),
-            scratch_shapes=[pltpu.VMEM(dims, x.dtype) for dims, x in zip(here, given)]
+            scratch_shapes=[pltpu.VMEM(dims, x.dtype) for dims, x in zip(here[1:], given[1:])]
             + [pltpu.SemaphoreType.DMA((len(given),)), pltpu.SemaphoreType.DMA((PASSED,))],
             compiler_params=params,
             cost_estimate=cost(1),
         )(*[pltpu.with_memory_space_constraint(x, pltpu.HBM) for x in given + passed])
-    msgs, kept = msgs[:count], msgs[count:]
-    with jax.named_scope("exchange"):
-        got = [trade(msg, "loans", s, count) if s else msg for s, msg in zip(plan.order, msgs)]
+    with jax.named_scope("exchange_far"):
+        got = [trade(msg, "loans", plan.order[0], count)]
+    with jax.named_scope("pack_near"):
+        msgs = pl.pallas_call(
+            functools.partial(near_kernel, plan),
+            out_shape=[pltpu.VMEM((plan.msg_rows, LANES), f32)] * (count - 1),
+            compiler_params=params,
+            cost_estimate=cost(1),
+        )(homes, fields)
+    with jax.named_scope("exchange_near"):
+        got += [trade(msg, "loans", s, count) if s else msg for s, msg in zip(plan.order[1:], msgs)]
     with jax.named_scope("deals"):
         table_shape = (tranches, plan.width)
         listing, ends, opening, rates, mort, disc = pl.pallas_call(
@@ -517,6 +537,7 @@
             scratch_shapes=[
                 pltpu.VMEM((plan.depth, len(plan.blocks) * LANES), f32),
                 pltpu.VMEM((steps * plan.pad, plan.depth), f32),
+                pltpu.VMEM((LANES, plan.depth), f32),
             ],
             compiler_params=params,
             cost_estimate=cost(0.5),

time: 31.1 us -> 30.8 us (level)
    pallas_call x1 -> x2, Pallas kernels: 1.91 us -> 1.64 us  [the longest x1 1.47 us: on_device(): pl.pallas_call(functools.partial(far_kernel, plan), out_shape=[pltpu.VMEM...]
  transfers between devices with their start and end apart: 10 -> 10, of which waited for: 6 -> 6; matrix products, arithmetic and copies ran while one was open for 0% -> 0% of each run, Pallas kernels for 8% -> 9%
where the time goes in v5:
time: 30.8 us; the launch traced here: 30.6 us
  starting transfers between devices  12.2 us (40%)
  waiting for transfers between devices  10.8 us (35%)
  Pallas kernels  6.83 us (22%)
  other arithmetic  0.62 us (2%)
    ppermute x9, starting transfers between devices, trade(): return lax.ppermute(x, axis, pairs)  12.1 us
    ppermute x9, waiting for transfers between devices, trade(): return lax.ppermute(x, axis, pairs)  10.8 us
    pallas_call x1, Pallas kernels, on_device(): pl.pallas_call(functools.partial(value_kernel, plan, float(paths * sides)...  2.35 us
    pallas_call x1, Pallas kernels, on_device(): pl.pallas_call(functools.partial(half_kernel, plan), out_shape=shape(*sum...  1.55 us
    pallas_call x1, Pallas kernels, on_device(): pl.pallas_call(functools.partial(far_kernel, plan), out_shape=[pltpu.VMEM...  1.47 us
    pallas_call x1, Pallas kernels, on_device(): pl.pallas_call(functools.partial(deal_kernel, plan), out_shape=[shape(dea...  0.97 us
  transfers between devices with their start and end apart: 10, of which 6 were waited for; matrix products, arithmetic and copies ran while one was open for 0% of the time, Pallas kernels for 9%

profile of v5, /device:TPU:0, one launch (start us, length us, event | category | flops | bytes accessed | tf_op | source)
XLA Modules:
  0.0 30.6 jit_solution(4666740963084519290)
XLA Ops:
  0.0 1.5 %pack_far.1 = (f32[184,128]{1,0:T(8,128)S(1)}, f32[28,128]{1,0:T(8,128)S(1)}, f32[6,104,128]{2,1,0:T(8,128)S(1)}, s32[1,32]{1,0:T(1,128)S(1)}, s32[32,64]{1,0:T(...) custom-call(f32[6,104,128]{2,1,0:T(8,128)} %bitcast.10, ...), custom_call_target="tpu_custom_call" | custom-call | flops 1000000000 | bytes 100000 | tf_op jit(solution)/shard_map/pack_far/pallas_call | solution.py:488
  1.5 5.1 %collective-permute-start = (f32[184,128]{1,0:T(8,128)S(1)}, f32[184,128]{1,0:T(8,128)S(1)}, u32[]{:S(2)}, u32[]{:S(2)}) collective-permute-start(f32[184,128]{1,0:T(8,128)S(1)} %get-tuple-element.26), channel_id=1, source_target_pairs={{0,12},{4,8},{8,4},{12,0},{1,13},{5,9},{9,5},{13,1},{2,14},{6,10},... | collective-permute-start | bytes 282632 | tf_op jit(solution)/shard_map/exchange_far/ppermute | solution.py:37
  6.6 0.2 pack_near.1
  6.8 0.1 collective-permute-start.1
  6.9 0.6 %collective-permute-start.2 = (f32[184,128]{1,0:T(8,128)S(1)}, f32[184,128]{1,0:T(8,128)S(1)}, u32[]{:S(2)}, u32[]{:S(2)}) collective-permute-start(f32[184,128]{1,0:T(8,128)S(1)} %get-tuple-element.30), channel_id=1, source_target_pairs={{0,4},{4,0},{8,12},{12,8},{1,5},{5,1},{9,13},{13,9},{2,6},{6,2},{1... | collective-permute-start | bytes 282632 | tf_op jit(solution)/shard_map/exchange_near/ppermute | solution.py:37
  7.4 1.0 %deals.1 = (f32[32,128]{1,0:T(8,128)S(1)}, f32[64,128]{1,0:T(8,128)S(1)}, f32[64,128]{1,0:T(8,128)S(1)}, f32[64,128]{1,0:T(8,128)S(1)}, f32[192,128]{1,0:T(8,128)S(1)}, /*index=5*/f32[6,8,128]{2,1,0:T(8,128)S(1)}) custom-call(s32[1,32]{1,0:T(1,128)S(1)} %get-tuple-element.32.owner_ref, s32[32,64]{1,0:T(8,128)S(1)} %get-tuple-element.33.order_ref, ...), custom_call_target="tpu_custom_call" | custom-call | flops 1000000000 | bytes 100000 | tf_op jit(solution)/shard_map/deals/pallas_call | solution.py:515
  8.4 1.5 %collective-permute-done.refs_0_ = f32[184,128]{1,0:T(8,128)S(1)} collective-permute-done((f32[184,128]{1,0:T(8,128)S(1)}, f32[184,128]{1,0:T(8,128)S(1)}, u32[]{:S(2)}, u32[]{:S(2)}) %collective-permute-start) | collective-permute-done | bytes 94240 | tf_op jit(solution)/shard_map/exchange_far/ppermute | solution.py:37
  9.9 4.6 %collective-permute-done.1.refs_1_ = f32[184,128]{1,0:T(8,128)S(1)} collective-permute-done((f32[184,128]{1,0:T(8,128)S(1)}, f32[184,128]{1,0:T(8,128)S(1)}, u32[]{:S(2)}, u32[]{:S(2)}) %collective-permute-start.1) | collective-permute-done | bytes 94240 | tf_op jit(solution)/shard_map/exchange_near/ppermute | solution.py:37
  14.5 0.0 collective-permute-done.2.refs_2_
  14.5 0.3 %sort.1 = (f32[112,128]{1,0:T(8,128)S(1)}, bf16[384,512]{1,0:T(8,128)(2,1)S(1)}) custom-call(f32[184,128]{1,0:T(8,128)S(1)} %collective-permute-done.refs_0_, f32[184,128]{1,0:T(8,128)S(1)} %collective-permute-done.1.refs_1_, f32[184,128]{1,0:T(8,128)S(1)} %collective-permute-done.2.refs_2_, f32[184,128]{1,0:T(8,128)S(1)} %get-tuple-element.38.refs_3_), custom_call_target="tpu_custom_call" | custom-call | flops 500000000 | bytes 100000 | tf_op jit(solution)/shard_map/sort/pallas_call | solution.py:531
  14.8 0.1 collective-permute-start.3
  14.9 1.5 %half.1.refs_0_ = f32[416,128]{1,0:T(8,128)S(1)} custom-call(f32[112,128]{1,0:T(8,128)S(1)} %get-tuple-element.39.half, bf16[384,512]{1,0:T(8,128)(2,1)S(1)} %get-tuple-element.40.table.refs_2_, f32[32,128]{1,0:T(8,128)S(1)} %get-tuple-element.41.list_ref.refs_3_, f32[192,128]{1,0:T(8,128)S(1)} %get-tuple-element.42.mort_ref.refs_7_), custom_call_target="tpu_custom_call" | custom-call | flops 2000000000 | bytes 100000 | tf_op jit(solution)/shard_map/half/pallas_call | solution.py:555
  16.5 0.0 collective-permute-done.3.refs_1_
  16.5 2.4 %value.1 = f32[16,128]{1,0:T(8,128)S(1)} custom-call(f32[416,128]{1,0:T(8,128)S(1)} %half.1.refs_0_, f32[112,128]{1,0:T(8,128)S(1)} %collective-permute-done.3.refs_1_, bf16[384,512]{1,0:T(8,128)(2,1)S(1)} %get-tuple-element.40.table.refs_2_, f32[32,128]{1,0:T(8,128)S(1)} %get-tuple-element.41.list_ref.refs_3_, f32[64,128]{1,0:T(8,128)S(1)} %get-tuple-element.43.refs_4_, ...), custom_call_target="tpu_custom_call" | custom-call | flops 3000000000 | bytes 100000 | tf_op jit(solution)/shard_map/value/pallas_call | solution.py:564
  18.8 2.7 %collective-permute-start.6 = (f32[16,128]{1,0:T(8,128)S(1)}, f32[16,128]{1,0:T(8,128)S(1)}, u32[]{:S(2)}, u32[]{:S(2)}) collective-permute-start(f32[16,128]{1,0:T(8,128)S(1)} %value.1), channel_id=1, source_target_pairs={{0,12},{4,8},{8,4},{12,0},{1,13},{5,9},{9,5},{13,1},{2,14},{6,10},... | collective-permute-start | bytes 24584 | tf_op jit(solution)/shard_map/total/ppermute | solution.py:37
  21.5 0.0 collective-permute-start.5
  21.5 1.8 %collective-permute-start.4 = (f32[16,128]{1,0:T(8,128)S(1)}, f32[16,128]{1,0:T(8,128)S(1)}, u32[]{:S(2)}, u32[]{:S(2)}) collective-permute-start(f32[16,128]{1,0:T(8,128)S(1)} %value.1), channel_id=1, source_target_pairs={{0,4},{4,0},{8,12},{12,8},{1,5},{5,1},{9,13},{13,9},{2,6},{6,2},{1... | collective-permute-start | bytes 24584 | tf_op jit(solution)/shard_map/total/ppermute | solution.py:37
  23.3 1.1 %collective-permute-done.6 = f32[16,128]{1,0:T(8,128)S(1)} collective-permute-done((f32[16,128]{1,0:T(8,128)S(1)}, f32[16,128]{1,0:T(8,128)S(1)}, u32[]{:S(2)}, u32[]{:S(2)}) %collective-permute-start.6) | collective-permute-done | bytes 8224 | tf_op jit(solution)/shard_map/total/ppermute | solution.py:37
  24.4 1.7 %collective-permute-done.5 = f32[16,128]{1,0:T(8,128)S(1)} collective-permute-done((f32[16,128]{1,0:T(8,128)S(1)}, f32[16,128]{1,0:T(8,128)S(1)}, u32[]{:S(2)}, u32[]{:S(2)}) %collective-permute-start.5) | collective-permute-done | bytes 8224 | tf_op jit(solution)/shard_map/total/ppermute | solution.py:37
  26.1 0.0 collective-permute-done.4
  26.1 0.2 collective-permute-start.9
  26.3 1.4 %collective-permute-start.8 = (f32[16,128]{1,0:T(8,128)S(1)}, f32[16,128]{1,0:T(8,128)S(1)}, u32[]{:S(2)}, u32[]{:S(2)}) collective-permute-start(f32[16,128]{1,0:T(8,128)S(1)} %add_add_fusion.1), channel_id=1, source_target_pairs={{0,2},{1,3},{2,0},{3,1},{4,6},{5,7},{6,4},{7,5},{8,10},{9,11},{10,... | collective-permute-start | bytes 24584 | tf_op jit(solution)/shard_map/total/ppermute | solution.py:37
  27.7 0.3 collective-permute-start.7
  28.0 1.3 %collective-permute-done.9 = f32[16,128]{1,0:T(8,128)S(1)} collective-permute-done((f32[16,128]{1,0:T(8,128)S(1)}, f32[16,128]{1,0:T(8,128)S(1)}, u32[]{:S(2)}, u32[]{:S(2)}) %collective-permute-start.9) | collective-permute-done | bytes 8224 | tf_op jit(solution)/shard_map/total/ppermute | solution.py:37
  29.2 0.7 %collective-permute-done.8 = f32[16,128]{1,0:T(8,128)S(1)} collective-permute-done((f32[16,128]{1,0:T(8,128)S(1)}, f32[16,128]{1,0:T(8,128)S(1)}, u32[]{:S(2)}, u32[]{:S(2)}) %collective-permute-start.8) | collective-permute-done | bytes 8224 | tf_op jit(solution)/shard_map/total/ppermute | solution.py:37
  29.9 0.0 collective-permute-done.7
  30.0 0.1 fusion
  30.0 0.6 %pad_maximum_fusion = f32[32,64]{1,0:T(8,128)} fusion(f32[16,64]{1,0:T(8,128)S(1)} %get-tuple-element.48, f32[16,64]{1,0:T(8,128)S(1)} %get-tuple-element.47), kind=kLoop, calls=%fused_computation | loop fusion | flops 2048 | bytes 16384 | tf_op jit(solution)/shard_map/total/concatenate | solution.py:573
  (2 shorter events, 0.0 us)
Async XLA Ops:
  1.5 8.4 %collective-permute-start = (f32[184,128]{1,0:T(8,128)S(1)}, f32[184,128]{1,0:T(8,128)S(1)}, u32[]{:S(2)}, u32[]{:S(2)}) collective-permute-start(f32[184,128]{1,0:T(8,128)S(1)} %get-tuple-element.26), channel_id=1, source_target_pairs={{0,12},{4,8},{8,4},{12,0},{1,13},{5,9},{9,5},{13,1},{2,14},{6,10},... | collective-permute-start | bytes 282632 | tf_op jit(solution)/shard_map/exchange_far/ppermute | solution.py:37
  6.8 7.7 %collective-permute-start.1 = (f32[184,128]{1,0:T(8,128)S(1)}, f32[184,128]{1,0:T(8,128)S(1)}, u32[]{:S(2)}, u32[]{:S(2)}) collective-permute-start(f32[184,128]{1,0:T(8,128)S(1)} %get-tuple-element.29), channel_id=1, source_target_pairs={{0,8},{4,12},{8,0},{12,4},{1,9},{5,13},{9,1},{13,5},{2,10},{6,14},... | collective-permute-start | bytes 282632 | tf_op jit(solution)/shard_map/exchange_near/ppermute | solution.py:37
  6.9 7.7 %collective-permute-start.2 = (f32[184,128]{1,0:T(8,128)S(1)}, f32[184,128]{1,0:T(8,128)S(1)}, u32[]{:S(2)}, u32[]{:S(2)}) collective-permute-start(f32[184,128]{1,0:T(8,128)S(1)} %get-tuple-element.30), channel_id=1, source_target_pairs={{0,4},{4,0},{8,12},{12,8},{1,5},{5,1},{9,13},{13,9},{2,6},{6,2},{1... | collective-permute-start | bytes 282632 | tf_op jit(solution)/shard_map/exchange_near/ppermute | solution.py:37
  14.8 1.6 %collective-permute-start.3 = (f32[112,128]{1,0:T(8,128)S(1)}, f32[112,128]{1,0:T(8,128)S(1)}, u32[]{:S(2)}, u32[]{:S(2)}) collective-permute-start(f32[112,128]{1,0:T(8,128)S(1)} %get-tuple-element.39.half), channel_id=1, source_target_pairs={{0,1},{1,0},{2,3},{3,2},{4,5},{5,4},{6,7},{7,6},{8,9},{9,8},{10,11... | collective-permute-start | bytes 172040 | tf_op jit(solution)/shard_map/share/ppermute | solution.py:548
  18.8 5.5 %collective-permute-start.6 = (f32[16,128]{1,0:T(8,128)S(1)}, f32[16,128]{1,0:T(8,128)S(1)}, u32[]{:S(2)}, u32[]{:S(2)}) collective-permute-start(f32[16,128]{1,0:T(8,128)S(1)} %value.1), channel_id=1, source_target_pairs={{0,12},{4,8},{8,4},{12,0},{1,13},{5,9},{9,5},{13,1},{2,14},{6,10},... | collective-permute-start | bytes 24584 | tf_op jit(solution)/shard_map/total/ppermute | solution.py:37
  21.5 4.5 %collective-permute-start.5 = (f32[16,128]{1,0:T(8,128)S(1)}, f32[16,128]{1,0:T(8,128)S(1)}, u32[]{:S(2)}, u32[]{:S(2)}) collective-permute-start(f32[16,128]{1,0:T(8,128)S(1)} %value.1), channel_id=1, source_target_pairs={{0,8},{4,12},{8,0},{12,4},{1,9},{5,13},{9,1},{13,5},{2,10},{6,14},... | collective-permute-start | bytes 24584 | tf_op jit(solution)/shard_map/total/ppermute | solution.py:37
  21.5 4.5 %collective-permute-start.4 = (f32[16,128]{1,0:T(8,128)S(1)}, f32[16,128]{1,0:T(8,128)S(1)}, u32[]{:S(2)}, u32[]{:S(2)}) collective-permute-start(f32[16,128]{1,0:T(8,128)S(1)} %value.1), channel_id=1, source_target_pairs={{0,4},{4,0},{8,12},{12,8},{1,5},{5,1},{9,13},{13,9},{2,6},{6,2},{1... | collective-permute-start | bytes 24584 | tf_op jit(solution)/shard_map/total/ppermute | solution.py:37
  26.1 3.2 %collective-permute-start.9 = (f32[16,128]{1,0:T(8,128)S(1)}, f32[16,128]{1,0:T(8,128)S(1)}, u32[]{:S(2)}, u32[]{:S(2)}) collective-permute-start(f32[16,128]{1,0:T(8,128)S(1)} %add_add_fusion.1), channel_id=1, source_target_pairs={{0,3},{1,2},{2,1},{3,0},{4,7},{5,6},{6,5},{7,4},{8,11},{9,10},{10,... | collective-permute-start | bytes 24584 | tf_op jit(solution)/shard_map/total/ppermute | solution.py:37
  26.3 3.7 %collective-permute-start.8 = (f32[16,128]{1,0:T(8,128)S(1)}, f32[16,128]{1,0:T(8,128)S(1)}, u32[]{:S(2)}, u32[]{:S(2)}) collective-permute-start(f32[16,128]{1,0:T(8,128)S(1)} %add_add_fusion.1), channel_id=1, source_target_pairs={{0,2},{1,3},{2,0},{3,1},{4,6},{5,7},{6,4},{7,5},{8,10},{9,11},{10,... | collective-permute-start | bytes 24584 | tf_op jit(solution)/shard_map/total/ppermute | solution.py:37
  27.7 2.2 %collective-permute-start.7 = (f32[16,128]{1,0:T(8,128)S(1)}, f32[16,128]{1,0:T(8,128)S(1)}, u32[]{:S(2)}, u32[]{:S(2)}) collective-permute-start(f32[16,128]{1,0:T(8,128)S(1)} %add_add_fusion.1), channel_id=1, source_target_pairs={{0,1},{1,0},{2,3},{3,2},{4,5},{5,4},{6,7},{7,6},{8,9},{9,8},{10,11... | collective-permute-start | bytes 24584 | tf_op jit(solution)/shard_map/total/ppermute | solution.py:37

commit v6 on v5

--- a/solution.py
+++ b/solution.py
@@ -37,11 +37,14 @@
     return lax.ppermute(x, axis, pairs)
 
 
-def sum_over(x, axis):
+def sum_over(x, axis, swap=False):
     count = lax.axis_size(axis)
     if count & (count - 1):
         return lax.psum(x, axis)
-    parts = [x] + [trade(x, axis, s, count) for s in range(1, count)]
+    shifts = list(range(1, count))
+    if swap and count > 2:
+        shifts[-2:] = [count - 1, count - 2]
+    parts = [x] + [trade(x, axis, s, count) for s in shifts]
     while len(parts) > 1:
         parts = [parts[i] + parts[i + 1] for i in range(0, len(parts), 2)]
     return parts[0]
@@ -136,10 +139,10 @@
         out[used:, :] = jnp.zeros((plan.msg_rows - used, LANES), jnp.float32)
 
 
-def far_kernel(plan, *refs):
+def pack_kernel(plan, *refs):
     given, passed, refs = refs[:9], refs[9 : 9 + PASSED], refs[9 + PASSED :]
-    out, fields_out, hpi_ref, refs = refs[0], refs[1], refs[2], refs[3:]
-    kept, here, sems, pass_sems = refs[:PASSED], refs[PASSED:-2], refs[-2], refs[-1]
+    outs, refs = refs[: plan.count], refs[plan.count :]
+    kept, hpi_ref, here, sems, pass_sems = refs[:PASSED], refs[PASSED], refs[PASSED + 1 : -2], refs[-2], refs[-1]
     side = lax.rem(lax.axis_index("paths"), plan.halves)
     lots = plan.half_rows * LANES
     sources = list(given)
@@ -171,19 +174,13 @@
         share(region_ref[...].astype(jnp.float32)),
         share(deal_ref[...].astype(jnp.float32)),
     )
-    for i, field in enumerate(fields):
-        fields_out[i * hr : (i + 1) * hr, :] = field
+    fields = jnp.concatenate(fields, axis=0)
     copies[0].wait()
-    write_homes(plan, hpi_ref, [(out, plan.order[0])])
-    write_loans(plan, out, fields_out[...])
+    write_homes(plan, hpi_ref, list(zip(outs, plan.order)))
+    for out in outs:
+        write_loans(plan, out, fields)
     for copy in passing:
         copy.wait()
-
-
-def near_kernel(plan, hpi_ref, fields_ref, *outs):
-    write_homes(plan, hpi_ref, list(zip(outs, plan.order[1:])))
-    for out in outs:
-        write_loans(plan, out, fields_ref[...])
 
 
 def list_deals(plan, owner, tall):
@@ -484,32 +481,20 @@
     passed = (deal_owner.T, tranche_order, tranche_share, tranche_rate, rate_paths.transpose(1, 0, 2))
     here = [x.shape for x in given]
     here[1] = (plan.half_rows * LANES,) + here[1][1:]
-    with jax.named_scope("pack_far"):
-        msg, fields, homes, *kept = pl.pallas_call(
-            functools.partial(far_kernel, plan),
-            out_shape=[
-                pltpu.VMEM((plan.msg_rows, LANES), f32),
-                pltpu.VMEM((FIELDS * plan.half_rows, LANES), f32),
-                pltpu.VMEM(given[0].shape, f32),
-            ]
+    with jax.named_scope("pack"):
+        made = pl.pallas_call(
+            functools.partial(pack_kernel, plan),
+            out_shape=[pltpu.VMEM((plan.msg_rows, LANES), f32)] * count
             + [pltpu.VMEM(x.shape, x.dtype) for x in passed],
             in_specs=[pl.BlockSpec(memory_space=pltpu.HBM)] * (len(given) + PASSED),
-            scratch_shapes=[pltpu.VMEM(dims, x.dtype) for dims, x in zip(here[1:], given[1:])]
+            scratch_shapes=[pltpu.VMEM(dims, x.dtype) for dims, x in zip(here, given)]
             + [pltpu.SemaphoreType.DMA((len(given),)), pltpu.SemaphoreType.DMA((PASSED,))],
             compiler_params=params,
             cost_estimate=cost(1),
         )(*[pltpu.with_memory_space_constraint(x, pltpu.HBM) for x in given + passed])
-    with jax.named_scope("exchange_far"):
-        got = [trade(msg, "loans", plan.order[0], count)]
-    with jax.named_scope("pack_near"):
-        msgs = pl.pallas_call(
-            functools.partial(near_kernel, plan),
-            out_shape=[pltpu.VMEM((plan.msg_rows, LANES), f32)] * (count - 1),
-            compiler_params=params,
-            cost_estimate=cost(1),
-        )(homes, fields)
-    with jax.named_scope("exchange_near"):
-        got += [trade(msg, "loans", s, count) if s else msg for s, msg in zip(plan.order[1:], msgs)]
+    msgs, kept = made[:count], made[count:]
+    with jax.named_scope("exchange"):
+        got = [trade(msg, "loans", s, count) if s else msg for s, msg in zip(plan.order, msgs)]
     with jax.named_scope("deals"):
         table_shape = (tranches, plan.width)
         listing, ends, opening, rates, mort, disc = pl.pallas_call(
@@ -569,7 +554,7 @@
             cost_estimate=cost(3),
         )(*other, halves[-1], table, listing, ends, opening, rates, mort, disc)
     with jax.named_scope("total"):
-        total = sum_over(sum_over(part, "loans"), "paths")
+        total = sum_over(sum_over(part, "loans", swap=True), "paths")
         return jnp.concatenate(
             [total[:, i * tranches : (i + 1) * tranches] for i in range(plan.out_fold)], axis=0
         )

time: 30.8 us -> 30.2 us (0.981)
  starting transfers between devices: 12.2 us -> 11.2 us
  waiting for transfers between devices: 10.8 us -> 11.4 us
    ppermute x9, starting transfers between devices: 12.1 us -> 11.2 us  [trade(): return lax.ppermute(x, axis, pairs)]
    ppermute x9, waiting for transfers between devices: 10.8 us -> 11.4 us  [trade(): return lax.ppermute(x, axis, pairs)]
    pallas_call x2 -> x1, Pallas kernels: 1.64 us -> 1.51 us  [on_device(): pl.pallas_call(functools.partial(pack_kernel, plan), out_shape=[pltpu.VME...]
  transfers between devices with their start and end apart: 10 -> 10, of which waited for: 6 -> 7; matrix products, arithmetic and copies ran while one was open for 0% -> 0% of each run, Pallas kernels for 9% -> 8%
where the time goes in v6:
time: 30.2 us; the launch traced here: 30.1 us
  waiting for transfers between devices  11.4 us (38%)
  starting transfers between devices  11.2 us (37%)
  Pallas kernels  6.69 us (22%)
  other arithmetic  0.62 us (2%)
    ppermute x9, waiting for transfers between devices, trade(): return lax.ppermute(x, axis, pairs)  11.4 us
    ppermute x9, starting transfers between devices, trade(): return lax.ppermute(x, axis, pairs)  11.2 us
    pallas_call x1, Pallas kernels, on_device(): pl.pallas_call(functools.partial(value_kernel, plan, float(paths * sides)...  2.35 us
    pallas_call x1, Pallas kernels, on_device(): pl.pallas_call(functools.partial(half_kernel, plan), out_shape=shape(*sum...  1.55 us
    pallas_call x1, Pallas kernels, on_device(): pl.pallas_call(functools.partial(pack_kernel, plan), out_shape=[pltpu.VME...  1.51 us
    pallas_call x1, Pallas kernels, on_device(): pl.pallas_call(functools.partial(deal_kernel, plan), out_shape=[shape(dea...  0.97 us
    concatenate x1, other arithmetic, on_device(): jnp.concatenate([total[:, i * tranches:(i + 1) * tranches] for i in range...  0.61 us
  transfers between devices with their start and end apart: 10, of which 7 were waited for; matrix products, arithmetic and copies ran while one was open for 0% of the time, Pallas kernels for 8%

profile of v6, /device:TPU:0, one launch (start us, length us, event | category | flops | bytes accessed | tf_op | source)
XLA Modules:
  0.0 30.1 jit_solution(12241573750139464842)
XLA Ops:
  0.0 1.5 %pack.1 = (f32[184,128]{1,0:T(8,128)S(1)}, f32[184,128]{1,0:T(8,128)S(1)}, f32[184,128]{1,0:T(8,128)S(1)}, f32[184,128]{1,0:T(8,128)S(1)}, s32[1,32]{1,0:T(1,128...) custom-call(f32[6,104,128]{2,1,0:T(8,128)} %bitcast.10, ...), custom_call_target="tpu_custom_call" | custom-call | flops 1000000000 | bytes 100000 | tf_op jit(solution)/shard_map/pack/pallas_call | solution.py:485
  1.5 5.1 %collective-permute-start = (f32[184,128]{1,0:T(8,128)S(1)}, f32[184,128]{1,0:T(8,128)S(1)}, u32[]{:S(2)}, u32[]{:S(2)}) collective-permute-start(f32[184,128]{1,0:T(8,128)S(1)} %get-tuple-element.24), channel_id=1, source_target_pairs={{0,12},{4,8},{8,4},{12,0},{1,13},{5,9},{9,5},{13,1},{2,14},{6,10},... | collective-permute-start | bytes 282632 | tf_op jit(solution)/shard_map/exchange/ppermute | solution.py:37
  6.6 0.0 collective-permute-start.1
  6.6 0.6 %collective-permute-start.2 = (f32[184,128]{1,0:T(8,128)S(1)}, f32[184,128]{1,0:T(8,128)S(1)}, u32[]{:S(2)}, u32[]{:S(2)}) collective-permute-start(f32[184,128]{1,0:T(8,128)S(1)} %get-tuple-element.26), channel_id=1, source_target_pairs={{0,4},{4,0},{8,12},{12,8},{1,5},{5,1},{9,13},{13,9},{2,6},{6,2},{1... | collective-permute-start | bytes 282632 | tf_op jit(solution)/shard_map/exchange/ppermute | solution.py:37
  7.3 1.0 %deals.1 = (f32[32,128]{1,0:T(8,128)S(1)}, f32[64,128]{1,0:T(8,128)S(1)}, f32[64,128]{1,0:T(8,128)S(1)}, f32[64,128]{1,0:T(8,128)S(1)}, f32[192,128]{1,0:T(8,128)S(1)}, /*index=5*/f32[6,8,128]{2,1,0:T(8,128)S(1)}) custom-call(s32[1,32]{1,0:T(1,128)S(1)} %get-tuple-element.28.owner_ref, s32[32,64]{1,0:T(8,128)S(1)} %get-tuple-element.29.order_ref, ...), custom_call_target="tpu_custom_call" | custom-call | flops 1000000000 | bytes 100000 | tf_op jit(solution)/shard_map/deals/pallas_call | solution.py:500
  8.3 1.9 %collective-permute-done.refs_0_ = f32[184,128]{1,0:T(8,128)S(1)} collective-permute-done((f32[184,128]{1,0:T(8,128)S(1)}, f32[184,128]{1,0:T(8,128)S(1)}, u32[]{:S(2)}, u32[]{:S(2)}) %collective-permute-start) | collective-permute-done | bytes 94240 | tf_op jit(solution)/shard_map/exchange/ppermute | solution.py:37
  10.2 4.4 %collective-permute-done.1.refs_1_ = f32[184,128]{1,0:T(8,128)S(1)} collective-permute-done((f32[184,128]{1,0:T(8,128)S(1)}, f32[184,128]{1,0:T(8,128)S(1)}, u32[]{:S(2)}, u32[]{:S(2)}) %collective-permute-start.1) | collective-permute-done | bytes 94240 | tf_op jit(solution)/shard_map/exchange/ppermute | solution.py:37
  14.5 0.0 collective-permute-done.2.refs_2_
  14.5 0.3 %sort.1 = (f32[112,128]{1,0:T(8,128)S(1)}, bf16[384,512]{1,0:T(8,128)(2,1)S(1)}) custom-call(f32[184,128]{1,0:T(8,128)S(1)} %collective-permute-done.refs_0_, f32[184,128]{1,0:T(8,128)S(1)} %collective-permute-done.1.refs_1_, f32[184,128]{1,0:T(8,128)S(1)} %collective-permute-done.2.refs_2_, f32[184,128]{1,0:T(8,128)S(1)} %get-tuple-element.34.refs_3_), custom_call_target="tpu_custom_call" | custom-call | flops 500000000 | bytes 100000 | tf_op jit(solution)/shard_map/sort/pallas_call | solution.py:516
  14.9 0.1 collective-permute-start.3
  15.0 1.5 %half.1.refs_0_ = f32[416,128]{1,0:T(8,128)S(1)} custom-call(f32[112,128]{1,0:T(8,128)S(1)} %get-tuple-element.35.half, bf16[384,512]{1,0:T(8,128)(2,1)S(1)} %get-tuple-element.36.table.refs_2_, f32[32,128]{1,0:T(8,128)S(1)} %get-tuple-element.37.list_ref.refs_3_, f32[192,128]{1,0:T(8,128)S(1)} %get-tuple-element.38.mort_ref.refs_7_), custom_call_target="tpu_custom_call" | custom-call | flops 2000000000 | bytes 100000 | tf_op jit(solution)/shard_map/half/pallas_call | solution.py:540
  16.5 0.0 collective-permute-done.3.refs_1_
  16.5 2.3 %value.1 = f32[16,128]{1,0:T(8,128)S(1)} custom-call(f32[416,128]{1,0:T(8,128)S(1)} %half.1.refs_0_, f32[112,128]{1,0:T(8,128)S(1)} %collective-permute-done.3.refs_1_, bf16[384,512]{1,0:T(8,128)(2,1)S(1)} %get-tuple-element.36.table.refs_2_, f32[32,128]{1,0:T(8,128)S(1)} %get-tuple-element.37.list_ref.refs_3_, f32[64,128]{1,0:T(8,128)S(1)} %get-tuple-element.39.refs_4_, ...), custom_call_target="tpu_custom_call" | custom-call | flops 3000000000 | bytes 100000 | tf_op jit(solution)/shard_map/value/pallas_call | solution.py:549
  18.9 0.7 %collective-permute-start.6 = (f32[16,128]{1,0:T(8,128)S(1)}, f32[16,128]{1,0:T(8,128)S(1)}, u32[]{:S(2)}, u32[]{:S(2)}) collective-permute-start(f32[16,128]{1,0:T(8,128)S(1)} %value.1), channel_id=1, source_target_pairs={{0,8},{4,12},{8,0},{12,4},{1,9},{5,13},{9,1},{13,5},{2,10},{6,14},... | collective-permute-start | bytes 24584 | tf_op jit(solution)/shard_map/total/ppermute | solution.py:37
  19.6 2.3 %collective-permute-start.5 = (f32[16,128]{1,0:T(8,128)S(1)}, f32[16,128]{1,0:T(8,128)S(1)}, u32[]{:S(2)}, u32[]{:S(2)}) collective-permute-start(f32[16,128]{1,0:T(8,128)S(1)} %value.1), channel_id=1, source_target_pairs={{0,12},{4,8},{8,4},{12,0},{1,13},{5,9},{9,5},{13,1},{2,14},{6,10},... | collective-permute-start | bytes 24584 | tf_op jit(solution)/shard_map/total/ppermute | solution.py:37
  21.9 0.5 %collective-permute-start.4 = (f32[16,128]{1,0:T(8,128)S(1)}, f32[16,128]{1,0:T(8,128)S(1)}, u32[]{:S(2)}, u32[]{:S(2)}) collective-permute-start(f32[16,128]{1,0:T(8,128)S(1)} %value.1), channel_id=1, source_target_pairs={{0,4},{4,0},{8,12},{12,8},{1,5},{5,1},{9,13},{13,9},{2,6},{6,2},{1... | collective-permute-start | bytes 24584 | tf_op jit(solution)/shard_map/total/ppermute | solution.py:37
  22.4 1.1 %collective-permute-done.6 = f32[16,128]{1,0:T(8,128)S(1)} collective-permute-done((f32[16,128]{1,0:T(8,128)S(1)}, f32[16,128]{1,0:T(8,128)S(1)}, u32[]{:S(2)}, u32[]{:S(2)}) %collective-permute-start.6) | collective-permute-done | bytes 8224 | tf_op jit(solution)/shard_map/total/ppermute | solution.py:37
  23.6 1.5 %collective-permute-done.5 = f32[16,128]{1,0:T(8,128)S(1)} collective-permute-done((f32[16,128]{1,0:T(8,128)S(1)}, f32[16,128]{1,0:T(8,128)S(1)}, u32[]{:S(2)}, u32[]{:S(2)}) %collective-permute-start.5) | collective-permute-done | bytes 8224 | tf_op jit(solution)/shard_map/total/ppermute | solution.py:37
  25.0 0.5 %collective-permute-done.4 = f32[16,128]{1,0:T(8,128)S(1)} collective-permute-done((f32[16,128]{1,0:T(8,128)S(1)}, f32[16,128]{1,0:T(8,128)S(1)}, u32[]{:S(2)}, u32[]{:S(2)}) %collective-permute-start.4) | collective-permute-done | bytes 8224 | tf_op jit(solution)/shard_map/total/ppermute | solution.py:37
  25.6 0.2 collective-permute-start.9
  25.7 1.4 %collective-permute-start.8 = (f32[16,128]{1,0:T(8,128)S(1)}, f32[16,128]{1,0:T(8,128)S(1)}, u32[]{:S(2)}, u32[]{:S(2)}) collective-permute-start(f32[16,128]{1,0:T(8,128)S(1)} %add_add_fusion.1), channel_id=1, source_target_pairs={{0,2},{1,3},{2,0},{3,1},{4,6},{5,7},{6,4},{7,5},{8,10},{9,11},{10,... | collective-permute-start | bytes 24584 | tf_op jit(solution)/shard_map/total/ppermute | solution.py:37
  27.1 0.3 collective-permute-start.7
  27.4 1.3 %collective-permute-done.9 = f32[16,128]{1,0:T(8,128)S(1)} collective-permute-done((f32[16,128]{1,0:T(8,128)S(1)}, f32[16,128]{1,0:T(8,128)S(1)}, u32[]{:S(2)}, u32[]{:S(2)}) %collective-permute-start.9) | collective-permute-done | bytes 8224 | tf_op jit(solution)/shard_map/total/ppermute | solution.py:37
  28.7 0.7 %collective-permute-done.8 = f32[16,128]{1,0:T(8,128)S(1)} collective-permute-done((f32[16,128]{1,0:T(8,128)S(1)}, f32[16,128]{1,0:T(8,128)S(1)}, u32[]{:S(2)}, u32[]{:S(2)}) %collective-permute-start.8) | collective-permute-done | bytes 8224 | tf_op jit(solution)/shard_map/total/ppermute | solution.py:37
  29.4 0.0 collective-permute-done.7
  29.4 0.1 fusion
  29.5 0.6 %pad_maximum_fusion = f32[32,64]{1,0:T(8,128)} fusion(f32[16,64]{1,0:T(8,128)S(1)} %get-tuple-element.44, f32[16,64]{1,0:T(8,128)S(1)} %get-tuple-element.43), kind=kLoop, calls=%fused_computation | loop fusion | flops 2048 | bytes 16384 | tf_op jit(solution)/shard_map/total/concatenate | solution.py:558
  (2 shorter events, 0.0 us)
Async XLA Ops:
  1.5 8.6 %collective-permute-start = (f32[184,128]{1,0:T(8,128)S(1)}, f32[184,128]{1,0:T(8,128)S(1)}, u32[]{:S(2)}, u32[]{:S(2)}) collective-permute-start(f32[184,128]{1,0:T(8,128)S(1)} %get-tuple-element.24), channel_id=1, source_target_pairs={{0,12},{4,8},{8,4},{12,0},{1,13},{5,9},{9,5},{13,1},{2,14},{6,10},... | collective-permute-start | bytes 282632 | tf_op jit(solution)/shard_map/exchange/ppermute | solution.py:37
  6.6 7.9 %collective-permute-start.1 = (f32[184,128]{1,0:T(8,128)S(1)}, f32[184,128]{1,0:T(8,128)S(1)}, u32[]{:S(2)}, u32[]{:S(2)}) collective-permute-start(f32[184,128]{1,0:T(8,128)S(1)} %get-tuple-element.25), channel_id=1, source_target_pairs={{0,8},{4,12},{8,0},{12,4},{1,9},{5,13},{9,1},{13,5},{2,10},{6,14},... | collective-permute-start | bytes 282632 | tf_op jit(solution)/shard_map/exchange/ppermute | solution.py:37
  6.6 7.9 %collective-permute-start.2 = (f32[184,128]{1,0:T(8,128)S(1)}, f32[184,128]{1,0:T(8,128)S(1)}, u32[]{:S(2)}, u32[]{:S(2)}) collective-permute-start(f32[184,128]{1,0:T(8,128)S(1)} %get-tuple-element.26), channel_id=1, source_target_pairs={{0,4},{4,0},{8,12},{12,8},{1,5},{5,1},{9,13},{13,9},{2,6},{6,2},{1... | collective-permute-start | bytes 282632 | tf_op jit(solution)/shard_map/exchange/ppermute | solution.py:37
  14.9 1.6 %collective-permute-start.3 = (f32[112,128]{1,0:T(8,128)S(1)}, f32[112,128]{1,0:T(8,128)S(1)}, u32[]{:S(2)}, u32[]{:S(2)}) collective-permute-start(f32[112,128]{1,0:T(8,128)S(1)} %get-tuple-element.35.half), channel_id=1, source_target_pairs={{0,1},{1,0},{2,3},{3,2},{4,5},{5,4},{6,7},{7,6},{8,9},{9,8},{10,11... | collective-permute-start | bytes 172040 | tf_op jit(solution)/shard_map/share/ppermute | solution.py:533
  18.9 4.7 %collective-permute-start.6 = (f32[16,128]{1,0:T(8,128)S(1)}, f32[16,128]{1,0:T(8,128)S(1)}, u32[]{:S(2)}, u32[]{:S(2)}) collective-permute-start(f32[16,128]{1,0:T(8,128)S(1)} %value.1), channel_id=1, source_target_pairs={{0,8},{4,12},{8,0},{12,4},{1,9},{5,13},{9,1},{13,5},{2,10},{6,14},... | collective-permute-start | bytes 24584 | tf_op jit(solution)/shard_map/total/ppermute | solution.py:37
  19.6 5.4 %collective-permute-start.5 = (f32[16,128]{1,0:T(8,128)S(1)}, f32[16,128]{1,0:T(8,128)S(1)}, u32[]{:S(2)}, u32[]{:S(2)}) collective-permute-start(f32[16,128]{1,0:T(8,128)S(1)} %value.1), channel_id=1, source_target_pairs={{0,12},{4,8},{8,4},{12,0},{1,13},{5,9},{9,5},{13,1},{2,14},{6,10},... | collective-permute-start | bytes 24584 | tf_op jit(solution)/shard_map/total/ppermute | solution.py:37
  21.9 3.7 %collective-permute-start.4 = (f32[16,128]{1,0:T(8,128)S(1)}, f32[16,128]{1,0:T(8,128)S(1)}, u32[]{:S(2)}, u32[]{:S(2)}) collective-permute-start(f32[16,128]{1,0:T(8,128)S(1)} %value.1), channel_id=1, source_target_pairs={{0,4},{4,0},{8,12},{12,8},{1,5},{5,1},{9,13},{13,9},{2,6},{6,2},{1... | collective-permute-start | bytes 24584 | tf_op jit(solution)/shard_map/total/ppermute | solution.py:37
  25.6 3.1 %collective-permute-start.9 = (f32[16,128]{1,0:T(8,128)S(1)}, f32[16,128]{1,0:T(8,128)S(1)}, u32[]{:S(2)}, u32[]{:S(2)}) collective-permute-start(f32[16,128]{1,0:T(8,128)S(1)} %add_add_fusion.1), channel_id=1, source_target_pairs={{0,3},{1,2},{2,1},{3,0},{4,7},{5,6},{6,5},{7,4},{8,11},{9,10},{10,... | collective-permute-start | bytes 24584 | tf_op jit(solution)/shard_map/total/ppermute | solution.py:37
  25.7 3.7 %collective-permute-start.8 = (f32[16,128]{1,0:T(8,128)S(1)}, f32[16,128]{1,0:T(8,128)S(1)}, u32[]{:S(2)}, u32[]{:S(2)}) collective-permute-start(f32[16,128]{1,0:T(8,128)S(1)} %add_add_fusion.1), channel_id=1, source_target_pairs={{0,2},{1,3},{2,0},{3,1},{4,6},{5,7},{6,4},{7,5},{8,10},{9,11},{10,... | collective-permute-start | bytes 24584 | tf_op jit(solution)/shard_map/total/ppermute | solution.py:37
  27.1 2.3 %collective-permute-start.7 = (f32[16,128]{1,0:T(8,128)S(1)}, f32[16,128]{1,0:T(8,128)S(1)}, u32[]{:S(2)}, u32[]{:S(2)}) collective-permute-start(f32[16,128]{1,0:T(8,128)S(1)} %add_add_fusion.1), channel_id=1, source_target_pairs={{0,1},{1,0},{2,3},{3,2},{4,5},{5,4},{6,7},{7,6},{8,9},{9,8},{10,11... | collective-permute-start | bytes 24584 | tf_op jit(solution)/shard_map/total/ppermute | solution.py:37

commit v7 on v5

--- a/solution.py
+++ b/solution.py
@@ -37,11 +37,14 @@
     return lax.ppermute(x, axis, pairs)
 
 
-def sum_over(x, axis):
+def sum_over(x, axis, swap=False):
     count = lax.axis_size(axis)
     if count & (count - 1):
         return lax.psum(x, axis)
-    parts = [x] + [trade(x, axis, s, count) for s in range(1, count)]
+    shifts = list(range(1, count))
+    if swap and count > 2:
+        shifts[-2:] = [count - 1, count - 2]
+    parts = [x] + [trade(x, axis, s, count) for s in shifts]
     while len(parts) > 1:
         parts = [parts[i] + parts[i + 1] for i in range(0, len(parts), 2)]
     return parts[0]
@@ -569,7 +572,7 @@
             cost_estimate=cost(3),
         )(*other, halves[-1], table, listing, ends, opening, rates, mort, disc)
     with jax.named_scope("total"):
-        total = sum_over(sum_over(part, "loans"), "paths")
+        total = sum_over(sum_over(part, "loans", swap=True), "paths")
         return jnp.concatenate(
             [total[:, i * tranches : (i + 1) * tranches] for i in range(plan.out_fold)], axis=0
         )

time: 30.8 us -> 30.2 us (0.981)
  starting transfers between devices: 12.2 us -> 11.2 us
  waiting for transfers between devices: 10.8 us -> 11.2 us
    ppermute x9, starting transfers between devices: 12.1 us -> 11.2 us  [trade(): return lax.ppermute(x, axis, pairs)]
    ppermute x9, waiting for transfers between devices: 10.8 us -> 11.2 us  [trade(): return lax.ppermute(x, axis, pairs)]
  transfers between devices with their start and end apart: 10 -> 10, of which waited for: 6 -> 7; matrix products, arithmetic and copies ran while one was open for 0% -> 0% of each run, Pallas kernels for 9% -> 9%
where the time goes in v7:
time: 30.2 us; the launch traced here: 30.1 us
  starting transfers between devices  11.2 us (37%)
  waiting for transfers between devices  11.2 us (37%)
  Pallas kernels  6.83 us (23%)
  other arithmetic  0.62 us (2%)
    ppermute x9, waiting for transfers between devices, trade(): return lax.ppermute(x, axis, pairs)  11.2 us
    ppermute x9, starting transfers between devices, trade(): return lax.ppermute(x, axis, pairs)  11.2 us
    pallas_call x1, Pallas kernels, on_device(): pl.pallas_call(functools.partial(value_kernel, plan, float(paths * sides)...  2.35 us
    pallas_call x1, Pallas kernels, on_device(): pl.pallas_call(functools.partial(half_kernel, plan), out_shape=shape(*sum...  1.55 us
    pallas_call x1, Pallas kernels, on_device(): pl.pallas_call(functools.partial(far_kernel, plan), out_shape=[pltpu.VMEM...  1.47 us
    pallas_call x1, Pallas kernels, on_device(): pl.pallas_call(functools.partial(deal_kernel, plan), out_shape=[shape(dea...  0.97 us
    concatenate x1, other arithmetic, on_device(): jnp.concatenate([total[:, i * tranches:(i + 1) * tranches] for i in range...  0.61 us
  transfers between devices with their start and end apart: 10, of which 7 were waited for; matrix products, arithmetic and copies ran while one was open for 0% of the time, Pallas kernels for 9%

profile of v7, /device:TPU:0, one launch (start us, length us, event | category | flops | bytes accessed | tf_op | source)
XLA Modules:
  0.0 30.1 jit_solution(11690125349786338417)
XLA Ops:
  0.0 1.5 %pack_far.1 = (f32[184,128]{1,0:T(8,128)S(1)}, f32[28,128]{1,0:T(8,128)S(1)}, f32[6,104,128]{2,1,0:T(8,128)S(1)}, s32[1,32]{1,0:T(1,128)S(1)}, s32[32,64]{1,0:T(...) custom-call(f32[6,104,128]{2,1,0:T(8,128)} %bitcast.10, ...), custom_call_target="tpu_custom_call" | custom-call | flops 1000000000 | bytes 100000 | tf_op jit(solution)/shard_map/pack_far/pallas_call | solution.py:491
  1.5 5.1 %collective-permute-start = (f32[184,128]{1,0:T(8,128)S(1)}, f32[184,128]{1,0:T(8,128)S(1)}, u32[]{:S(2)}, u32[]{:S(2)}) collective-permute-start(f32[184,128]{1,0:T(8,128)S(1)} %get-tuple-element.26), channel_id=1, source_target_pairs={{0,12},{4,8},{8,4},{12,0},{1,13},{5,9},{9,5},{13,1},{2,14},{6,10},... | collective-permute-start | bytes 282632 | tf_op jit(solution)/shard_map/exchange_far/ppermute | solution.py:37
  6.6 0.2 pack_near.1
  6.8 0.1 collective-permute-start.1
  6.9 0.6 %collective-permute-start.2 = (f32[184,128]{1,0:T(8,128)S(1)}, f32[184,128]{1,0:T(8,128)S(1)}, u32[]{:S(2)}, u32[]{:S(2)}) collective-permute-start(f32[184,128]{1,0:T(8,128)S(1)} %get-tuple-element.30), channel_id=1, source_target_pairs={{0,4},{4,0},{8,12},{12,8},{1,5},{5,1},{9,13},{13,9},{2,6},{6,2},{1... | collective-permute-start | bytes 282632 | tf_op jit(solution)/shard_map/exchange_near/ppermute | solution.py:37
  7.4 1.0 %deals.1 = (f32[32,128]{1,0:T(8,128)S(1)}, f32[64,128]{1,0:T(8,128)S(1)}, f32[64,128]{1,0:T(8,128)S(1)}, f32[64,128]{1,0:T(8,128)S(1)}, f32[192,128]{1,0:T(8,128)S(1)}, /*index=5*/f32[6,8,128]{2,1,0:T(8,128)S(1)}) custom-call(s32[1,32]{1,0:T(1,128)S(1)} %get-tuple-element.32.owner_ref, s32[32,64]{1,0:T(8,128)S(1)} %get-tuple-element.33.order_ref, ...), custom_call_target="tpu_custom_call" | custom-call | flops 1000000000 | bytes 100000 | tf_op jit(solution)/shard_map/deals/pallas_call | solution.py:518
  8.4 1.5 %collective-permute-done.refs_0_ = f32[184,128]{1,0:T(8,128)S(1)} collective-permute-done((f32[184,128]{1,0:T(8,128)S(1)}, f32[184,128]{1,0:T(8,128)S(1)}, u32[]{:S(2)}, u32[]{:S(2)}) %collective-permute-start) | collective-permute-done | bytes 94240 | tf_op jit(solution)/shard_map/exchange_far/ppermute | solution.py:37
  9.9 4.6 %collective-permute-done.1.refs_1_ = f32[184,128]{1,0:T(8,128)S(1)} collective-permute-done((f32[184,128]{1,0:T(8,128)S(1)}, f32[184,128]{1,0:T(8,128)S(1)}, u32[]{:S(2)}, u32[]{:S(2)}) %collective-permute-start.1) | collective-permute-done | bytes 94240 | tf_op jit(solution)/shard_map/exchange_near/ppermute | solution.py:37
  14.5 0.0 collective-permute-done.2.refs_2_
  14.5 0.3 %sort.1 = (f32[112,128]{1,0:T(8,128)S(1)}, bf16[384,512]{1,0:T(8,128)(2,1)S(1)}) custom-call(f32[184,128]{1,0:T(8,128)S(1)} %collective-permute-done.refs_0_, f32[184,128]{1,0:T(8,128)S(1)} %collective-permute-done.1.refs_1_, f32[184,128]{1,0:T(8,128)S(1)} %collective-permute-done.2.refs_2_, f32[184,128]{1,0:T(8,128)S(1)} %get-tuple-element.38.refs_3_), custom_call_target="tpu_custom_call" | custom-call | flops 500000000 | bytes 100000 | tf_op jit(solution)/shard_map/sort/pallas_call | solution.py:534
  14.8 0.1 collective-permute-start.3
  14.9 1.5 %half.1.refs_0_ = f32[416,128]{1,0:T(8,128)S(1)} custom-call(f32[112,128]{1,0:T(8,128)S(1)} %get-tuple-element.39.half, bf16[384,512]{1,0:T(8,128)(2,1)S(1)} %get-tuple-element.40.table.refs_2_, f32[32,128]{1,0:T(8,128)S(1)} %get-tuple-element.41.list_ref.refs_3_, f32[192,128]{1,0:T(8,128)S(1)} %get-tuple-element.42.mort_ref.refs_7_), custom_call_target="tpu_custom_call" | custom-call | flops 2000000000 | bytes 100000 | tf_op jit(solution)/shard_map/half/pallas_call | solution.py:558
  16.5 0.0 collective-permute-done.3.refs_1_
  16.5 2.4 %value.1 = f32[16,128]{1,0:T(8,128)S(1)} custom-call(f32[416,128]{1,0:T(8,128)S(1)} %half.1.refs_0_, f32[112,128]{1,0:T(8,128)S(1)} %collective-permute-done.3.refs_1_, bf16[384,512]{1,0:T(8,128)(2,1)S(1)} %get-tuple-element.40.table.refs_2_, f32[32,128]{1,0:T(8,128)S(1)} %get-tuple-element.41.list_ref.refs_3_, f32[64,128]{1,0:T(8,128)S(1)} %get-tuple-element.43.refs_4_, ...), custom_call_target="tpu_custom_call" | custom-call | flops 3000000000 | bytes 100000 | tf_op jit(solution)/shard_map/value/pallas_call | solution.py:567
  18.8 0.6 %collective-permute-start.6 = (f32[16,128]{1,0:T(8,128)S(1)}, f32[16,128]{1,0:T(8,128)S(1)}, u32[]{:S(2)}, u32[]{:S(2)}) collective-permute-start(f32[16,128]{1,0:T(8,128)S(1)} %value.1), channel_id=1, source_target_pairs={{0,8},{4,12},{8,0},{12,4},{1,9},{5,13},{9,1},{13,5},{2,10},{6,14},... | collective-permute-start | bytes 24584 | tf_op jit(solution)/shard_map/total/ppermute | solution.py:37
  19.5 2.4 %collective-permute-start.5 = (f32[16,128]{1,0:T(8,128)S(1)}, f32[16,128]{1,0:T(8,128)S(1)}, u32[]{:S(2)}, u32[]{:S(2)}) collective-permute-start(f32[16,128]{1,0:T(8,128)S(1)} %value.1), channel_id=1, source_target_pairs={{0,12},{4,8},{8,4},{12,0},{1,13},{5,9},{9,5},{13,1},{2,14},{6,10},... | collective-permute-start | bytes 24584 | tf_op jit(solution)/shard_map/total/ppermute | solution.py:37
  21.9 0.5 %collective-permute-start.4 = (f32[16,128]{1,0:T(8,128)S(1)}, f32[16,128]{1,0:T(8,128)S(1)}, u32[]{:S(2)}, u32[]{:S(2)}) collective-permute-start(f32[16,128]{1,0:T(8,128)S(1)} %value.1), channel_id=1, source_target_pairs={{0,4},{4,0},{8,12},{12,8},{1,5},{5,1},{9,13},{13,9},{2,6},{6,2},{1... | collective-permute-start | bytes 24584 | tf_op jit(solution)/shard_map/total/ppermute | solution.py:37
  22.4 1.1 %collective-permute-done.6 = f32[16,128]{1,0:T(8,128)S(1)} collective-permute-done((f32[16,128]{1,0:T(8,128)S(1)}, f32[16,128]{1,0:T(8,128)S(1)}, u32[]{:S(2)}, u32[]{:S(2)}) %collective-permute-start.6) | collective-permute-done | bytes 8224 | tf_op jit(solution)/shard_map/total/ppermute | solution.py:37
  23.5 1.4 %collective-permute-done.5 = f32[16,128]{1,0:T(8,128)S(1)} collective-permute-done((f32[16,128]{1,0:T(8,128)S(1)}, f32[16,128]{1,0:T(8,128)S(1)}, u32[]{:S(2)}, u32[]{:S(2)}) %collective-permute-start.5) | collective-permute-done | bytes 8224 | tf_op jit(solution)/shard_map/total/ppermute | solution.py:37
  24.9 0.6 %collective-permute-done.4 = f32[16,128]{1,0:T(8,128)S(1)} collective-permute-done((f32[16,128]{1,0:T(8,128)S(1)}, f32[16,128]{1,0:T(8,128)S(1)}, u32[]{:S(2)}, u32[]{:S(2)}) %collective-permute-start.4) | collective-permute-done | bytes 8224 | tf_op jit(solution)/shard_map/total/ppermute | solution.py:37
  25.5 0.2 collective-permute-start.9
  25.7 1.4 %collective-permute-start.8 = (f32[16,128]{1,0:T(8,128)S(1)}, f32[16,128]{1,0:T(8,128)S(1)}, u32[]{:S(2)}, u32[]{:S(2)}) collective-permute-start(f32[16,128]{1,0:T(8,128)S(1)} %add_add_fusion.1), channel_id=1, source_target_pairs={{0,2},{1,3},{2,0},{3,1},{4,6},{5,7},{6,4},{7,5},{8,10},{9,11},{10,... | collective-permute-start | bytes 24584 | tf_op jit(solution)/shard_map/total/ppermute | solution.py:37
  27.1 0.3 %collective-permute-start.7 = (f32[16,128]{1,0:T(8,128)S(1)}, f32[16,128]{1,0:T(8,128)S(1)}, u32[]{:S(2)}, u32[]{:S(2)}) collective-permute-start(f32[16,128]{1,0:T(8,128)S(1)} %add_add_fusion.1), channel_id=1, source_target_pairs={{0,1},{1,0},{2,3},{3,2},{4,5},{5,4},{6,7},{7,6},{8,9},{9,8},{10,11... | collective-permute-start | bytes 24584 | tf_op jit(solution)/shard_map/total/ppermute | solution.py:37
  27.4 1.3 %collective-permute-done.9 = f32[16,128]{1,0:T(8,128)S(1)} collective-permute-done((f32[16,128]{1,0:T(8,128)S(1)}, f32[16,128]{1,0:T(8,128)S(1)}, u32[]{:S(2)}, u32[]{:S(2)}) %collective-permute-start.9) | collective-permute-done | bytes 8224 | tf_op jit(solution)/shard_map/total/ppermute | solution.py:37
  28.7 0.7 %collective-permute-done.8 = f32[16,128]{1,0:T(8,128)S(1)} collective-permute-done((f32[16,128]{1,0:T(8,128)S(1)}, f32[16,128]{1,0:T(8,128)S(1)}, u32[]{:S(2)}, u32[]{:S(2)}) %collective-permute-start.8) | collective-permute-done | bytes 8224 | tf_op jit(solution)/shard_map/total/ppermute | solution.py:37
  29.4 0.0 collective-permute-done.7
  29.4 0.1 fusion
  29.4 0.6 %pad_maximum_fusion = f32[32,64]{1,0:T(8,128)} fusion(f32[16,64]{1,0:T(8,128)S(1)} %get-tuple-element.48, f32[16,64]{1,0:T(8,128)S(1)} %get-tuple-element.47), kind=kLoop, calls=%fused_computation | loop fusion | flops 2048 | bytes 16384 | tf_op jit(solution)/shard_map/total/concatenate | solution.py:576
  (2 shorter events, 0.0 us)
Async XLA Ops:
  1.5 8.4 %collective-permute-start = (f32[184,128]{1,0:T(8,128)S(1)}, f32[184,128]{1,0:T(8,128)S(1)}, u32[]{:S(2)}, u32[]{:S(2)}) collective-permute-start(f32[184,128]{1,0:T(8,128)S(1)} %get-tuple-element.26), channel_id=1, source_target_pairs={{0,12},{4,8},{8,4},{12,0},{1,13},{5,9},{9,5},{13,1},{2,14},{6,10},... | collective-permute-start | bytes 282632 | tf_op jit(solution)/shard_map/exchange_far/ppermute | solution.py:37
  6.8 7.7 %collective-permute-start.1 = (f32[184,128]{1,0:T(8,128)S(1)}, f32[184,128]{1,0:T(8,128)S(1)}, u32[]{:S(2)}, u32[]{:S(2)}) collective-permute-start(f32[184,128]{1,0:T(8,128)S(1)} %get-tuple-element.29), channel_id=1, source_target_pairs={{0,8},{4,12},{8,0},{12,4},{1,9},{5,13},{9,1},{13,5},{2,10},{6,14},... | collective-permute-start | bytes 282632 | tf_op jit(solution)/shard_map/exchange_near/ppermute | solution.py:37
  6.9 7.7 %collective-permute-start.2 = (f32[184,128]{1,0:T(8,128)S(1)}, f32[184,128]{1,0:T(8,128)S(1)}, u32[]{:S(2)}, u32[]{:S(2)}) collective-permute-start(f32[184,128]{1,0:T(8,128)S(1)} %get-tuple-element.30), channel_id=1, source_target_pairs={{0,4},{4,0},{8,12},{12,8},{1,5},{5,1},{9,13},{13,9},{2,6},{6,2},{1... | collective-permute-start | bytes 282632 | tf_op jit(solution)/shard_map/exchange_near/ppermute | solution.py:37
  14.8 1.6 %collective-permute-start.3 = (f32[112,128]{1,0:T(8,128)S(1)}, f32[112,128]{1,0:T(8,128)S(1)}, u32[]{:S(2)}, u32[]{:S(2)}) collective-permute-start(f32[112,128]{1,0:T(8,128)S(1)} %get-tuple-element.39.half), channel_id=1, source_target_pairs={{0,1},{1,0},{2,3},{3,2},{4,5},{5,4},{6,7},{7,6},{8,9},{9,8},{10,11... | collective-permute-start | bytes 172040 | tf_op jit(solution)/shard_map/share/ppermute | solution.py:551
  18.8 4.7 %collective-permute-start.6 = (f32[16,128]{1,0:T(8,128)S(1)}, f32[16,128]{1,0:T(8,128)S(1)}, u32[]{:S(2)}, u32[]{:S(2)}) collective-permute-start(f32[16,128]{1,0:T(8,128)S(1)} %value.1), channel_id=1, source_target_pairs={{0,8},{4,12},{8,0},{12,4},{1,9},{5,13},{9,1},{13,5},{2,10},{6,14},... | collective-permute-start | bytes 24584 | tf_op jit(solution)/shard_map/total/ppermute | solution.py:37
  19.5 5.4 %collective-permute-start.5 = (f32[16,128]{1,0:T(8,128)S(1)}, f32[16,128]{1,0:T(8,128)S(1)}, u32[]{:S(2)}, u32[]{:S(2)}) collective-permute-start(f32[16,128]{1,0:T(8,128)S(1)} %value.1), channel_id=1, source_target_pairs={{0,12},{4,8},{8,4},{12,0},{1,13},{5,9},{9,5},{13,1},{2,14},{6,10},... | collective-permute-start | bytes 24584 | tf_op jit(solution)/shard_map/total/ppermute | solution.py:37
  21.9 3.7 %collective-permute-start.4 = (f32[16,128]{1,0:T(8,128)S(1)}, f32[16,128]{1,0:T(8,128)S(1)}, u32[]{:S(2)}, u32[]{:S(2)}) collective-permute-start(f32[16,128]{1,0:T(8,128)S(1)} %value.1), channel_id=1, source_target_pairs={{0,4},{4,0},{8,12},{12,8},{1,5},{5,1},{9,13},{13,9},{2,6},{6,2},{1... | collective-permute-start | bytes 24584 | tf_op jit(solution)/shard_map/total/ppermute | solution.py:37
  25.5 3.1 %collective-permute-start.9 = (f32[16,128]{1,0:T(8,128)S(1)}, f32[16,128]{1,0:T(8,128)S(1)}, u32[]{:S(2)}, u32[]{:S(2)}) collective-permute-start(f32[16,128]{1,0:T(8,128)S(1)} %add_add_fusion.1), channel_id=1, source_target_pairs={{0,3},{1,2},{2,1},{3,0},{4,7},{5,6},{6,5},{7,4},{8,11},{9,10},{10,... | collective-permute-start | bytes 24584 | tf_op jit(solution)/shard_map/total/ppermute | solution.py:37
  25.7 3.7 %collective-permute-start.8 = (f32[16,128]{1,0:T(8,128)S(1)}, f32[16,128]{1,0:T(8,128)S(1)}, u32[]{:S(2)}, u32[]{:S(2)}) collective-permute-start(f32[16,128]{1,0:T(8,128)S(1)} %add_add_fusion.1), channel_id=1, source_target_pairs={{0,2},{1,3},{2,0},{3,1},{4,6},{5,7},{6,4},{7,5},{8,10},{9,11},{10,... | collective-permute-start | bytes 24584 | tf_op jit(solution)/shard_map/total/ppermute | solution.py:37
  27.1 2.3 %collective-permute-start.7 = (f32[16,128]{1,0:T(8,128)S(1)}, f32[16,128]{1,0:T(8,128)S(1)}, u32[]{:S(2)}, u32[]{:S(2)}) collective-permute-start(f32[16,128]{1,0:T(8,128)S(1)} %add_add_fusion.1), channel_id=1, source_target_pairs={{0,1},{1,0},{2,3},{3,2},{4,5},{5,4},{6,7},{7,6},{8,9},{9,8},{10,11... | collective-permute-start | bytes 24584 | tf_op jit(solution)/shard_map/total/ppermute | solution.py:37

commit v8 on v6

--- a/solution.py
+++ b/solution.py
@@ -419,11 +419,12 @@
     ends, opening, coupon = ends_ref[...], open_ref[...], rate_ref[...]
     worth = jnp.zeros_like(opening)
     income = jnp.zeros_like(opening)
+    first_due = jnp.sum(coupon * opening, axis=0, keepdims=True)
     for r in range(rows):
-        held = jnp.clip(ends - paid_by[0][r : r + 1], 0.0, opening)
+        held = opening
         for t in range(steps):
             later = jnp.clip(ends - paid_by[t + 1][r : r + 1], 0.0, opening)
-            due = jnp.sum(coupon * held, axis=0, keepdims=True)
+            due = jnp.sum(coupon * held, axis=0, keepdims=True) if t else first_due
             income = income + held * (incomes[t][r : r + 1] / due)
             worth = worth + (held - later) * (disc_ref[t, r : r + 1, :] - 1.0)
             held = later

time: 30.2 us -> 30.2 us (level)
  no operation moved by 1% of the time
where the time goes in v8:
time: 30.2 us; the launch traced here: 30.1 us
  waiting for transfers between devices  11.4 us (38%)
  starting transfers between devices  11.2 us (37%)
  Pallas kernels  6.69 us (22%)
  other arithmetic  0.62 us (2%)
    ppermute x9, waiting for transfers between devices, trade(): return lax.ppermute(x, axis, pairs)  11.4 us
    ppermute x9, starting transfers between devices, trade(): return lax.ppermute(x, axis, pairs)  11.2 us
    pallas_call x1, Pallas kernels, on_device(): pl.pallas_call(functools.partial(value_kernel, plan, float(paths * sides)...  2.34 us
    pallas_call x1, Pallas kernels, on_device(): pl.pallas_call(functools.partial(half_kernel, plan), out_shape=shape(*sum...  1.55 us
    pallas_call x1, Pallas kernels, on_device(): pl.pallas_call(functools.partial(pack_kernel, plan), out_shape=[pltpu.VME...  1.51 us
    pallas_call x1, Pallas kernels, on_device(): pl.pallas_call(functools.partial(deal_kernel, plan), out_shape=[shape(dea...  0.97 us
    concatenate x1, other arithmetic, on_device(): jnp.concatenate([total[:, i * tranches:(i + 1) * tranches] for i in range...  0.61 us
  transfers between devices with their start and end apart: 10, of which 7 were waited for; matrix products, arithmetic and copies ran while one was open for 0% of the time, Pallas kernels for 8%

profile of v8, /device:TPU:0, one launch (start us, length us, event | category | flops | bytes accessed | tf_op | source)
XLA Modules:
  0.0 30.1 jit_solution(14563650777099314869)
XLA Ops:
  0.0 1.5 %pack.1 = (f32[184,128]{1,0:T(8,128)S(1)}, f32[184,128]{1,0:T(8,128)S(1)}, f32[184,128]{1,0:T(8,128)S(1)}, f32[184,128]{1,0:T(8,128)S(1)}, s32[1,32]{1,0:T(1,128...) custom-call(f32[6,104,128]{2,1,0:T(8,128)} %bitcast.10, ...), custom_call_target="tpu_custom_call" | custom-call | flops 1000000000 | bytes 100000 | tf_op jit(solution)/shard_map/pack/pallas_call | solution.py:486
  1.5 5.1 %collective-permute-start = (f32[184,128]{1,0:T(8,128)S(1)}, f32[184,128]{1,0:T(8,128)S(1)}, u32[]{:S(2)}, u32[]{:S(2)}) collective-permute-start(f32[184,128]{1,0:T(8,128)S(1)} %get-tuple-element.24), channel_id=1, source_target_pairs={{0,12},{4,8},{8,4},{12,0},{1,13},{5,9},{9,5},{13,1},{2,14},{6,10},... | collective-permute-start | bytes 282632 | tf_op jit(solution)/shard_map/exchange/ppermute | solution.py:37
  6.6 0.0 collective-permute-start.1
  6.6 0.6 %collective-permute-start.2 = (f32[184,128]{1,0:T(8,128)S(1)}, f32[184,128]{1,0:T(8,128)S(1)}, u32[]{:S(2)}, u32[]{:S(2)}) collective-permute-start(f32[184,128]{1,0:T(8,128)S(1)} %get-tuple-element.26), channel_id=1, source_target_pairs={{0,4},{4,0},{8,12},{12,8},{1,5},{5,1},{9,13},{13,9},{2,6},{6,2},{1... | collective-permute-start | bytes 282632 | tf_op jit(solution)/shard_map/exchange/ppermute | solution.py:37
  7.3 1.0 %deals.1 = (f32[32,128]{1,0:T(8,128)S(1)}, f32[64,128]{1,0:T(8,128)S(1)}, f32[64,128]{1,0:T(8,128)S(1)}, f32[64,128]{1,0:T(8,128)S(1)}, f32[192,128]{1,0:T(8,128)S(1)}, /*index=5*/f32[6,8,128]{2,1,0:T(8,128)S(1)}) custom-call(s32[1,32]{1,0:T(1,128)S(1)} %get-tuple-element.28.owner_ref, s32[32,64]{1,0:T(8,128)S(1)} %get-tuple-element.29.order_ref, ...), custom_call_target="tpu_custom_call" | custom-call | flops 1000000000 | bytes 100000 | tf_op jit(solution)/shard_map/deals/pallas_call | solution.py:501
  8.3 1.9 %collective-permute-done.refs_0_ = f32[184,128]{1,0:T(8,128)S(1)} collective-permute-done((f32[184,128]{1,0:T(8,128)S(1)}, f32[184,128]{1,0:T(8,128)S(1)}, u32[]{:S(2)}, u32[]{:S(2)}) %collective-permute-start) | collective-permute-done | bytes 94240 | tf_op jit(solution)/shard_map/exchange/ppermute | solution.py:37
  10.2 4.4 %collective-permute-done.1.refs_1_ = f32[184,128]{1,0:T(8,128)S(1)} collective-permute-done((f32[184,128]{1,0:T(8,128)S(1)}, f32[184,128]{1,0:T(8,128)S(1)}, u32[]{:S(2)}, u32[]{:S(2)}) %collective-permute-start.1) | collective-permute-done | bytes 94240 | tf_op jit(solution)/shard_map/exchange/ppermute | solution.py:37
  14.5 0.0 collective-permute-done.2.refs_2_
  14.5 0.3 %sort.1 = (f32[112,128]{1,0:T(8,128)S(1)}, bf16[384,512]{1,0:T(8,128)(2,1)S(1)}) custom-call(f32[184,128]{1,0:T(8,128)S(1)} %collective-permute-done.refs_0_, f32[184,128]{1,0:T(8,128)S(1)} %collective-permute-done.1.refs_1_, f32[184,128]{1,0:T(8,128)S(1)} %collective-permute-done.2.refs_2_, f32[184,128]{1,0:T(8,128)S(1)} %get-tuple-element.34.refs_3_), custom_call_target="tpu_custom_call" | custom-call | flops 500000000 | bytes 100000 | tf_op jit(solution)/shard_map/sort/pallas_call | solution.py:517
  14.9 0.1 collective-permute-start.3
  15.0 1.5 %half.1.refs_0_ = f32[416,128]{1,0:T(8,128)S(1)} custom-call(f32[112,128]{1,0:T(8,128)S(1)} %get-tuple-element.35.half, bf16[384,512]{1,0:T(8,128)(2,1)S(1)} %get-tuple-element.36.table.refs_2_, f32[32,128]{1,0:T(8,128)S(1)} %get-tuple-element.37.list_ref.refs_3_, f32[192,128]{1,0:T(8,128)S(1)} %get-tuple-element.38.mort_ref.refs_7_), custom_call_target="tpu_custom_call" | custom-call | flops 2000000000 | bytes 100000 | tf_op jit(solution)/shard_map/half/pallas_call | solution.py:541
  16.5 0.0 collective-permute-done.3.refs_1_
  16.5 2.3 %value.1 = f32[16,128]{1,0:T(8,128)S(1)} custom-call(f32[416,128]{1,0:T(8,128)S(1)} %half.1.refs_0_, f32[112,128]{1,0:T(8,128)S(1)} %collective-permute-done.3.refs_1_, bf16[384,512]{1,0:T(8,128)(2,1)S(1)} %get-tuple-element.36.table.refs_2_, f32[32,128]{1,0:T(8,128)S(1)} %get-tuple-element.37.list_ref.refs_3_, f32[64,128]{1,0:T(8,128)S(1)} %get-tuple-element.39.refs_4_, ...), custom_call_target="tpu_custom_call" | custom-call | flops 3000000000 | bytes 100000 | tf_op jit(solution)/shard_map/value/pallas_call | solution.py:550
  18.9 0.7 %collective-permute-start.6 = (f32[16,128]{1,0:T(8,128)S(1)}, f32[16,128]{1,0:T(8,128)S(1)}, u32[]{:S(2)}, u32[]{:S(2)}) collective-permute-start(f32[16,128]{1,0:T(8,128)S(1)} %value.1), channel_id=1, source_target_pairs={{0,8},{4,12},{8,0},{12,4},{1,9},{5,13},{9,1},{13,5},{2,10},{6,14},... | collective-permute-start | bytes 24584 | tf_op jit(solution)/shard_map/total/ppermute | solution.py:37
  19.6 2.3 %collective-permute-start.5 = (f32[16,128]{1,0:T(8,128)S(1)}, f32[16,128]{1,0:T(8,128)S(1)}, u32[]{:S(2)}, u32[]{:S(2)}) collective-permute-start(f32[16,128]{1,0:T(8,128)S(1)} %value.1), channel_id=1, source_target_pairs={{0,12},{4,8},{8,4},{12,0},{1,13},{5,9},{9,5},{13,1},{2,14},{6,10},... | collective-permute-start | bytes 24584 | tf_op jit(solution)/shard_map/total/ppermute | solution.py:37
  21.9 0.5 %collective-permute-start.4 = (f32[16,128]{1,0:T(8,128)S(1)}, f32[16,128]{1,0:T(8,128)S(1)}, u32[]{:S(2)}, u32[]{:S(2)}) collective-permute-start(f32[16,128]{1,0:T(8,128)S(1)} %value.1), channel_id=1, source_target_pairs={{0,4},{4,0},{8,12},{12,8},{1,5},{5,1},{9,13},{13,9},{2,6},{6,2},{1... | collective-permute-start | bytes 24584 | tf_op jit(solution)/shard_map/total/ppermute | solution.py:37
  22.4 1.1 %collective-permute-done.6 = f32[16,128]{1,0:T(8,128)S(1)} collective-permute-done((f32[16,128]{1,0:T(8,128)S(1)}, f32[16,128]{1,0:T(8,128)S(1)}, u32[]{:S(2)}, u32[]{:S(2)}) %collective-permute-start.6) | collective-permute-done | bytes 8224 | tf_op jit(solution)/shard_map/total/ppermute | solution.py:37
  23.6 1.5 %collective-permute-done.5 = f32[16,128]{1,0:T(8,128)S(1)} collective-permute-done((f32[16,128]{1,0:T(8,128)S(1)}, f32[16,128]{1,0:T(8,128)S(1)}, u32[]{:S(2)}, u32[]{:S(2)}) %collective-permute-start.5) | collective-permute-done | bytes 8224 | tf_op jit(solution)/shard_map/total/ppermute | solution.py:37
  25.0 0.5 %collective-permute-done.4 = f32[16,128]{1,0:T(8,128)S(1)} collective-permute-done((f32[16,128]{1,0:T(8,128)S(1)}, f32[16,128]{1,0:T(8,128)S(1)}, u32[]{:S(2)}, u32[]{:S(2)}) %collective-permute-start.4) | collective-permute-done | bytes 8224 | tf_op jit(solution)/shard_map/total/ppermute | solution.py:37
  25.6 0.2 collective-permute-start.9
  25.7 1.4 %collective-permute-start.8 = (f32[16,128]{1,0:T(8,128)S(1)}, f32[16,128]{1,0:T(8,128)S(1)}, u32[]{:S(2)}, u32[]{:S(2)}) collective-permute-start(f32[16,128]{1,0:T(8,128)S(1)} %add_add_fusion.1), channel_id=1, source_target_pairs={{0,2},{1,3},{2,0},{3,1},{4,6},{5,7},{6,4},{7,5},{8,10},{9,11},{10,... | collective-permute-start | bytes 24584 | tf_op jit(solution)/shard_map/total/ppermute | solution.py:37
  27.1 0.3 collective-permute-start.7
  27.4 1.3 %collective-permute-done.9 = f32[16,128]{1,0:T(8,128)S(1)} collective-permute-done((f32[16,128]{1,0:T(8,128)S(1)}, f32[16,128]{1,0:T(8,128)S(1)}, u32[]{:S(2)}, u32[]{:S(2)}) %collective-permute-start.9) | collective-permute-done | bytes 8224 | tf_op jit(solution)/shard_map/total/ppermute | solution.py:37
  28.7 0.7 %collective-permute-done.8 = f32[16,128]{1,0:T(8,128)S(1)} collective-permute-done((f32[16,128]{1,0:T(8,128)S(1)}, f32[16,128]{1,0:T(8,128)S(1)}, u32[]{:S(2)}, u32[]{:S(2)}) %collective-permute-start.8) | collective-permute-done | bytes 8224 | tf_op jit(solution)/shard_map/total/ppermute | solution.py:37
  29.4 0.0 collective-permute-done.7
  29.4 0.1 fusion
  29.5 0.6 %pad_maximum_fusion = f32[32,64]{1,0:T(8,128)} fusion(f32[16,64]{1,0:T(8,128)S(1)} %get-tuple-element.44, f32[16,64]{1,0:T(8,128)S(1)} %get-tuple-element.43), kind=kLoop, calls=%fused_computation | loop fusion | flops 2048 | bytes 16384 | tf_op jit(solution)/shard_map/total/concatenate | solution.py:559
  (2 shorter events, 0.0 us)
Async XLA Ops:
  1.5 8.6 %collective-permute-start = (f32[184,128]{1,0:T(8,128)S(1)}, f32[184,128]{1,0:T(8,128)S(1)}, u32[]{:S(2)}, u32[]{:S(2)}) collective-permute-start(f32[184,128]{1,0:T(8,128)S(1)} %get-tuple-element.24), channel_id=1, source_target_pairs={{0,12},{4,8},{8,4},{12,0},{1,13},{5,9},{9,5},{13,1},{2,14},{6,10},... | collective-permute-start | bytes 282632 | tf_op jit(solution)/shard_map/exchange/ppermute | solution.py:37
  6.6 7.9 %collective-permute-start.1 = (f32[184,128]{1,0:T(8,128)S(1)}, f32[184,128]{1,0:T(8,128)S(1)}, u32[]{:S(2)}, u32[]{:S(2)}) collective-permute-start(f32[184,128]{1,0:T(8,128)S(1)} %get-tuple-element.25), channel_id=1, source_target_pairs={{0,8},{4,12},{8,0},{12,4},{1,9},{5,13},{9,1},{13,5},{2,10},{6,14},... | collective-permute-start | bytes 282632 | tf_op jit(solution)/shard_map/exchange/ppermute | solution.py:37
  6.6 7.9 %collective-permute-start.2 = (f32[184,128]{1,0:T(8,128)S(1)}, f32[184,128]{1,0:T(8,128)S(1)}, u32[]{:S(2)}, u32[]{:S(2)}) collective-permute-start(f32[184,128]{1,0:T(8,128)S(1)} %get-tuple-element.26), channel_id=1, source_target_pairs={{0,4},{4,0},{8,12},{12,8},{1,5},{5,1},{9,13},{13,9},{2,6},{6,2},{1... | collective-permute-start | bytes 282632 | tf_op jit(solution)/shard_map/exchange/ppermute | solution.py:37
  14.9 1.6 %collective-permute-start.3 = (f32[112,128]{1,0:T(8,128)S(1)}, f32[112,128]{1,0:T(8,128)S(1)}, u32[]{:S(2)}, u32[]{:S(2)}) collective-permute-start(f32[112,128]{1,0:T(8,128)S(1)} %get-tuple-element.35.half), channel_id=1, source_target_pairs={{0,1},{1,0},{2,3},{3,2},{4,5},{5,4},{6,7},{7,6},{8,9},{9,8},{10,11... | collective-permute-start | bytes 172040 | tf_op jit(solution)/shard_map/share/ppermute | solution.py:534
  18.9 4.7 %collective-permute-start.6 = (f32[16,128]{1,0:T(8,128)S(1)}, f32[16,128]{1,0:T(8,128)S(1)}, u32[]{:S(2)}, u32[]{:S(2)}) collective-permute-start(f32[16,128]{1,0:T(8,128)S(1)} %value.1), channel_id=1, source_target_pairs={{0,8},{4,12},{8,0},{12,4},{1,9},{5,13},{9,1},{13,5},{2,10},{6,14},... | collective-permute-start | bytes 24584 | tf_op jit(solution)/shard_map/total/ppermute | solution.py:37
  19.6 5.4 %collective-permute-start.5 = (f32[16,128]{1,0:T(8,128)S(1)}, f32[16,128]{1,0:T(8,128)S(1)}, u32[]{:S(2)}, u32[]{:S(2)}) collective-permute-start(f32[16,128]{1,0:T(8,128)S(1)} %value.1), channel_id=1, source_target_pairs={{0,12},{4,8},{8,4},{12,0},{1,13},{5,9},{9,5},{13,1},{2,14},{6,10},... | collective-permute-start | bytes 24584 | tf_op jit(solution)/shard_map/total/ppermute | solution.py:37
  21.9 3.7 %collective-permute-start.4 = (f32[16,128]{1,0:T(8,128)S(1)}, f32[16,128]{1,0:T(8,128)S(1)}, u32[]{:S(2)}, u32[]{:S(2)}) collective-permute-start(f32[16,128]{1,0:T(8,128)S(1)} %value.1), channel_id=1, source_target_pairs={{0,4},{4,0},{8,12},{12,8},{1,5},{5,1},{9,13},{13,9},{2,6},{6,2},{1... | collective-permute-start | bytes 24584 | tf_op jit(solution)/shard_map/total/ppermute | solution.py:37
  25.6 3.1 %collective-permute-start.9 = (f32[16,128]{1,0:T(8,128)S(1)}, f32[16,128]{1,0:T(8,128)S(1)}, u32[]{:S(2)}, u32[]{:S(2)}) collective-permute-start(f32[16,128]{1,0:T(8,128)S(1)} %add_add_fusion.1), channel_id=1, source_target_pairs={{0,3},{1,2},{2,1},{3,0},{4,7},{5,6},{6,5},{7,4},{8,11},{9,10},{10,... | collective-permute-start | bytes 24584 | tf_op jit(solution)/shard_map/total/ppermute | solution.py:37
  25.7 3.7 %collective-permute-start.8 = (f32[16,128]{1,0:T(8,128)S(1)}, f32[16,128]{1,0:T(8,128)S(1)}, u32[]{:S(2)}, u32[]{:S(2)}) collective-permute-start(f32[16,128]{1,0:T(8,128)S(1)} %add_add_fusion.1), channel_id=1, source_target_pairs={{0,2},{1,3},{2,0},{3,1},{4,6},{5,7},{6,4},{7,5},{8,10},{9,11},{10,... | collective-permute-start | bytes 24584 | tf_op jit(solution)/shard_map/total/ppermute | solution.py:37
  27.1 2.3 %collective-permute-start.7 = (f32[16,128]{1,0:T(8,128)S(1)}, f32[16,128]{1,0:T(8,128)S(1)}, u32[]{:S(2)}, u32[]{:S(2)}) collective-permute-start(f32[16,128]{1,0:T(8,128)S(1)} %add_add_fusion.1), channel_id=1, source_target_pairs={{0,1},{1,0},{2,3},{3,2},{4,5},{5,4},{6,7},{7,6},{8,9},{9,8},{10,11... | collective-permute-start | bytes 24584 | tf_op jit(solution)/shard_map/total/ppermute | solution.py:37
